TPU v7x, 32 devices: a whole 2x2x4 slice. The times are simulated.
32 devices in a mesh: ctx: 8 (over z, core), fsdp: 4 (over y, x).
Axes of the slice: x: 2, y: 2, z: 4, core: 2. Of those that a mesh axis runs over, the one named last changes fastest.
Arguments:
- hidden_in: bfloat16 [4, 3072, 1024], P('fsdp', 'ctx'), may hold values from -6 to 6
- w_qkv: bfloat16 [1024, 3072], P(None, 'fsdp'), may hold values from -0.25 to 0.25
- w_out: bfloat16 [1024, 1024], P(None, 'fsdp'), may hold values from -1 to 1
- w_in: bfloat16 [1024, 4096], P(None, 'fsdp'), may hold values from -0.1875 to 0.1875
- w_back: bfloat16 [4096, 1024], P(None, 'fsdp'), may hold values from -0.09375 to 0.09375
- vectors: float32 [8, 1024], replicated, may hold values from -1 to 1.5, as said below
- bias_in: float32 [4096], replicated, may hold values from -3 to 3
- cotangent: float32 [4, 3072, 1024], P('fsdp', 'ctx'), may hold values from -6 to 6
Outputs:
- layer_out: bfloat16 [4, 3072, 1024], P('fsdp', 'ctx')
- input_grad: float32 [4, 3072, 1024], P('fsdp', 'ctx')
- qkv_weight_grad: float32 [1024, 3072], P(('ctx', 'fsdp'))
- out_weight_grad: float32 [1024, 1024], P(('ctx', 'fsdp'))
- in_weight_grad: float32 [1024, 4096], P(('ctx', 'fsdp'))
- back_weight_grad: float32 [4096, 1024], P(None, ('ctx', 'fsdp'))
- vector_grad: float32 [8, 1024], P(None, ('ctx', 'fsdp'))
- in_bias_grad: float32 [4096], P(('ctx', 'fsdp'))
Inputs may be any that keep to these rules, and one draw needn't show every extreme that they name: `vectors`: rows 3 and 6 (norm gains) lie within 0.5 to 1.5, the other rows within -1 to 1.
All inputs are finite; a program needn't handle non-finite values.
Results may differ from a plain program's by a relative error of at most 0.015.
The roundings to bfloat16 on the way count: a program that leaves them out, or rounds other values in their place, can miss the bound.
Values may be sent and summed in bfloat16 or wider, within the bound.
A program may use at most 384 MiB of HBM per device.

v0:
```python
from functools import partial
import math

import jax
import jax.numpy as jnp
from jax import lax
from jax.sharding import PartitionSpec as P

HEADS = 16
HEAD = 64


EPS = 1e-12


def project(left, piece):
    return jnp.dot(left, piece, preferred_element_type=jnp.float32)


def back_fold(grad_low, total, piece):
    columns = lax.slice_in_dim(grad_low, 0, piece.shape[1], axis=1)
    return total + lax.dot_general(
        columns, piece, (((1,), (1,)), ((), ())), preferred_element_type=jnp.float32
    )


def outer_rows(left, right, start, count):
    columns = lax.dynamic_slice_in_dim(left, start, count, 1)
    return lax.dot_general(
        columns, right, (((0,), (0,)), ((), ())), preferred_element_type=jnp.float32
    )


def norm_fwd(resid, gain, shift):
    centre = resid - jnp.mean(resid, axis=-1, keepdims=True)
    spread = jnp.mean(centre * centre, axis=-1, keepdims=True)
    rstd = lax.rsqrt(spread + EPS)
    unit = centre * rstd
    return (unit * gain + shift, unit, rstd)


def norm_back(grad, unit, rstd, gain):
    scaled = grad * gain
    inner = (
        scaled
        - jnp.mean(scaled, axis=-1, keepdims=True)
        - unit * jnp.mean(scaled * unit, axis=-1, keepdims=True)
    )
    return (rstd * inner, jnp.sum(grad * unit, axis=0), jnp.sum(grad, axis=0))


def scores_of(query3, key_block, scale):
    return jnp.einsum("qhe,khe->hqk", query3, key_block, preferred_element_type=jnp.float32) * scale


def on_device(hidden_in, w_qkv, w_out, w_in, w_back, vectors, bias_in, cotangent):
    tok_rows = hidden_in[0]
    count_tok, width = tok_rows.shape
    scale = 1.0 / math.sqrt(HEAD)
    gelu_fn = partial(jax.nn.gelu, approximate=True)
    qkv_bias = jnp.concatenate([vectors[0], jnp.zeros((width,), jnp.float32), vectors[1]])
    qkv = project(tok_rows, lax.all_gather(w_qkv, "fsdp", axis=1, tiled=True)) + qkv_bias
    qkv_low = qkv.astype(jnp.bfloat16)
    query = qkv_low[:, :width]
    keys = qkv_low[:, width : 2 * width]
    values = qkv_low[:, 2 * width :]
    key_all, value_all = (
        lax.all_gather(keys, "ctx", axis=0, tiled=True),
        lax.all_gather(values, "ctx", axis=0, tiled=True),
    )
    query3 = query.reshape(count_tok, HEADS, HEAD)
    key3 = key_all.reshape(-1, HEADS, HEAD)
    value3 = value_all.reshape(-1, HEADS, HEAD)
    length = key3.shape[0]
    block = min(512, length)
    blocks = length // block

    def lse_step(idx, carry):
        top, total = carry
        key_block = lax.dynamic_slice_in_dim(key3, idx * block, block, 0)
        scores = scores_of(query3, key_block, scale)
        new_top = jnp.maximum(top, jnp.max(scores, axis=-1))
        total = total * jnp.exp(top - new_top) + jnp.sum(
            jnp.exp(scores - new_top[:, :, None]), axis=-1
        )
        return (new_top, total)

    start_top = jnp.full((HEADS, count_tok), -1e30, jnp.float32)
    start_total = jnp.zeros((HEADS, count_tok), jnp.float32)
    top, total = lax.fori_loop(0, blocks, lse_step, (start_top, start_total))
    log_total = top + jnp.log(total)

    def attend_step(idx, acc):
        key_block = lax.dynamic_slice_in_dim(key3, idx * block, block, 0)
        value_block = lax.dynamic_slice_in_dim(value3, idx * block, block, 0)
        probs = jnp.exp(scores_of(query3, key_block, scale) - log_total[:, :, None])
        return acc + jnp.einsum(
            "hqk,khe->qhe",
            probs.astype(jnp.bfloat16),
            value_block,
            preferred_element_type=jnp.float32,
        )

    attended = lax.fori_loop(
        0, blocks, attend_step, jnp.zeros((count_tok, HEADS, HEAD), jnp.float32)
    )
    attended_low = attended.reshape(count_tok, width).astype(jnp.bfloat16)
    attn_out = project(attended_low, lax.all_gather(w_out, "fsdp", axis=1, tiled=True)) + vectors[2]
    resid_one = tok_rows.astype(jnp.float32) + attn_out
    normed, unit_one, rstd_one = norm_fwd(resid_one, vectors[3], vectors[4])
    normed_low = normed.astype(jnp.bfloat16)
    pre = project(normed_low, lax.all_gather(w_in, "fsdp", axis=1, tiled=True)) + bias_in
    act, gelu_pull = jax.vjp(gelu_fn, pre)
    act_low = act.astype(jnp.bfloat16)
    ffn_out = project(act_low, lax.all_gather(w_back, "fsdp", axis=1, tiled=True)) + vectors[5]
    resid_two = normed + ffn_out
    result, unit_two, rstd_two = norm_fwd(resid_two, vectors[6], vectors[7])
    layer_out = result.astype(jnp.bfloat16)[None]
    grad_out = cotangent[0]
    grad_two, gain_two, shift_two = norm_back(grad_out, unit_two, rstd_two, vectors[6])
    grad_two_low = grad_two.astype(jnp.bfloat16)
    hidden_units = w_in.shape[1] * lax.axis_size("fsdp")
    grad_act = back_fold(
        grad_two_low,
        jnp.zeros((count_tok, hidden_units), jnp.float32),
        lax.all_gather(w_back, "fsdp", axis=1, tiled=True),
    )
    grad_pre = gelu_pull(grad_act)[0]
    grad_pre_low = grad_pre.astype(jnp.bfloat16)
    grad_normed = grad_two + back_fold(
        grad_pre_low,
        jnp.zeros((count_tok, width), jnp.float32),
        lax.all_gather(w_in, "fsdp", axis=1, tiled=True),
    )
    grad_one, gain_one, shift_one = norm_back(grad_normed, unit_one, rstd_one, vectors[3])
    grad_one_low = grad_one.astype(jnp.bfloat16)
    share = width // (lax.axis_size("ctx") * lax.axis_size("fsdp"))
    grad_att = back_fold(
        grad_one_low,
        jnp.zeros((count_tok, width), jnp.float32),
        lax.all_gather(w_out, "fsdp", axis=1, tiled=True),
    )
    grad_att3 = grad_att.astype(jnp.bfloat16).reshape(count_tok, HEADS, HEAD)

    def block_terms(key_block, value_block):
        probs = jnp.exp(scores_of(query3, key_block, scale) - log_total[:, :, None])
        grad_probs = jnp.einsum(
            "qhe,khe->hqk", grad_att3, value_block, preferred_element_type=jnp.float32
        )
        return (probs, grad_probs)

    def delta_step(idx, acc):
        key_block = lax.dynamic_slice_in_dim(key3, idx * block, block, 0)
        value_block = lax.dynamic_slice_in_dim(value3, idx * block, block, 0)
        probs, grad_probs = block_terms(key_block, value_block)
        return acc + jnp.sum(probs * grad_probs, axis=-1)

    delta = lax.fori_loop(0, blocks, delta_step, jnp.zeros((HEADS, count_tok), jnp.float32))

    def query_step(idx, acc):
        key_block = lax.dynamic_slice_in_dim(key3, idx * block, block, 0)
        value_block = lax.dynamic_slice_in_dim(value3, idx * block, block, 0)
        probs, grad_probs = block_terms(key_block, value_block)
        grad_scores = (probs * (grad_probs - delta[:, :, None])).astype(jnp.bfloat16)
        return acc + jnp.einsum(
            "hqk,khe->qhe", grad_scores, key_block, preferred_element_type=jnp.float32
        )

    grad_query = lax.fori_loop(
        0, blocks, query_step, jnp.zeros((count_tok, HEADS, HEAD), jnp.float32)
    )
    grad_query = (grad_query * scale).reshape(count_tok, width)
    count = lax.axis_size("ctx") * count_tok
    key_block = key3
    value_block = value3
    probs, grad_probs = block_terms(key_block, value_block)
    grad_scores = (probs * (grad_probs - delta[:, :, None])).astype(jnp.bfloat16)
    grad_keys = (
        jnp.einsum("hqk,qhe->khe", grad_scores, query3, preferred_element_type=jnp.float32) * scale
    )
    grad_values = jnp.einsum(
        "hqk,qhe->khe", probs.astype(jnp.bfloat16), grad_att3, preferred_element_type=jnp.float32
    )
    kv_rows = lax.psum_scatter(
        jnp.concatenate(
            [grad_keys.reshape(count, width), grad_values.reshape(count, width)], axis=1
        ).astype(jnp.bfloat16),
        "ctx",
        scatter_dimension=0,
        tiled=True,
    ).astype(jnp.float32)
    grad_qkv = jnp.concatenate([grad_query, kv_rows], axis=1)
    grad_qkv_low = grad_qkv.astype(jnp.bfloat16)
    grad_in = grad_one + back_fold(
        grad_qkv_low,
        jnp.zeros((count_tok, width), jnp.float32),
        lax.all_gather(w_qkv, "fsdp", axis=1, tiled=True),
    )
    vector_terms = jnp.stack(
        [
            jnp.sum(grad_query, axis=0),
            jnp.sum(kv_rows[:, width:], axis=0),
            jnp.sum(grad_one, axis=0),
            gain_one,
            shift_one,
            jnp.sum(grad_two, axis=0),
            gain_two,
            shift_two,
        ],
        axis=1,
    )
    ratio = hidden_units // width
    bias_terms = jnp.sum(grad_pre, axis=0).reshape(width, ratio)
    small_table = jnp.concatenate(
        [vector_terms, bias_terms, jnp.zeros((width, 128 - 8 - ratio), jnp.float32)], axis=1
    )
    start = jnp.int32(0)
    all_rows = lax.psum_scatter(
        jnp.concatenate(
            [
                jnp.concatenate(
                    [
                        outer_rows(
                            normed_low, grad_pre_low, start, share * lax.axis_size(("ctx", "fsdp"))
                        ),
                        outer_rows(
                            grad_two_low, act_low, start, share * lax.axis_size(("ctx", "fsdp"))
                        ),
                    ],
                    axis=1,
                ),
                jnp.concatenate(
                    [
                        outer_rows(
                            tok_rows, grad_qkv_low, start, share * lax.axis_size(("ctx", "fsdp"))
                        ),
                        outer_rows(
                            attended_low,
                            grad_one_low,
                            start,
                            share * lax.axis_size(("ctx", "fsdp")),
                        ),
                        lax.dynamic_slice_in_dim(
                            small_table, start, share * lax.axis_size(("ctx", "fsdp")), 0
                        ),
                    ],
                    axis=1,
                ),
            ],
            axis=1,
        ),
        ("ctx", "fsdp"),
        scatter_dimension=0,
        tiled=True,
    )
    ffn_rows = all_rows[:, : 2 * hidden_units]
    attn_rows = all_rows[:, 2 * hidden_units :]
    in_weight_grad = ffn_rows[:, :hidden_units]
    back_weight_grad = ffn_rows[:, hidden_units:].T
    qkv_weight_grad = attn_rows[:, : 3 * width]
    out_weight_grad = attn_rows[:, 3 * width : 4 * width]
    small_rows = attn_rows[:, 4 * width :]
    vector_grad = small_rows[:, :8].T
    in_bias_grad = small_rows[:, 8 : 8 + ratio].reshape(-1)
    return (
        layer_out,
        grad_in[None],
        qkv_weight_grad,
        out_weight_grad,
        in_weight_grad,
        back_weight_grad,
        vector_grad,
        in_bias_grad,
    )


def solution(mesh):
    return jax.shard_map(
        on_device,
        mesh=mesh,
        in_specs=(
            P("fsdp", "ctx", None),
            P(None, "fsdp"),
            P(None, "fsdp"),
            P(None, "fsdp"),
            P(None, "fsdp"),
            P(),
            P(),
            P("fsdp", "ctx", None),
        ),
        out_specs=(
            P("fsdp", "ctx", None),
            P("fsdp", "ctx", None),
            P(("ctx", "fsdp"), None),
            P(("ctx", "fsdp"), None),
            P(("ctx", "fsdp"), None),
            P(None, ("ctx", "fsdp")),
            P(None, ("ctx", "fsdp")),
            P(("ctx", "fsdp")),
        ),
        check_vma=False,
    )
```

profile of v0, /device:TPU:23, one launch (start us, length us, event | category | flops | bytes accessed | tf_op | source)
XLA Modules:
  0.0 1878.9 jit_solution(1233266115698632532)
XLA Ops:
  9.1 71.1 %all-gather.7.cloned.1.call-done = bf16[1024,3072]{1,0:T(8,128)(2,1)} async-done(((bf16[1024,768]{1,0:T(8,128)(2,1)}), bf16[1024,3072]{1,0:T(8,128)(2,1)}) %all-gather.7.cloned.1.call-update) | async-done | bytes 6291472 | tf_op jit(solution)/shard_map/all_gather | solution.py:62
  90.3 61.8 %all-gather.11.cloned.1.call-done = bf16[3072,1024]{1,0:T(8,128)(2,1)} async-done(((bf16[384,1024]{1,0:T(8,128)(2,1)}), bf16[3072,1024]{1,0:T(8,128)(2,1)}) %all-gather.11.cloned.1.call-update) | async-done | bytes 6291472 | tf_op jit(solution)/shard_map/all_gather | solution.py:68
  160.8 87.3 %while.58 = (s32[]{:T(128)}, f32[16,384]{1,0:T(8,128)S(1)}, f32[16,384]{1,0:T(8,128)S(1)}, bf16[3072,16,64]{0,2,1:T(8,128)(2,1)}, bf16[384,16,64]{0,2,1:T(8,128)...) while((s32[]{:T(128)}, f32[16,384]{1,0:T(8,128)S(1)}, f32[16,384]{1,0:T(8,128)S(1)}, ...), condition=%wide.region_3.0_spmd.clone, body=%wide.region_0.0_spmd.clone.sunk | while | flops 418412544 | bytes 27320472 | solution.py:90
  256.8 32.4 %while.59 = (s32[]{:T(128)}, f32[384,16,64]{0,2,1:T(8,128)S(1)}, bf16[3072,16,64]{0,2,1:T(8,128)(2,1)}, bf16[3072,16,64]{0,2,1:T(8,128)(2,1)}, bf16[384,16,64]{0...) while((s32[]{:T(128)}, f32[384,16,64]{0,2,1:T(8,128)S(1)}, ...), condition=%wide.region_5.0_spmd.clone, body=%wide.region_4.0_spmd.clone.sunk | while | flops 815529984 | bytes 6055580 | solution.py:104
  295.4 47.3 %all-gather.15.cloned.1.call-done = bf16[1024,4096]{1,0:T(8,128)(2,1)} async-done(((bf16[1024,1024]{1,0:T(8,128)(2,1)}), bf16[1024,4096]{1,0:T(8,128)(2,1)}) %all-gather.15.cloned.1.call-update) | async-done | bytes 8388624 | tf_op jit(solution)/shard_map/all_gather | solution.py:112
  342.7 8.9 convolution_add_fusion
  351.6 31.3 %fusion.87 = f32[16,384,3072]{2,1,0:T(8,128)} fusion(bf16[384,16,64]{0,2,1:T(8,128)(2,1)S(1)} %get-tuple-element.1025, bf16[3072,16,64]{0,2,1:T(8,128)(2,1)} %get-tuple-element.1030), kind=kOutput, calls=%fused_computation.125 | convolution fusion | flops 2415919104 | bytes 82575360 | tf_op jit(solution)/shard_map/qhe,khe->hqk/dot_general | solution.py:53
  382.9 49.0 %all-gather.17.cloned.1.call-done = bf16[4096,1024]{1,0:T(8,128)(2,1)} async-done(((bf16[4096,256]{1,0:T(8,128)(2,1)}), bf16[4096,1024]{1,0:T(8,128)(2,1)}) %all-gather.17.cloned.1.call-update) | async-done | bytes 8388624 | tf_op jit(solution)/shard_map/all_gather | solution.py:115
  431.9 9.5 fusion.85
  445.1 10.6 fusion.86
  467.8 43.1 %while.60 = (s32[]{:T(128)}, f32[16,384]{1,0:T(8,128)S(1)}, bf16[3072,16,64]{0,2,1:T(8,128)(2,1)}, bf16[384,16,64]{0,2,1:T(8,128)(2,1)S(1)}, f32[16,384]{1,0:T(8...) while((s32[]{:T(128)}, f32[16,384]{1,0:T(8,128)S(1)}, ...), condition=%wide.region_16.0_spmd.clone, body=%wide.region_14.16_spmd.clone.sunk | while | flops 817895424 | bytes 28958892 | solution.py:158
  510.9 29.1 %fusion.48 = bf16[16,64,3072]{2,1,0:T(8,128)(2,1)} fusion(bf16[384,16,64]{0,2,1:T(8,128)(2,1)S(1)} %get-tuple-element.1038, f32[16,384,3072]{2,1,0:T(8,128)} %fusion.87, f32[16,384]{1,0:T(8,128)S(1)} %get-tuple-element.1055), kind=kOutput, calls=%fused_computation.58 | convolution fusion | flops 2475687936 | bytes 82599936 | tf_op jit(solution)/shard_map/hqk,qhe->khe/dot_general | solution.py:181
  540.0 34.3 %multiply_convert_fusion.6 = bf16[16,64,3072]{2,1,0:T(8,128)(2,1)} fusion(bf16[384,16,64]{0,2,1:T(8,128)(2,1)S(1)} %get-tuple-element.1026, f32[16,384,3072]{2,1,0:T(8,128)} %fusion.87, f32[16,384]{1,0:T(8,128)S(1)} %get-tuple-element.987, f32[16,384]{1,0:T(8,128)S(1)} %get-tuple-element.1055, bf16[384,16,64]{0,2,1:T(8,128)(2,1)S(1)} %get-tuple-element.1038, ...), kind=kOutput, calls=%fused_computation.47 | convolution fusion | flops 4932501504 | bytes 89702400 | tf_op jit(solution)/shard_map/hqk,qhe->khe/dot_general | solution.py:179
  574.2 10.5 pad_maximum_fusion
  584.7 16.1 copy.68
  603.4 112.4 %while.61 = (s32[]{:T(128)}, f32[384,16,64]{0,2,1:T(8,128)}, bf16[3072,16,64]{0,2,1:T(8,128)(2,1)}, bf16[384,16,64]{0,2,1:T(8,128)(2,1)S(1)}, f32[16,384]{1,0:T(...) while((s32[]{:T(128)}, f32[384,16,64]{0,2,1:T(8,128)}, ...), condition=%wide.region_18.19_spmd.clone, body=%wide.region_17.0_spmd.clone.sunk | while | flops 1224474624 | bytes 45663976 | solution.py:169
  612.0 9.7 bitcast_add_fusion.5
  630.6 9.7 bitcast_add_fusion.5
  649.2 9.7 bitcast_add_fusion.5
  667.7 9.7 bitcast_add_fusion.5
  686.3 9.7 bitcast_add_fusion.5
  704.9 9.7 bitcast_add_fusion.5
  757.4 60.4 %concatenate.17 = f32[1024,12416]{1,0:T(8,128)} concatenate(f32[1024,4096]{1,0:T(8,128)} %fusion.52, f32[1024,4096]{1,0:T(8,128)} %fusion.68, f32[1024,3072]{1,0:T(8,128)} %convolution_bitcast_fusion, f32[1024,1024]{1,0:T(8,128)} %fusion.65, f32[1024,1]{1,0:T(8,128)} %stack.32, f32[1024,1]{1,0:T(8,128)S(1)} %copy.58, f32[1024,1]{1,0:T(8,128)} %copy.59, f32[1024,1]{1,0:T(8,128)} %copy.60, ...), dimensions={1} | concatenate | bytes 101711872 | tf_op jit(solution)/shard_map/concatenate | solution.py:219
  826.1 1037.2 %reduce-scatter.5.cloned.1.call-done = f32[32,12416]{1,0:T(8,128)} async-done(((f32[1024,12416]{1,0:T(8,128)}), f32[32,12416]{1,0:T(8,128)}) %reduce-scatter.5.cloned.1.call-update) | async-done | bytes 1589264 | tf_op jit(solution)/shard_map/reduce_scatter | solution.py:218
  (232 shorter events, 327.7 us)
Async XLA Ops:
  7.2 73.0 %all-gather.7.cloned.1.call-start = ((), (), s32[]{:S(2)}) async-start(), calls=%async_computation.2 | async-start | bytes 7864320 | tf_op jit(solution)/shard_map/all_gather | solution.py:62
  7.9 144.2 %all-gather.11.cloned.1.call-start = ((), (), s32[]{:S(2)}) async-start(), calls=%async_computation.4 | async-start | bytes 7077888 | tf_op jit(solution)/shard_map/all_gather | solution.py:68
  9.0 422.8 %copy-start.20 = (f32[1,1024]{1,0:T(1,128)}, f32[1,1024]{1,0:T(1,128)S(1)}, u32[]{:S(2)}) copy-start(f32[1,1024]{1,0:T(1,128)S(1)} %get-tuple-element.709) | copy-start | bytes 12292
  9.0 455.1 %copy-start.18 = (f32[1,1024]{1,0:T(1,128)}, f32[1,1024]{1,0:T(1,128)S(1)}, u32[]{:S(2)}) copy-start(f32[1,1024]{1,0:T(1,128)S(1)} %get-tuple-element.710) | copy-start | bytes 12292
  87.2 160.9 %all-gather.9.cloned.1.call-start = ((), (), s32[]{:S(2)}) async-start(), calls=%async_computation.3 | async-start | bytes 7077888 | tf_op jit(solution)/shard_map/all_gather | solution.py:69
  88.0 204.0 %all-gather.13.cloned.1.call-start = ((), (), s32[]{:S(2)}) async-start(), calls=%async_computation.5 | async-start | bytes 2621440 | tf_op jit(solution)/shard_map/all_gather | solution.py:108
  88.5 254.1 %all-gather.15.cloned.1.call-start = ((), (), s32[]{:S(2)}) async-start(), calls=%async_computation.6 | async-start | bytes 10485760 | tf_op jit(solution)/shard_map/all_gather | solution.py:112
  89.1 342.8 %all-gather.17.cloned.1.call-start = ((), (), s32[]{:S(2)}) async-start(), calls=%async_computation.7 | async-start | bytes 10485760 | tf_op jit(solution)/shard_map/all_gather | solution.py:115
  89.7 657.6 %reduce-scatter.7.cloned.1.call-start = ((), (), s32[]{:S(2)}) async-start(), calls=%async_computation.9 | async-start | bytes 14155776
  290.4 52.3 %copy-start.32 = (f32[4096]{0:T(1024)S(1)}, f32[4096]{0:T(1024)}, u32[]{:S(2)}) copy-start(f32[4096]{0:T(1024)} %param.22) | copy-start | bytes 49156
  291.9 59.7 %copy-start.4 = (bf16[384,16,64]{0,2,1:T(8,128)(2,1)}, bf16[384,16,64]{0,2,1:T(8,128)(2,1)S(1)}, u32[]{:S(2)}) copy-start(bf16[384,16,64]{0,2,1:T(8,128)(2,1)S(1)} %convert_element_type.57) | copy-start | bytes 2359300
  295.1 169.0 %copy-start = (f32[384,1024]{1,0:T(8,128)}, f32[384,1024]{1,0:T(8,128)S(1)}, u32[]{:S(2)}) copy-start(f32[384,1024]{1,0:T(8,128)S(1)} %get-tuple-element.716) | copy-start | bytes 4718596
  295.1 169.0 %copy-start.22 = (f32[384]{0:T(512)}, f32[384]{0:T(512)S(1)}, u32[]{:S(2)}) copy-start(f32[384]{0:T(512)S(1)} %broadcast_multiply_fusion.5) | copy-start | bytes 4612
  295.4 168.7 %copy-start.24 = (f32[384]{0:T(512)}, f32[384]{0:T(512)S(1)}, u32[]{:S(2)}) copy-start(f32[384]{0:T(512)S(1)} %add_rsqrt_fusion.1) | copy-start | bytes 4612
  431.9 13.3 slice-start
  600.9 1262.4 %reduce-scatter.5.cloned.1.call-start = ((), (), s32[]{:S(2)}) async-start(), calls=%async_computation.8 | async-start | bytes 52445184 | tf_op jit(solution)/shard_map/reduce_scatter | solution.py:218
  603.4 115.4 %copy-start.28 = (f32[1024]{0:T(1024)S(1)}, f32[1024]{0:T(1024)}, u32[]{:S(2)}) copy-start(f32[1024]{0:T(1024)} %get-tuple-element.695) | copy-start | bytes 12292
  603.4 116.4 %copy-start.31 = (f32[1024]{0:T(1024)S(1)}, f32[1024]{0:T(1024)}, u32[]{:S(2)}) copy-start(f32[1024]{0:T(1024)} %get-tuple-element.636) | copy-start | bytes 12292
  603.4 117.5 %copy-start.30 = (f32[1024]{0:T(1024)S(1)}, f32[1024]{0:T(1024)}, u32[]{:S(2)}) copy-start(f32[1024]{0:T(1024)} %get-tuple-element.640) | copy-start | bytes 12292
  603.4 118.6 %copy-start.29 = (f32[4096]{0:T(1024)S(1)}, f32[4096]{0:T(1024)}, u32[]{:S(2)}) copy-start(f32[4096]{0:T(1024)} %get-tuple-element.720) | copy-start | bytes 49156
  603.4 119.9 %copy-start.27 = (f32[1024]{0:T(1024)S(1)}, f32[1024]{0:T(1024)}, u32[]{:S(2)}) copy-start(f32[1024]{0:T(1024)} %get-tuple-element.693) | copy-start | bytes 12292
  603.4 120.9 %copy-start.26 = (f32[1024]{0:T(1024)S(1)}, f32[1024]{0:T(1024)}, u32[]{:S(2)}) copy-start(f32[1024]{0:T(1024)} %get-tuple-element.634) | copy-start | bytes 12292
  717.5 31.8 %copy-start.10 = (bf16[384,16,64]{0,2,1:T(8,128)(2,1)}, bf16[384,16,64]{0,2,1:T(8,128)(2,1)S(1)}, u32[]{:S(2)}) copy-start(bf16[384,16,64]{0,2,1:T(8,128)(2,1)S(1)} %get-tuple-element.706) | copy-start | bytes 2359300
  725.4 13.3 slice-start.2
  (31 other events, 200.0 us)
Sparse Core Ops, SparseCore 0:
  9.8 70.2 all-gather.6
  87.3 64.7 all-gather.10
  154.3 63.3 all-gather.8
  219.5 33.8 all-gather.12
  255.0 87.5 all-gather.14
  344.3 87.4 all-gather.16
  601.0 128.4 reduce-scatter.6
  818.0 1045.2 reduce-scatter.4
where the time goes:
time: 1910 us; the launch traced here: 1880 us
  waiting for transfers between devices  1270 us (66%)
  matrix products  404 us (21%)
  local copies, waits for them, and re-layouts  128 us (7%)
  other arithmetic  60.6 us (3%)
    reduce_scatter x1, waiting for transfers between devices, on_device(): lax.psum_scatter(jnp.concatenate([jnp.concatenate([outer_rows(normed_low,...  1040 us
    dot_general x19, matrix products, scores_of(): jnp.einsum('qhe,khe->hqk', query3, key_block, preferred_element_type=jnp....  142 us
    all_gather x1, waiting for transfers between devices, on_device(): lax.all_gather(w_qkv, 'fsdp', axis=1, tiled=True)  71.1 us
    all_gather x1, waiting for transfers between devices, on_device(): lax.all_gather(keys, 'ctx', axis=0, tiled=True)  61.8 us
    concatenate x1, local copies, waits for them, and re-layouts, on_device(): jnp.concatenate([jnp.concatenate([outer_rows(normed_low, grad_pre_low, st...  60.4 us
    dot_general x6, matrix products, query_step(): jnp.einsum('hqk,khe->qhe', grad_scores, key_block, preferred_element_type...  58.4 us
    all_gather x1, waiting for transfers between devices, on_device(): lax.all_gather(w_back, 'fsdp', axis=1, tiled=True)  49 us
    all_gather x1, waiting for transfers between devices, on_device(): lax.all_gather(w_in, 'fsdp', axis=1, tiled=True)  47.3 us
  transfers between devices with their start and end apart: 8, of which 5 were waited for; matrix products, arithmetic and copies ran while one was open for 17% of the time, Pallas kernels for 0%

commit v1 on v0

v1 whole, which is shorter than its diff:
```python
from functools import partial
import math

import jax
import jax.numpy as jnp
from jax import lax
from jax.experimental import pallas as pl
from jax.experimental.pallas import tpu as pltpu
from jax.sharding import PartitionSpec as P

HEADS = 16
HEAD = 64
EPS = 1e-12
F32 = jnp.float32
BF16 = jnp.bfloat16
NN = (((1,), (0,)), ((), ()))
NT = (((1,), (1,)), ((), ()))
TN = (((0,), (0,)), ((), ()))
VMEM_LIMIT = 50 * 1024 * 1024


def dot(left, right, dims):
    return lax.dot_general(left, right, dims, preferred_element_type=F32)


def one_head(block, head, heads):
    if heads == 1:
        return block
    lane = lax.broadcasted_iota(jnp.int32, block.shape, 1)
    return jnp.where(lane // HEAD == head, block, jnp.zeros_like(block))


def merge_heads(parts):
    if len(parts) == 1:
        return parts[0]
    lane = lax.broadcasted_iota(jnp.int32, parts[0].shape, 1)
    result = parts[0]
    for head in range(1, len(parts)):
        result = jnp.where(lane // HEAD == head, parts[head], result)
    return result


def attend_kernel(*refs, blocks, heads, q_rows, k_rows):
    ins, rest = refs[:blocks], refs[blocks:]
    outs, (full_ref, lse_ref, key_s, value_s) = rest[:blocks], rest[blocks:]
    rows = ins[0].shape[0]
    width = heads * HEAD
    length = rows * blocks
    for b in range(blocks):
        here = slice(b * rows, (b + 1) * rows)
        key_s[here, :] = ins[b][:, width : 2 * width]
        value_s[here, :] = ins[b][:, 2 * width : 3 * width]
    for b in range(blocks):

        def step(i, carry, b=b):
            local = pl.ds(pl.multiple_of(i * q_rows, q_rows), q_rows)
            where = pl.ds(pl.multiple_of(b * rows + i * q_rows, q_rows), q_rows)
            query = ins[b][local, 0:width] * BF16(HEAD**-0.5)
            outputs, sums = [], []
            for head in range(heads):
                masked = one_head(query, head, heads)
                scores = [
                    dot(masked, key_s[j : j + k_rows, :], NT) for j in range(0, length, k_rows)
                ]
                top = None
                for part in scores:
                    part_top = jnp.max(part, axis=1, keepdims=True)
                    top = part_top if top is None else jnp.maximum(top, part_top)
                total = acc = None
                for j, part in enumerate(scores):
                    probs = jnp.exp(part - top)
                    part_total = jnp.sum(probs, axis=1, keepdims=True)
                    value = value_s[j * k_rows : (j + 1) * k_rows, :]
                    part_acc = dot(probs.astype(BF16), value, NN)
                    total = part_total if total is None else total + part_total
                    acc = part_acc if acc is None else acc + part_acc
                outputs.append(acc / total)
                sums.append(jnp.broadcast_to(top + jnp.log(total), (q_rows, width)))
            result = merge_heads(outputs)
            full_ref[where, :] = result
            outs[b][local, :] = result.astype(BF16)
            lse_ref[where, :] = merge_heads(sums)
            return carry

        lax.fori_loop(0, rows // q_rows, step, 0)


def attend(qkv, heads):
    blocks = len(qkv)
    rows = qkv[0].shape[0]
    width = heads * HEAD
    length = rows * blocks
    out = [jax.ShapeDtypeStruct((rows, width), BF16)] * blocks
    out += [jax.ShapeDtypeStruct((length, width), F32)] * 2
    results = pl.pallas_call(
        partial(attend_kernel, blocks=blocks, heads=heads, q_rows=256, k_rows=512),
        out_shape=out,
        scratch_shapes=[pltpu.VMEM((length, width), BF16)] * 2,
        compiler_params=pltpu.CompilerParams(vmem_limit_bytes=VMEM_LIMIT),
        cost_estimate=pl.CostEstimate(
            flops=16 * length * length * width, bytes_accessed=10 * length * width,
            transcendentals=heads * length * length,
        ),
        name="attend",
    )(*qkv)
    return results[:blocks], results[blocks], results[blocks + 1]


def attend_back_kernel(*refs, blocks, heads, q_rows, k_rows):
    ins, grads, rest = refs[:blocks], refs[blocks : 2 * blocks], refs[2 * blocks :]
    full_ref, lse_ref, rest = rest[0], rest[1], rest[2:]
    outs, (lse_t, delta_t, gq_t, key_t) = rest[:blocks], rest[blocks:]
    rows = ins[0].shape[0]
    width = heads * HEAD
    scale = HEAD**-0.5
    chunk = 256
    for b in range(blocks):
        for i in range(0, rows, chunk):
            local = slice(i, i + chunk)
            where = slice(b * rows + i, b * rows + i + chunk)
            logs = lse_ref[where, :].T
            terms = (grads[b][local, :].astype(F32) * full_ref[where, :]).T
            for head in range(heads):
                first = head * HEAD
                lse_t[head : head + 1, where] = logs[first : first + 1]
                delta_t[head : head + 1, where] = jnp.sum(
                    terms[first : first + HEAD], axis=0, keepdims=True
                )
        key_t[:, b * rows : (b + 1) * rows] = ins[b][:, width : 2 * width].T
    gq_t[...] = jnp.zeros_like(gq_t)
    for b in range(blocks):

        def step(j, carry, b=b):
            local = pl.ds(pl.multiple_of(j * k_rows, k_rows), k_rows)
            where = pl.ds(pl.multiple_of(b * rows + j * k_rows, k_rows), k_rows)
            key = ins[b][local, width : 2 * width]
            value = ins[b][local, 2 * width : 3 * width]
            key_grads, value_grads = [], []
            for head in range(heads):
                feats = slice(head * HEAD, (head + 1) * HEAD)
                key_h = one_head(key, head, heads) * BF16(scale)
                value_h = one_head(value, head, heads)
                key_grad = value_grad = None
                for other in range(blocks):
                    for i in range(0, rows, q_rows):
                        here = slice(i, i + q_rows)
                        there = slice(other * rows + i, other * rows + i + q_rows)
                        query = ins[other][here, 0:width]
                        grad = grads[other][here, :]
                        scores = dot(key_h, query, NT)
                        probs = jnp.exp(scores - lse_t[head : head + 1, there])
                        grad_probs = dot(value_h, grad, NT)
                        grad_scores = probs * (grad_probs - delta_t[head : head + 1, there])
                        grad_scores = grad_scores.astype(BF16)
                        term = dot(probs.astype(BF16), grad, NN)
                        value_grad = term if value_grad is None else value_grad + term
                        term = dot(grad_scores, query, NN)
                        key_grad = term if key_grad is None else key_grad + term
                        gq_t[feats, there] += dot(key_t[feats, where], grad_scores, NN)
                key_grads.append(key_grad)
                value_grads.append(value_grad)
            outs[b][local, width : 2 * width] = (merge_heads(key_grads) * scale).astype(BF16)
            outs[b][local, 2 * width : 3 * width] = merge_heads(value_grads).astype(BF16)
            return carry

        lax.fori_loop(0, rows // k_rows, step, 0)
    for b in range(blocks):
        for i in range(0, rows, chunk):
            there = slice(b * rows + i, b * rows + i + chunk)
            outs[b][i : i + chunk, 0:width] = (gq_t[:, there].T * scale).astype(BF16)


def attend_back(qkv, grads, full, lse, heads):
    blocks = len(qkv)
    rows = qkv[0].shape[0]
    width = heads * HEAD
    length = rows * blocks
    return pl.pallas_call(
        partial(attend_back_kernel, blocks=blocks, heads=heads, q_rows=256, k_rows=rows),
        out_shape=[jax.ShapeDtypeStruct((rows, 3 * width), BF16)] * blocks,
        scratch_shapes=[
            pltpu.VMEM((8, length), F32),
            pltpu.VMEM((8, length), F32),
            pltpu.VMEM((width, length), F32),
            pltpu.VMEM((width, length), BF16),
        ],
        compiler_params=pltpu.CompilerParams(vmem_limit_bytes=VMEM_LIMIT),
        cost_estimate=pl.CostEstimate(
            flops=40 * length * length * width, bytes_accessed=20 * length * width,
            transcendentals=heads * length * length,
        ),
        name="attend_back",
    )(*qkv, *grads, full, lse)


def norm_fwd(resid, gain, shift):
    centre = resid - jnp.mean(resid, axis=-1, keepdims=True)
    spread = jnp.mean(centre * centre, axis=-1, keepdims=True)
    rstd = lax.rsqrt(spread + EPS)
    unit = centre * rstd
    return (unit * gain + shift, unit, rstd)


def norm_back(grad, unit, rstd, gain):
    scaled = grad * gain
    inner = (
        scaled
        - jnp.mean(scaled, axis=-1, keepdims=True)
        - unit * jnp.mean(scaled * unit, axis=-1, keepdims=True)
    )
    return (rstd * inner, jnp.sum(grad * unit, axis=0), jnp.sum(grad, axis=0))


def gelu_both(pre):
    slope = math.sqrt(2.0 / math.pi)
    square = pre * pre
    th = jnp.tanh(slope * (pre + 0.044715 * pre * square))
    half = 0.5 * (1.0 + th)
    grad = half + 0.5 * pre * (1.0 - th * th) * (slope * (1.0 + 3 * 0.044715 * square))
    return pre * half, grad


def on_device(x_in, w_qkv, w_out, w_in, w_back, vectors, bias_in, cot, *, n_ctx, n_f):
    ctx, fs = lax.axis_index("ctx"), lax.axis_index("fsdp")
    core, zed = ctx % 2, ctx // 2
    n_z = n_ctx // 2
    x_own = x_in[0]
    grad_out = cot[0]
    rows, width = x_own.shape
    hidden = w_back.shape[0]
    half_heads = HEADS // 2
    heads = half_heads // n_z
    wide = heads * HEAD

    def swap(v):
        return lax.ppermute(v, "ctx", [(i, i ^ 1) for i in range(n_ctx)])

    def over_z(v, m):
        return lax.ppermute(v, "ctx", [(i, i ^ (2 * m)) for i in range(n_ctx)])

    def over_f(v, m):
        return lax.ppermute(v, "fsdp", [(i, i ^ m) for i in range(n_f)])

    bits = [1 << b for b in range(n_f.bit_length() - 1)]

    def pair(v):
        return jnp.concatenate([v, swap(v)], axis=0)

    def pair_sum(partial_sum):
        return partial_sum[:rows] + swap(partial_sum[rows:])

    def place(pieces, index, axis):
        count = len(pieces)
        for bit in range(count.bit_length() - 1):
            flag = (index >> bit) & 1
            pieces = [jnp.where(flag, pieces[m ^ (1 << bit)], pieces[m]) for m in range(count)]
        return jnp.concatenate(pieces, axis=axis)

    def gather_cols(shard):
        half = shard.shape[0] // 2
        parts = []
        for piece, order in ((shard[:half], bits), (shard[half:], bits[1:] + bits[:1])):
            held = {0: piece}
            for bit in order:
                for m in list(held):
                    held[m ^ bit] = over_f(held[m], bit)
            parts.append(place([held[m] for m in range(n_f)], fs, 1))
        return jnp.concatenate(parts, axis=0)

    def after(value, *others):
        return lax.optimization_barrier((value,) + others)[0]

    half_in = width // 2
    mine = lax.dynamic_slice_in_dim(w_qkv, core * half_in, half_in, 0)
    all_cols = gather_cols(mine).reshape(half_in, 3, 2, width // 2)
    keep = lax.dynamic_index_in_dim(all_cols, core, 2, False)
    give = lax.dynamic_index_in_dim(all_cols, 1 - core, 2, False)
    got = swap(give)
    w_attn = place([keep, got], core, 0)
    w_attn = w_attn.reshape(width, 3, n_z, wide).transpose(0, 2, 1, 3).reshape(width, -1)

    ff_part = w_in.shape[1] // 2
    token = w_attn[0, 0]
    wo_mine = lax.dynamic_slice_in_dim(w_out, core * (width // 2), width // 2, 0)
    wo_half = gather_cols(after(wo_mine, got))
    wi_mine = lax.dynamic_slice_in_dim(w_in, core * ff_part, ff_part, 1)
    wi_half = gather_cols(after(wi_mine, wo_half))
    wb_mine = lax.dynamic_index_in_dim(
        w_back.reshape(n_f, 2, ff_part, w_back.shape[1]), core, 1, False
    ).reshape(n_f * ff_part, -1)
    wb_half = gather_cols(after(wb_mine, wi_half))

    x_two = pair(x_own)
    span = 3 * wide
    bias_q = vectors[0].reshape(2, n_z, 1, wide)
    bias_v = vectors[1].reshape(2, n_z, 1, wide)
    bias_qkv = jnp.concatenate([bias_q, jnp.zeros_like(bias_q), bias_v], axis=2)
    bias_qkv = lax.dynamic_index_in_dim(bias_qkv.reshape(2, n_z * span), core, 0, False)
    qkv = []
    for m in range(n_z):
        start = (zed ^ m) * span
        w_part = lax.dynamic_slice_in_dim(w_attn, start, span, 1)
        b_part = lax.dynamic_slice_in_dim(bias_qkv, start, span, 0)
        block = (dot(x_two, w_part, NN) + b_part).astype(BF16)
        qkv.append(block if m == 0 else over_z(block, m))
    att, att_full, lse = attend(qkv, heads)
    att = [att[m] if m == 0 else over_z(att[m], m) for m in range(n_z)]
    att_half = place(att, zed, 1)

    resid_one = (
        x_own.astype(F32) + pair_sum(dot(att_half, wo_half, NN)) + vectors[2]
    )
    normed, unit_one, rstd_one = norm_fwd(resid_one, vectors[3], vectors[4])
    h_two = pair(normed.astype(BF16))
    bias_half = lax.dynamic_index_in_dim(
        bias_in.reshape(n_f, 2, ff_part), core, 1, False
    ).reshape(-1)
    pre = dot(h_two, wi_half, NN) + bias_half
    act, slope = gelu_both(pre)
    act = act.astype(BF16)
    resid_two = normed + pair_sum(dot(act, wb_half, NN)) + vectors[5]
    result, unit_two, rstd_two = norm_fwd(resid_two, vectors[6], vectors[7])
    layer_out = result.astype(BF16)[None]
    grad_two, gain_two, shift_two = norm_back(grad_out, unit_two, rstd_two, vectors[6])
    g_two = pair(grad_two.astype(BF16))
    grad_pre = dot(g_two, wb_half, NT) * slope
    grad_pre_low = grad_pre.astype(BF16)
    grad_normed = grad_two + pair_sum(dot(grad_pre_low, wi_half, NT))
    grad_one, gain_one, shift_one = norm_back(grad_normed, unit_one, rstd_one, vectors[3])
    g_one = pair(grad_one.astype(BF16))
    grad_att = dot(g_one, wo_half, NT).astype(BF16)
    g_att = []
    for m in range(n_z):
        block = lax.dynamic_slice_in_dim(grad_att, (zed ^ m) * wide, wide, 1)
        g_att.append(block if m == 0 else over_z(block, m))

    def reduce_rows(partial_grad):
        cols = partial_grad.shape[1]
        low = width // (n_ctx * n_f)
        view = partial_grad.reshape((n_z, 2) + (2,) * len(bits) + (low, cols))
        done = []
        for side in range(2):
            now = view[:, side]
            order = bits if side == 0 else bits[1:] + bits[:1]
            left = list(reversed(bits))
            for bit in order:
                axis = 1 + left.index(bit)
                left.remove(bit)
                flag = (fs // bit) % 2
                stay = lax.dynamic_index_in_dim(now, flag, axis, False)
                go = lax.dynamic_index_in_dim(now, 1 - flag, axis, False)
                now = (stay.astype(F32) + over_f(go, bit).astype(F32)).astype(BF16)
            done.append(now)
        both = jnp.stack(done, axis=1)
        total = lax.dynamic_index_in_dim(both, zed, 0, False).astype(F32)
        for m in range(1, n_z):
            part = lax.dynamic_index_in_dim(both, zed ^ m, 0, False)
            total = total + over_z(part, m).astype(F32)
        stay = lax.dynamic_index_in_dim(total, core, 0, False)
        go = lax.dynamic_index_in_dim(total, 1 - core, 0, False)
        return stay, swap(go.astype(BF16)).astype(F32)

    def halves(stay, came, parts):
        low = stay.shape[0]
        first = jnp.where(core == 0, stay, came).reshape(low, parts, 1, -1)
        second = jnp.where(core == 0, came, stay).reshape(low, parts, 1, -1)
        return jnp.concatenate([first, second], axis=2).reshape(low, -1)

    ffn_grad = jnp.concatenate(
        [dot(h_two, grad_pre_low, TN).astype(BF16), dot(g_two, act, TN).astype(BF16)], axis=1
    )
    ffn_grad = after(ffn_grad, g_att[0])
    stay, came = reduce_rows(ffn_grad)
    n_half = hidden // 2
    in_weight_grad = halves(stay[:, :n_half], came[:, :n_half], n_f)
    back_weight_grad = halves(stay[:, n_half:], came[:, n_half:], n_f).T

    att_other = swap(att_half)
    att_other = jnp.concatenate([att_other[rows:], att_other[:rows]], axis=0)
    att_both = place([att_half, att_other], core, 1)
    out_cols = lax.dynamic_slice_in_dim(g_one, core * half_in, half_in, 1)
    out_grad = dot(att_both, out_cols, TN).astype(BF16)

    g_qkv = attend_back(qkv, g_att, att_full, lse, heads)
    g_qkv = [g_qkv[m] if m == 0 else over_z(g_qkv[m], m) for m in range(n_z)]
    g_qkv = place(g_qkv, zed, 1)
    grad_in = grad_one + pair_sum(dot(g_qkv, w_attn, NT))
    attn_grad = jnp.concatenate([dot(x_two, g_qkv, TN).astype(BF16), out_grad], axis=1)
    stay, came = reduce_rows(attn_grad)
    low = stay.shape[0]

    def heads_order(cols):
        return cols.reshape(low, n_z, 3, wide).transpose(0, 2, 1, 3).reshape(low, -1)

    cut = n_z * span
    qkv_weight_grad = halves(heads_order(stay[:, :cut]), heads_order(came[:, :cut]), 3)
    out_weight_grad = halves(stay[:, cut:], came[:, cut:], 1)

    def spread(half_row, parts):
        piece = half_row.reshape(parts, 1, -1)
        empty = jnp.zeros_like(piece)
        both = jnp.where(core == 0, jnp.concatenate([piece, empty], 1), jnp.concatenate([empty, piece], 1))
        return both.reshape(-1)

    sums = jnp.sum(g_qkv.astype(F32), axis=0).reshape(n_z, 3, wide)
    ratio = hidden // width
    early = jnp.stack(
        [
            jnp.sum(grad_one, axis=0),
            gain_one,
            shift_one,
            jnp.sum(grad_two, axis=0),
            gain_two,
            shift_two,
        ],
        axis=1,
    )
    bias_terms = spread(jnp.sum(grad_pre, axis=0), n_f).reshape(width, ratio)
    late = jnp.stack([spread(sums[:, 0], 1), spread(sums[:, 2], 1)], axis=1)
    table = jnp.concatenate([late, early, bias_terms], axis=1)
    table = jnp.pad(table, ((0, 0), (0, 128 - table.shape[1])))
    table = lax.psum_scatter(table, ("ctx", "fsdp"), scatter_dimension=0, tiled=True)
    vector_grad = table[:, :8].T
    in_bias_grad = table[:, 8 : 8 + ratio].reshape(-1)
    return (
        layer_out,
        grad_in[None],
        qkv_weight_grad,
        out_weight_grad,
        in_weight_grad,
        back_weight_grad,
        vector_grad,
        in_bias_grad,
    )


def solution(mesh):
    tokens = P("fsdp", "ctx", None)
    cols = P(None, "fsdp")
    shared = P(("ctx", "fsdp"), None)
    return jax.shard_map(
        partial(on_device, n_ctx=mesh.shape["ctx"], n_f=mesh.shape["fsdp"]),
        mesh=mesh,
        in_specs=(tokens, cols, cols, cols, cols, P(), P(), tokens),
        out_specs=(
            tokens,
            tokens,
            shared,
            shared,
            shared,
            P(None, ("ctx", "fsdp")),
            P(None, ("ctx", "fsdp")),
            P(("ctx", "fsdp")),
        ),
        check_vma=False,
    )
```

time: 1910 us -> 795 us (0.42)
  waiting for transfers between devices: 1270 us -> 363 us
  matrix products: 404 us -> 82.8 us
  Pallas kernels: 0 us -> 82.2 us
  starting transfers between devices: 0.52 us -> 72.3 us
  local copies, waits for them, and re-layouts: 128 us -> 57 us
  other arithmetic: 60.6 us -> 106 us
    reduce_scatter x1 -> x0, waiting for transfers between devices: 1040 us -> none  [on_device(): lax.psum_scatter(jnp.concatenate([jnp.concatenate([outer_rows(normed_low,...]
    dot_general x51 -> x15, matrix products: 404 us -> 82.8 us  [dot(): return lax.dot_general(left, right, dims, preferred_element_type=F32)]
    ppermute x0 -> x62, waiting for transfers between devices: none -> 261 us  [the longest x18 157 us: over_z(): return lax.ppermute(v, 'ctx', [(i, i ^ 2 * m) for i in range(n_ctx)])]
    all_gather x6 -> x0, waiting for transfers between devices: 229 us -> none  [the longest x1 71.1 us: on_device(): lax.all_gather(w_qkv, 'fsdp', axis=1, tiled=True)]
    unnamed x9 -> x2, waiting for transfers between devices: 2.99 us -> 102 us
    pallas_call x0 -> x2, Pallas kernels: none -> 82.2 us  [the longest x1 49.6 us: attend_back(): pl.pallas_call(partial(attend_back_kernel, blocks=blocks, heads=heads, q_...]
    ppermute x0 -> x62, starting transfers between devices: none -> 72.3 us  [the longest x18 30.8 us: over_z(): return lax.ppermute(v, 'ctx', [(i, i ^ 2 * m) for i in range(n_ctx)])]
    concatenate x1 -> x5, local copies, waits for them, and re-layouts: 60.4 us -> 5.41 us  [the longest x1 4.85 us: place(): return jnp.concatenate(pieces, axis=axis)]
  transfers between devices with their start and end apart: 8 -> 63, of which waited for: 5 -> 38; matrix products, arithmetic and copies ran while one was open for 17% -> 24% of each run, Pallas kernels for 0% -> 4%
where the time goes in v1:
time: 795 us; the launch traced here: 780 us
  waiting for transfers between devices  363 us (46%)
  other arithmetic  106 us (13%)
  matrix products  82.8 us (10%)
  Pallas kernels  82.2 us (10%)
  starting transfers between devices  72.3 us (9%)
  local copies, waits for them, and re-layouts  57 us (7%)
  between operations  15.7 us (2%)
    ppermute x18, waiting for transfers between devices, over_z(): return lax.ppermute(v, 'ctx', [(i, i ^ 2 * m) for i in range(n_ctx)])  157 us
    unnamed x2, waiting for transfers between devices  102 us
    ppermute x32, waiting for transfers between devices, over_f(): return lax.ppermute(v, 'fsdp', [(i, i ^ m) for i in range(n_f)])  94.7 us
    dot_general x15, matrix products, dot(): return lax.dot_general(left, right, dims, preferred_element_type=F32)  82.8 us
    concatenate x3, other arithmetic, gather_cols(): return jnp.concatenate(parts, axis=0)  52.7 us
    pallas_call x1, Pallas kernels, attend_back(): pl.pallas_call(partial(attend_back_kernel, blocks=blocks, heads=heads, q_...  49.6 us
    pallas_call x1, Pallas kernels, attend(): pl.pallas_call(partial(attend_kernel, blocks=blocks, heads=heads, q_rows=...  32.6 us
    ppermute x18, starting transfers between devices, over_z(): return lax.ppermute(v, 'ctx', [(i, i ^ 2 * m) for i in range(n_ctx)])  30.8 us
  transfers between devices with their start and end apart: 63, of which 38 were waited for; matrix products, arithmetic and copies ran while one was open for 24% of the time, Pallas kernels for 4%

profile of v1, /device:TPU:23, one launch (start us, length us, event | category | flops | bytes accessed | tf_op | source)
XLA Modules:
  0.0 779.5 jit_solution(8545595306629926824)
XLA Ops:
  10.8 8.1 %collective-permute-done.1 = bf16[256,768]{0,1:T(8,128)(2,1)} collective-permute-done((bf16[256,768]{0,1:T(8,128)(2,1)S(1)}, bf16[256,768]{0,1:T(8,128)(2,1)}, u32[]{:S(2)}, u32[]{:S(2)}) %collective-permute-start.1) | collective-permute-done | bytes 393248 | tf_op jit(solution)/shard_map/ppermute | solution.py:242
  27.5 8.4 %collective-permute-done.2 = bf16[256,768]{0,1:T(8,128)(2,1)} collective-permute-done((bf16[256,768]{0,1:T(8,128)(2,1)}, bf16[256,768]{0,1:T(8,128)(2,1)}, u32[]{:S(2)}, u32[]{:S(2)}) %collective-permute-start.2) | collective-permute-done | bytes 393248 | tf_op jit(solution)/shard_map/ppermute | solution.py:242
  38.6 20.6 %maximum_maximum_fusion.2 = bf16[512,3072]{0,1:T(8,128)(2,1)S(1)} fusion(bf16[256,768]{0,1:T(8,128)(2,1)S(1)} %get-tuple-element.129, bf16[256,768]{0,1:T(8,128)(2,1)S(1)} %get-tuple-element.128, bf16[256,768]{0,1:T(8,128)(2,1)S(1)} %get-tuple-element.127, bf16[256,768]{0,1:T(8,128)(2,1)S(1)} %get-tuple-element.126, ...), kind=kLoop, calls=%fused_computation.17 | loop fusion | flops 25165824 | bytes 6291456 | tf_op jit(solution)/shard_map/concatenate | solution.py:268
  119.3 8.6 %collective-permute-done.23 = bf16[512,512]{1,0:T(8,128)(2,1)S(1)} collective-permute-done((bf16[512,512]{1,0:T(8,128)(2,1)}, bf16[512,512]{1,0:T(8,128)(2,1)S(1)}, u32[]{:S(2)}, u32[]{:S(2)}) %collective-permute-start.23) | collective-permute-done | bytes 524320 | tf_op jit(solution)/shard_map/ppermute | solution.py:242
  131.8 13.8 %collective-permute-done.10.refs_3_ = bf16[768,384]{1,0:T(8,128)(2,1)S(1)} collective-permute-done((bf16[768,384]{1,0:T(8,128)(2,1)S(1)}, bf16[768,384]{1,0:T(8,128)(2,1)S(1)}, u32[]{:S(2)}, u32[]{:S(2)}) %collective-permute-start.10) | collective-permute-done | bytes 589856 | tf_op jit(solution)/shard_map/ppermute | solution.py:239
  145.7 11.7 %collective-permute-done.9.refs_2_ = bf16[768,384]{1,0:T(8,128)(2,1)S(1)} collective-permute-done((bf16[768,384]{1,0:T(8,128)(2,1)S(1)}, bf16[768,384]{1,0:T(8,128)(2,1)S(1)}, u32[]{:S(2)}, u32[]{:S(2)}) %collective-permute-start.9) | collective-permute-done | bytes 589856 | tf_op jit(solution)/shard_map/ppermute | solution.py:239
  157.3 32.6 %attend.1 = (bf16[768,128]{1,0:T(8,128)(2,1)S(1)}, bf16[768,128]{1,0:T(8,128)(2,1)}, bf16[768,128]{1,0:T(8,128)(2,1)}, bf16[768,128]{1,0:T(8,128)(2,1)}, f32[3072,128]{1,0:T(8,128)}, /*index=5*/f32[3072,128]{1,0:T(8,128)}) custom-call(bf16[768,384]{1,0:T(8,128)(2,1)S(1)} %fusion.28.refs_0_, bf16[768,384]{1,0:T(8,128)(2,1)S(1)} %collective-permute-done.8.refs_1_, ...), custom_call_target="tpu_custom_call" | custom-call | flops 19327352832 | bytes 3932160 | tf_op jit(solution)/shard_map/attend/pallas_call | solution.py:95
  195.2 12.4 %collective-permute-done.12 = bf16[768,128]{1,0:T(8,128)(2,1)} collective-permute-done((bf16[768,128]{1,0:T(8,128)(2,1)}, bf16[768,128]{1,0:T(8,128)(2,1)}, u32[]{:S(2)}, u32[]{:S(2)}) %collective-permute-start.12) | collective-permute-done | bytes 196640 | tf_op jit(solution)/shard_map/ppermute | solution.py:239
  221.0 11.2 %collective-permute-done.26 = bf16[512,512]{1,0:T(8,128)(2,1)S(1)} collective-permute-done((bf16[512,512]{1,0:T(8,128)(2,1)}, bf16[512,512]{1,0:T(8,128)(2,1)S(1)}, u32[]{:S(2)}, u32[]{:S(2)}) %collective-permute-start.26) | collective-permute-done | bytes 524320 | tf_op jit(solution)/shard_map/ppermute | solution.py:242
  233.5 29.9 %maximum_maximum_fusion = bf16[1024,2048]{1,0:T(8,128)(2,1)} fusion(bf16[512,512]{1,0:T(8,128)(2,1)S(1)} %get-tuple-element.105, bf16[512,512]{1,0:T(8,128)(2,1)S(1)} %get-tuple-element.104, bf16[512,512]{1,0:T(8,128)(2,1)S(1)} %get-tuple-element.103, bf16[512,512]{1,0:T(8,128)(2,1)S(1)} %get-tuple-element.102, bf16[512,512]{1,0:T(8,128)(2,1)S(1)} %copy-done.38, ...), kind=kLoop, calls=%fused_computation.7 | loop fusion | flops 33554432 | bytes 8388608 | tf_op jit(solution)/shard_map/concatenate | solution.py:268
  266.5 7.9 %collective-permute-done.28 = bf16[1024,256]{1,0:T(8,128)(2,1)S(1)} collective-permute-done((bf16[1024,256]{1,0:T(8,128)(2,1)S(1)}, bf16[1024,256]{1,0:T(8,128)(2,1)S(1)}, u32[]{:S(2)}, u32[]{:S(2)}) %collective-permute-start.28) | collective-permute-done | bytes 524320 | tf_op jit(solution)/shard_map/ppermute | solution.py:242
  279.7 8.8 %collective-permute-done.29 = bf16[1024,256]{1,0:T(8,128)(2,1)S(1)} collective-permute-done((bf16[1024,256]{1,0:T(8,128)(2,1)S(1)}, bf16[1024,256]{1,0:T(8,128)(2,1)S(1)}, u32[]{:S(2)}, u32[]{:S(2)}) %collective-permute-start.29) | collective-permute-done | bytes 524320 | tf_op jit(solution)/shard_map/ppermute | solution.py:242
  291.8 9.1 %collective-permute-done.31 = bf16[1024,256]{1,0:T(8,128)(2,1)S(1)} collective-permute-done((bf16[1024,256]{1,0:T(8,128)(2,1)}, bf16[1024,256]{1,0:T(8,128)(2,1)S(1)}, u32[]{:S(2)}, u32[]{:S(2)}) %collective-permute-start.31) | collective-permute-done | bytes 524320 | tf_op jit(solution)/shard_map/ppermute | solution.py:242
  331.9 29.7 %fusion.93 = (f32[2048]{0:T(1024)S(1)}, bf16[768,2048]{1,0:T(8,128)(2,1)}) fusion(f32[768,2048]{1,0:T(8,128)} %copy-done.67, f32[2048]{0:T(1024)S(1)} %bitcast.220, bf16[1024,256]{1,0:T(8,128)(2,1)S(1)} %get-tuple-element.97, bf16[1024,256]{1,0:T(8,128)(2,1)S(1)} %get-tuple-element.96, bf16[1024,256]{1,0:T(8,128)(2,1)S(1)} %get-tuple-element.95, ...), kind=kOutput, calls=%fused_computation.307 | convolution fusion | flops 3289380864 | bytes 15220736 | tf_op jit(solution)/shard_map/dot_general | solution.py:23
  374.8 8.7 %convolution_convert_fusion.1 = bf16[1024,2048]{1,0:T(8,128)(2,1)} fusion(bf16[384,1024]{1,0:T(8,128)(2,1)S(1)} %copy-done.64, bf16[384,1024]{1,0:T(8,128)(2,1)S(1)} %copy-done.50, f32[768,2048]{1,0:T(8,128)} %copy-done.67, f32[2048]{0:T(1024)S(1)} %bitcast.221), kind=kOutput, calls=%fused_computation.15 | convolution fusion | flops 3242196992 | bytes 12066816 | tf_op jit(solution)/shard_map/dot_general | solution.py:23
  395.4 8.0 %pad_maximum_fusion = bf16[1024,4096]{1,0:T(8,128)(2,1)} fusion(bf16[1024,2048]{1,0:T(8,128)(2,1)} %convolution_convert_fusion.1, bf16[1024,2048]{1,0:T(8,128)(2,1)} %convolution_convert_fusion.2), kind=kLoop, calls=%fused_computation | loop fusion | flops 16777216 | bytes 16777216 | tf_op jit(solution)/shard_map/concatenate | solution.py:369
  426.5 49.6 %attend_back.1 = (bf16[768,384]{1,0:T(8,128)(2,1)S(1)}, bf16[768,384]{1,0:T(8,128)(2,1)S(1)}, bf16[768,384]{1,0:T(8,128)(2,1)S(1)}, bf16[768,384]{1,0:T(8,128)(2,1)S(1)}) custom-call(bf16[768,384]{1,0:T(8,128)(2,1)S(1)} %copy-done.6, bf16[768,384]{1,0:T(8,128)(2,1)} %copy-done.4, bf16[768,384]{1,0:T(8,128)(2,1)} %copy-done.3, bf16[768,384]{1,0:T(8,128)(2,1)} %copy-done.2, ...), custom_call_target="tpu_custom_call" | custom-call | flops 48318382080 | bytes 7864320 | tf_op jit(solution)/shard_map/attend_back/pallas_call | solution.py:178
  483.1 31.3 %collective-permute-done.41 = bf16[768,384]{1,0:T(8,128)(2,1)S(1)} collective-permute-done((bf16[768,384]{1,0:T(8,128)(2,1)S(1)}, bf16[768,384]{1,0:T(8,128)(2,1)S(1)}, u32[]{:S(2)}, u32[]{:S(2)}) %collective-permute-start.41) | collective-permute-done | bytes 589856 | tf_op jit(solution)/shard_map/ppermute | solution.py:239
  514.4 11.6 %collective-permute-done.42 = bf16[768,384]{1,0:T(8,128)(2,1)S(1)} collective-permute-done((bf16[768,384]{1,0:T(8,128)(2,1)S(1)}, bf16[768,384]{1,0:T(8,128)(2,1)S(1)}, u32[]{:S(2)}, u32[]{:S(2)}) %collective-permute-start.42) | collective-permute-done | bytes 589856 | tf_op jit(solution)/shard_map/ppermute | solution.py:239
  549.0 101.7 %reduce-scatter.4.cloned.1.call-done = f32[32,128]{1,0:T(8,128)} async-done(((f32[1024,128]{1,0:T(8,128)}), f32[32,128]{1,0:T(8,128)}) %reduce-scatter.4.cloned.1.call-update) | async-done | bytes 16400
  671.7 12.8 %collective-permute-start.50 = (bf16[2,32,2048]{2,1,0:T(8,128)(2,1)S(1)}, bf16[2,32,2048]{2,1,0:T(8,128)(2,1)S(1)}, u32[]{:S(2)}, u32[]{:S(2)}) collective-permute-start(bf16[2,32,2048]{2,1,0:T(8,128)(2,1)S(1)} %get-tuple-element.134), channel_id=1, source_target_pairs={{0,8},{4,12},{8,0},{12,4},{16,24},{20,28},{24,16},{28,20},{1,9},{5... | collective-permute-start | bytes 786440 | tf_op jit(solution)/shard_map/ppermute | solution.py:239
  693.7 14.4 %collective-permute-done.52 = bf16[2,32,2048]{2,1,0:T(8,128)(2,1)S(1)} collective-permute-done((bf16[2,32,2048]{2,1,0:T(8,128)(2,1)S(1)}, bf16[2,32,2048]{2,1,0:T(8,128)(2,1)S(1)}, u32[]{:S(2)}, u32[]{:S(2)}) %collective-permute-start.52) | collective-permute-done | bytes 262176 | tf_op jit(solution)/shard_map/ppermute | solution.py:239
  718.4 16.9 %collective-permute-done.58 = bf16[2,32,4096]{2,1,0:T(8,128)(2,1)S(1)} collective-permute-done((bf16[2,32,4096]{2,1,0:T(8,128)(2,1)}, bf16[2,32,4096]{2,1,0:T(8,128)(2,1)S(1)}, u32[]{:S(2)}, u32[]{:S(2)}) %collective-permute-start.58) | collective-permute-done | bytes 524320 | tf_op jit(solution)/shard_map/ppermute | solution.py:239
  738.3 23.5 %collective-permute-done.60 = bf16[2,32,4096]{2,1,0:T(8,128)(2,1)} collective-permute-done((bf16[2,32,4096]{2,1,0:T(8,128)(2,1)}, bf16[2,32,4096]{2,1,0:T(8,128)(2,1)}, u32[]{:S(2)}, u32[]{:S(2)}) %collective-permute-start.60) | collective-permute-done | bytes 524320 | tf_op jit(solution)/shard_map/ppermute | solution.py:239
  (394 shorter events, 272.6 us)
Async XLA Ops:
  7.2 643.5 %reduce-scatter.4.cloned.1.call-start = ((), (), s32[]{:S(2)}) async-start(), calls=%async_computation.1 | async-start | bytes 540672
  70.2 33.3 %collective-permute-start = (bf16[384,1024]{1,0:T(8,128)(2,1)}, bf16[384,1024]{1,0:T(8,128)(2,1)}, u32[]{:S(2)}, u32[]{:S(2)}) collective-permute-start(bf16[384,1024]{1,0:T(8,128)(2,1)} %bitcast), channel_id=1, source_target_pairs={{0,4},{4,0},{8,12},{12,8},{16,20},{20,16},{24,28},{28,24},{1,5},{5... | collective-permute-start | bytes 2359304 | tf_op jit(solution)/shard_map/ppermute | solution.py:236
  107.0 38.6 %collective-permute-start.10 = (bf16[768,384]{1,0:T(8,128)(2,1)S(1)}, bf16[768,384]{1,0:T(8,128)(2,1)S(1)}, u32[]{:S(2)}, u32[]{:S(2)}) collective-permute-start(bf16[768,384]{1,0:T(8,128)(2,1)S(1)} %fusion.31), channel_id=1, source_target_pairs={{0,24},{4,28},{8,16},{12,20},{16,8},{20,12},{24,0},{28,4},{1,25},{... | collective-permute-start | bytes 1769480 | tf_op jit(solution)/shard_map/ppermute | solution.py:239
  111.1 46.2 %collective-permute-start.9 = (bf16[768,384]{1,0:T(8,128)(2,1)S(1)}, bf16[768,384]{1,0:T(8,128)(2,1)S(1)}, u32[]{:S(2)}, u32[]{:S(2)}) collective-permute-start(bf16[768,384]{1,0:T(8,128)(2,1)S(1)} %fusion.30), channel_id=1, source_target_pairs={{0,16},{4,20},{8,24},{12,28},{16,0},{20,4},{24,8},{28,12},{1,17},{... | collective-permute-start | bytes 1769480 | tf_op jit(solution)/shard_map/ppermute | solution.py:239
  116.8 40.6 %collective-permute-start.8 = (bf16[768,384]{1,0:T(8,128)(2,1)S(1)}, bf16[768,384]{1,0:T(8,128)(2,1)S(1)}, u32[]{:S(2)}, u32[]{:S(2)}) collective-permute-start(bf16[768,384]{1,0:T(8,128)(2,1)S(1)} %fusion.29), channel_id=1, source_target_pairs={{0,8},{4,12},{8,0},{12,4},{16,24},{20,28},{24,16},{28,20},{1,9},{5... | collective-permute-start | bytes 1769480 | tf_op jit(solution)/shard_map/ppermute | solution.py:239
  130.7 79.0 %collective-permute-start.25 = (bf16[512,512]{1,0:T(8,128)(2,1)}, bf16[512,512]{1,0:T(8,128)(2,1)}, u32[]{:S(2)}, u32[]{:S(2)}) collective-permute-start(bf16[512,512]{1,0:T(8,128)(2,1)} %get-tuple-element.138), channel_id=1, source_target_pairs={{0,2},{1,3},{2,0},{3,1},{4,6},{5,7},{6,4},{7,5},{8,10},{9,11},{10,... | collective-permute-start | bytes 1572872 | tf_op jit(solution)/shard_map/ppermute | solution.py:242
  209.7 22.5 %collective-permute-start.26 = (bf16[512,512]{1,0:T(8,128)(2,1)}, bf16[512,512]{1,0:T(8,128)(2,1)S(1)}, u32[]{:S(2)}, u32[]{:S(2)}) collective-permute-start(bf16[512,512]{1,0:T(8,128)(2,1)} %collective-permute-done.25), channel_id=1, source_target_pairs={{0,1},{1,0},{2,3},{3,2},{4,5},{5,4},{6,7},{7,6},{8,9},{9,8},{10,11... | collective-permute-start | bytes 1572872 | tf_op jit(solution)/shard_map/ppermute | solution.py:242
  212.8 51.5 %collective-permute-start.20 = (f32[384,1024]{1,0:T(8,128)S(1)}, f32[384,1024]{1,0:T(8,128)S(1)}, u32[]{:S(2)}, u32[]{:S(2)}) collective-permute-start(f32[384,1024]{1,0:T(8,128)S(1)} %slice.171), channel_id=1, source_target_pairs={{0,4},{4,0},{8,12},{12,8},{16,20},{20,16},{24,28},{28,24},{1,5},{5... | collective-permute-start | bytes 4718600 | tf_op jit(solution)/shard_map/ppermute | solution.py:236
  275.9 25.8 %collective-permute-start.21 = (bf16[384,1024]{1,0:T(8,128)(2,1)S(1)}, bf16[384,1024]{1,0:T(8,128)(2,1)}, u32[]{:S(2)}, u32[]{:S(2)}) collective-permute-start(bf16[384,1024]{1,0:T(8,128)(2,1)S(1)} %fusion.26), channel_id=1, source_target_pairs={{0,4},{4,0},{8,12},{12,8},{16,20},{20,16},{24,28},{28,24},{1,5},{5... | collective-permute-start | bytes 2359304 | tf_op jit(solution)/shard_map/ppermute | solution.py:236
  330.1 41.8 %collective-permute-start.45 = (bf16[768,512]{1,0:T(8,128)(2,1)S(1)}, bf16[768,512]{1,0:T(8,128)(2,1)}, u32[]{:S(2)}, u32[]{:S(2)}) collective-permute-start(bf16[768,512]{1,0:T(8,128)(2,1)S(1)} %pad_maximum_fusion.15), channel_id=1, source_target_pairs={{0,4},{4,0},{8,12},{12,8},{16,20},{20,16},{24,28},{28,24},{1,5},{5... | collective-permute-start | bytes 2359304 | tf_op jit(solution)/shard_map/ppermute | solution.py:236
  476.1 38.2 %collective-permute-start.41 = (bf16[768,384]{1,0:T(8,128)(2,1)S(1)}, bf16[768,384]{1,0:T(8,128)(2,1)S(1)}, u32[]{:S(2)}, u32[]{:S(2)}) collective-permute-start(bf16[768,384]{1,0:T(8,128)(2,1)S(1)} %get-tuple-element.31), channel_id=1, source_target_pairs={{0,24},{4,28},{8,16},{12,20},{16,8},{20,12},{24,0},{28,4},{1,25},{... | collective-permute-start | bytes 1769480 | tf_op jit(solution)/shard_map/ppermute | solution.py:239
  477.5 48.6 %collective-permute-start.42 = (bf16[768,384]{1,0:T(8,128)(2,1)S(1)}, bf16[768,384]{1,0:T(8,128)(2,1)S(1)}, u32[]{:S(2)}, u32[]{:S(2)}) collective-permute-start(bf16[768,384]{1,0:T(8,128)(2,1)S(1)} %get-tuple-element.32), channel_id=1, source_target_pairs={{0,16},{4,20},{8,24},{12,28},{16,0},{20,4},{24,8},{28,12},{1,17},{... | collective-permute-start | bytes 1769480 | tf_op jit(solution)/shard_map/ppermute | solution.py:239
  477.5 48.6 %collective-permute-start.43 = (bf16[768,384]{1,0:T(8,128)(2,1)S(1)}, bf16[768,384]{1,0:T(8,128)(2,1)S(1)}, u32[]{:S(2)}, u32[]{:S(2)}) collective-permute-start(bf16[768,384]{1,0:T(8,128)(2,1)S(1)} %get-tuple-element.33), channel_id=1, source_target_pairs={{0,8},{4,12},{8,0},{12,4},{16,24},{20,28},{24,16},{28,20},{1,9},{5... | collective-permute-start | bytes 1769480 | tf_op jit(solution)/shard_map/ppermute | solution.py:239
  480.4 177.5 %collective-permute-start.56 = (bf16[4,2,32,4096]{3,2,1,0:T(8,128)(2,1)}, bf16[4,2,32,4096]{3,2,1,0:T(8,128)(2,1)}, u32[]{:S(2)}, u32[]{:S(2)}) collective-permute-start(bf16[4,2,32,4096]{3,2,1,0:T(8,128)(2,1)} %dynamic-slice_bitcast_fusion), channel_id=1, source_target_pairs={{0,2},{1,3},{2,0},{3,1},{4,6},{5,7},{6,4},{7,5},{8,10},{9,11},{10,... | collective-permute-start | bytes 6291464 | tf_op jit(solution)/shard_map/ppermute | solution.py:242
  535.3 118.2 %collective-permute-start.48 = (bf16[4,2,32,2048]{3,2,0,1:T(8,128)(2,1)}, bf16[4,2,32,2048]{3,2,0,1:T(8,128)(2,1)}, u32[]{:S(2)}, u32[]{:S(2)}) collective-permute-start(bf16[4,2,32,2048]{3,2,0,1:T(8,128)(2,1)} %bitcast.174), channel_id=1, source_target_pairs={{0,2},{1,3},{2,0},{3,1},{4,6},{5,7},{6,4},{7,5},{8,10},{9,11},{10,... | collective-permute-start | bytes 3145736 | tf_op jit(solution)/shard_map/ppermute | solution.py:242
  538.6 122.7 %collective-permute-start.54 = (bf16[4,2,32,4096]{3,2,0,1:T(8,128)(2,1)}, bf16[4,2,32,4096]{3,2,0,1:T(8,128)(2,1)}, u32[]{:S(2)}, u32[]{:S(2)}) collective-permute-start(bf16[4,2,32,4096]{3,2,0,1:T(8,128)(2,1)} %bitcast.173), channel_id=1, source_target_pairs={{0,1},{1,0},{2,3},{3,2},{4,5},{5,4},{6,7},{7,6},{8,9},{9,8},{10,11... | collective-permute-start | bytes 6291464 | tf_op jit(solution)/shard_map/ppermute | solution.py:242
  541.4 114.4 %collective-permute-start.46 = (bf16[4,2,32,2048]{3,2,0,1:T(8,128)(2,1)}, bf16[4,2,32,2048]{3,2,0,1:T(8,128)(2,1)}, u32[]{:S(2)}, u32[]{:S(2)}) collective-permute-start(bf16[4,2,32,2048]{3,2,0,1:T(8,128)(2,1)} %bitcast.175), channel_id=1, source_target_pairs={{0,1},{1,0},{2,3},{3,2},{4,5},{5,4},{6,7},{7,6},{8,9},{9,8},{10,11... | collective-permute-start | bytes 3145736 | tf_op jit(solution)/shard_map/ppermute | solution.py:242
  548.1 136.3 %collective-permute-start.44 = (f32[384,1024]{1,0:T(8,128)}, f32[384,1024]{1,0:T(8,128)}, u32[]{:S(2)}, u32[]{:S(2)}) collective-permute-start(f32[384,1024]{1,0:T(8,128)} %slice.177), channel_id=1, source_target_pairs={{0,4},{4,0},{8,12},{12,8},{16,20},{20,16},{24,28},{28,24},{1,5},{5... | collective-permute-start | bytes 4718600 | tf_op jit(solution)/shard_map/ppermute | solution.py:236
  660.4 51.5 %collective-permute-start.57 = (bf16[4,32,4096]{2,1,0:T(8,128)(2,1)S(1)}, bf16[4,32,4096]{2,1,0:T(8,128)(2,1)S(1)}, u32[]{:S(2)}, u32[]{:S(2)}) collective-permute-start(bf16[4,32,4096]{2,1,0:T(8,128)(2,1)S(1)} %dynamic-slice_bitcast_fusion.1), channel_id=1, source_target_pairs={{0,1},{1,0},{2,3},{3,2},{4,5},{5,4},{6,7},{7,6},{8,9},{9,8},{10,11... | collective-permute-start | bytes 3145736 | tf_op jit(solution)/shard_map/ppermute | solution.py:242
  663.8 48.4 %collective-permute-start.55 = (bf16[4,32,4096]{2,1,0:T(8,128)(2,1)S(1)}, bf16[4,32,4096]{2,1,0:T(8,128)(2,1)S(1)}, u32[]{:S(2)}, u32[]{:S(2)}) collective-permute-start(bf16[4,32,4096]{2,1,0:T(8,128)(2,1)S(1)} %dynamic-slice_bitcast_fusion.2), channel_id=1, source_target_pairs={{0,2},{1,3},{2,0},{3,1},{4,6},{5,7},{6,4},{7,5},{8,10},{9,11},{10,... | collective-permute-start | bytes 3145736 | tf_op jit(solution)/shard_map/ppermute | solution.py:242
  684.4 23.6 %collective-permute-start.52 = (bf16[2,32,2048]{2,1,0:T(8,128)(2,1)S(1)}, bf16[2,32,2048]{2,1,0:T(8,128)(2,1)S(1)}, u32[]{:S(2)}, u32[]{:S(2)}) collective-permute-start(bf16[2,32,2048]{2,1,0:T(8,128)(2,1)S(1)} %get-tuple-element.136), channel_id=1, source_target_pairs={{0,24},{4,28},{8,16},{12,20},{16,8},{20,12},{24,0},{28,4},{1,25},{... | collective-permute-start | bytes 786440 | tf_op jit(solution)/shard_map/ppermute | solution.py:239
  713.7 21.6 %collective-permute-start.58 = (bf16[2,32,4096]{2,1,0:T(8,128)(2,1)}, bf16[2,32,4096]{2,1,0:T(8,128)(2,1)S(1)}, u32[]{:S(2)}, u32[]{:S(2)}) collective-permute-start(bf16[2,32,4096]{2,1,0:T(8,128)(2,1)} %get-tuple-element.110), channel_id=1, source_target_pairs={{0,8},{4,12},{8,0},{12,4},{16,24},{20,28},{24,16},{28,20},{1,9},{5... | collective-permute-start | bytes 1572872 | tf_op jit(solution)/shard_map/ppermute | solution.py:239
  713.7 24.6 %collective-permute-start.59 = (bf16[2,32,4096]{2,1,0:T(8,128)(2,1)}, bf16[2,32,4096]{2,1,0:T(8,128)(2,1)}, u32[]{:S(2)}, u32[]{:S(2)}) collective-permute-start(bf16[2,32,4096]{2,1,0:T(8,128)(2,1)} %get-tuple-element.111), channel_id=1, source_target_pairs={{0,16},{4,20},{8,24},{12,28},{16,0},{20,4},{24,8},{28,12},{1,17},{... | collective-permute-start | bytes 1572872 | tf_op jit(solution)/shard_map/ppermute | solution.py:239
  715.0 46.8 %collective-permute-start.60 = (bf16[2,32,4096]{2,1,0:T(8,128)(2,1)}, bf16[2,32,4096]{2,1,0:T(8,128)(2,1)}, u32[]{:S(2)}, u32[]{:S(2)}) collective-permute-start(bf16[2,32,4096]{2,1,0:T(8,128)(2,1)} %get-tuple-element.112), channel_id=1, source_target_pairs={{0,24},{4,28},{8,16},{12,20},{16,8},{20,12},{24,0},{28,4},{1,25},{... | collective-permute-start | bytes 1572872 | tf_op jit(solution)/shard_map/ppermute | solution.py:239
  (108 other events, 1546.5 us)
Sparse Core Ops, SparseCore 0:
  528.1 122.5 reduce-scatter.3

commit v2 on v1

--- a/solution.py
+++ b/solution.py
@@ -17,6 +17,8 @@
 NT = (((1,), (1,)), ((), ()))
 TN = (((0,), (0,)), ((), ()))
 VMEM_LIMIT = 50 * 1024 * 1024
+VMEM_MIDDLE = 56 * 1024 * 1024
+MESH = pl.DeviceIdType.MESH
 
 
 def dot(left, right, dims):
@@ -193,24 +195,6 @@
     )(*qkv, *grads, full, lse)
 
 
-def norm_fwd(resid, gain, shift):
-    centre = resid - jnp.mean(resid, axis=-1, keepdims=True)
-    spread = jnp.mean(centre * centre, axis=-1, keepdims=True)
-    rstd = lax.rsqrt(spread + EPS)
-    unit = centre * rstd
-    return (unit * gain + shift, unit, rstd)
-
-
-def norm_back(grad, unit, rstd, gain):
-    scaled = grad * gain
-    inner = (
-        scaled
-        - jnp.mean(scaled, axis=-1, keepdims=True)
-        - unit * jnp.mean(scaled * unit, axis=-1, keepdims=True)
-    )
-    return (rstd * inner, jnp.sum(grad * unit, axis=0), jnp.sum(grad, axis=0))
-
-
 def gelu_both(pre):
     slope = math.sqrt(2.0 / math.pi)
     square = pre * pre
@@ -218,6 +202,272 @@
     half = 0.5 * (1.0 + th)
     grad = half + 0.5 * pre * (1.0 - th * th) * (slope * (1.0 + 3 * 0.044715 * square))
     return pre * half, grad
+
+
+def row_stats(value):
+    return jnp.mean(value, axis=1, keepdims=True)
+
+
+def mid_kernel(*refs, n_f, n_z, cfg):
+    att_refs, refs = refs[:n_z], refs[n_z:]
+    (x_ref, cot_ref, vec_ref, bias_ref), refs = refs[:4], refs[4:]
+    wo_refs, refs = refs[: 2 * n_f], refs[2 * n_f :]
+    wi_refs, refs = refs[: 2 * n_f], refs[2 * n_f :]
+    wb_refs, refs = refs[: 2 * n_f], refs[2 * n_f :]
+    (layer_ref, grad_one_ref, att_ref, h_ref, act_ref, g2_ref, gp_ref, g1_ref), refs = refs[:8], refs[8:]
+    (sums_ref, bias_sum_ref), refs = refs[:2], refs[2:]
+    ga_refs, refs = refs[:n_z], refs[n_z:]
+    (wo_s, wi_s, wb_s, slope_s, normed_s, unit_s, acc_s, send_s, recv_s, rstd_s), refs = refs[:10], refs[10:]
+    w_sem, send_sem, recv_sem = refs
+    ctx, fs = lax.axis_index("ctx"), lax.axis_index("fsdp")
+    core, zed = ctx % 2, ctx // 2
+    partner = {"ctx": zed * 2 + (1 - core)}
+    rows, width = x_ref.shape
+    own, other = slice(0, rows), slice(rows, 2 * rows)
+    wide = att_refs[0].shape[1]
+    half_in = n_z * wide
+    ff_half = wi_s.shape[1]
+    step = cfg["step"]
+    chunk = cfg["rows"]
+
+    copies = []
+    for pieces, target in ((wo_refs, wo_s), (wi_refs, wi_s), (wb_refs, wb_s)):
+        group = []
+        for side in range(2):
+            for m in range(n_f):
+                piece = pieces[side * n_f + m]
+                p_rows, p_cols = piece.shape
+                where = pl.ds(pl.multiple_of((fs ^ m) * p_cols, p_cols), p_cols)
+                copy = pltpu.make_async_copy(
+                    piece, target.at[pl.ds(side * p_rows, p_rows), where], w_sem.at[len(copies), side * n_f + m]
+                )
+                copy.start()
+                group.append(copy)
+        copies.append(group)
+    barrier = pltpu.get_barrier_semaphore()
+    pl.semaphore_signal(barrier, inc=1, device_id=partner, device_id_type=MESH)
+    pl.semaphore_wait(barrier, 1)
+
+    def exchange(n, src, dst):
+        return pltpu.make_async_remote_copy(
+            src_ref=src, dst_ref=dst, send_sem=send_sem.at[n], recv_sem=recv_sem.at[n],
+            device_id=partner, device_id_type=MESH,
+        )
+
+    def over_cols(total, body):
+        def run(i, carry):
+            body(pl.ds(pl.multiple_of(i * step, step), step))
+            return carry
+
+        lax.fori_loop(0, total // step, run, 0)
+
+    def over_rows(body):
+        def run(i, carry):
+            return body(pl.ds(pl.multiple_of(i * chunk, chunk), chunk), carry)
+
+        zero = jnp.zeros((1, width), F32)
+        return lax.fori_loop(0, rows // chunk, run, (zero, zero, zero))
+
+    if wide % 128 == 0:
+        for m in range(n_z):
+            att_ref[:, pl.ds(pl.multiple_of((zed ^ m) * wide, wide), wide)] = att_refs[m][...]
+    else:
+        for m in range(0, n_z, 2):
+            one, two = att_refs[m][...].astype(F32), att_refs[m + 1][...].astype(F32)
+            odd = zed % 2 == 1
+            block = jnp.concatenate([jnp.where(odd, two, one), jnp.where(odd, one, two)], axis=1)
+            at = pl.ds(pl.multiple_of((zed // 2 ^ (m // 2)) * 2 * wide, 2 * wide), 2 * wide)
+            att_ref[:, at] = block.astype(BF16)
+
+    def wait_all(group):
+        for copy in group:
+            copy.wait()
+
+    wait_all(copies[0])
+
+    def out_other(cols):
+        send_s[:, cols] = dot(att_ref[other, :], wo_s[:, cols], NN)
+
+    over_cols(width, out_other)
+    move = exchange(0, send_s, recv_s)
+    move.start()
+
+    def out_own(cols):
+        part = dot(att_ref[own, :], wo_s[:, cols], NN)
+        acc_s[:, cols] = part + x_ref[:, cols].astype(F32) + vec_ref[2:3, cols]
+
+    over_cols(width, out_own)
+    move.wait()
+
+    def norm_one(r, carry):
+        resid = acc_s[r, :] + recv_s[r, :]
+        centre = resid - row_stats(resid)
+        rstd = lax.rsqrt(row_stats(centre * centre) + EPS)
+        unit = centre * rstd
+        normed = unit * vec_ref[3:4, :] + vec_ref[4:5, :]
+        unit_s[r, :] = unit
+        rstd_s[r, :] = jnp.broadcast_to(rstd, (chunk, 128))
+        normed_s[r, :] = normed
+        h_ref[r, :] = normed.astype(BF16)
+        return carry
+
+    over_rows(norm_one)
+    move = exchange(1, h_ref.at[own], h_ref.at[other])
+    move.start()
+
+    wait_all(copies[1])
+
+    def up(where):
+        def body(cols):
+            pre = dot(h_ref[where, :], wi_s[:, cols], NN) + bias_ref[0:1, cols]
+            act, slope = gelu_both(pre)
+            act_ref[where, cols] = act.astype(BF16)
+            slope_s[where, cols] = slope
+
+        over_cols(ff_half, body)
+
+    up(own)
+    move.wait()
+    up(other)
+    wait_all(copies[2])
+
+    def down_other(cols):
+        send_s[:, cols] = dot(act_ref[other, :], wb_s[:, cols], NN)
+
+    over_cols(width, down_other)
+    move = exchange(2, send_s, recv_s)
+    move.start()
+
+    def down_own(cols):
+        part = dot(act_ref[own, :], wb_s[:, cols], NN)
+        acc_s[:, cols] = part + normed_s[:, cols] + vec_ref[5:6, cols]
+
+    over_cols(width, down_own)
+    move.wait()
+
+    def norm_two(r, carry):
+        resid = acc_s[r, :] + recv_s[r, :]
+        centre = resid - row_stats(resid)
+        rstd = lax.rsqrt(row_stats(centre * centre) + EPS)
+        unit = centre * rstd
+        gain = vec_ref[6:7, :]
+        layer_ref[r, :] = (unit * gain + vec_ref[7:8, :]).astype(BF16)
+        grad = cot_ref[r, :]
+        scaled = grad * gain
+        back = rstd * (scaled - row_stats(scaled) - unit * row_stats(scaled * unit))
+        acc_s[r, :] = back
+        g2_ref[r, :] = back.astype(BF16)
+        sums = (back, grad * unit, grad)
+        return tuple(c + jnp.sum(s, axis=0, keepdims=True) for c, s in zip(carry, sums))
+
+    shift_two = over_rows(norm_two)
+    move = exchange(3, g2_ref.at[own], g2_ref.at[other])
+    move.start()
+    for i, total in enumerate(shift_two):
+        sums_ref[3 + i : 4 + i, :] = total
+
+    def back_act(where, first):
+        def body(cols):
+            grad = dot(g2_ref[where, :], wb_s[cols, :], NT) * slope_s[where, cols]
+            gp_ref[where, cols] = grad.astype(BF16)
+            total = jnp.sum(grad, axis=0, keepdims=True)
+            bias_sum_ref[0:1, cols] = total if first else bias_sum_ref[0:1, cols] + total
+
+        over_cols(ff_half, body)
+
+    back_act(own, True)
+    move.wait()
+    back_act(other, False)
+
+    def back_other(cols):
+        send_s[:, cols] = dot(gp_ref[other, :], wi_s[cols, :], NT)
+
+    over_cols(width, back_other)
+    move = exchange(4, send_s, recv_s)
+    move.start()
+
+    def back_own(cols):
+        acc_s[:, cols] += dot(gp_ref[own, :], wi_s[cols, :], NT)
+
+    over_cols(width, back_own)
+    move.wait()
+
+    def back_one(r, carry):
+        grad = acc_s[r, :] + recv_s[r, :]
+        unit = unit_s[r, :]
+        rstd = rstd_s[r, 0:1]
+        scaled = grad * vec_ref[3:4, :]
+        back = rstd * (scaled - row_stats(scaled) - unit * row_stats(scaled * unit))
+        grad_one_ref[r, :] = back
+        g1_ref[r, :] = back.astype(BF16)
+        sums = (back, grad * unit, grad)
+        return tuple(c + jnp.sum(s, axis=0, keepdims=True) for c, s in zip(carry, sums))
+
+    shift_one = over_rows(back_one)
+    move = exchange(5, g1_ref.at[own], g1_ref.at[other])
+    move.start()
+    for i, total in enumerate(shift_one):
+        sums_ref[i : 1 + i, :] = total
+    sums_ref[6:8, :] = jnp.zeros((2, width), F32)
+
+    for where in (own, other):
+        if where is other:
+            move.wait()
+        for m in range(n_z):
+            at = pl.ds(pl.multiple_of((zed ^ m) * wide, wide), wide)
+            ga_refs[m][where, :] = dot(g1_ref[where, :], wo_s[at, :], NT).astype(BF16)
+
+
+def middle(att, x_own, cot, vectors, bias_half, wo, wi, wb, n_f, n_z):
+    rows, width = x_own.shape
+    wide = att[0].shape[1]
+    ff_half = bias_half.shape[0]
+    half_in = n_z * wide
+    sds = jax.ShapeDtypeStruct
+    out_shape = [
+        sds((rows, width), BF16),
+        sds((rows, width), F32),
+        sds((2 * rows, half_in), BF16),
+        sds((2 * rows, width), BF16),
+        sds((2 * rows, ff_half), BF16),
+        sds((2 * rows, width), BF16),
+        sds((2 * rows, ff_half), BF16),
+        sds((2 * rows, width), BF16),
+        sds((8, width), F32),
+        sds((1, ff_half), F32),
+    ] + [sds((2 * rows, wide), BF16)] * n_z
+    in_vmem, anywhere = pl.BlockSpec(memory_space=pltpu.VMEM), pl.BlockSpec(memory_space=pl.ANY)
+    cfg = {"step": 512, "rows": 64}
+    results = pl.pallas_call(
+        partial(mid_kernel, n_f=n_f, n_z=n_z, cfg=cfg),
+        out_shape=out_shape,
+        in_specs=[in_vmem] * (n_z + 4) + [anywhere] * (6 * n_f),
+        out_specs=[in_vmem] * len(out_shape),
+        scratch_shapes=[
+            pltpu.VMEM((half_in, width), BF16),
+            pltpu.VMEM((width, ff_half), BF16),
+            pltpu.VMEM((ff_half, width), BF16),
+            pltpu.VMEM((2 * rows, ff_half), F32),
+            pltpu.VMEM((rows, width), F32),
+            pltpu.VMEM((rows, width), F32),
+            pltpu.VMEM((rows, width), F32),
+            pltpu.VMEM((rows, width), F32),
+            pltpu.VMEM((rows, width), F32),
+            pltpu.VMEM((rows, 128), F32),
+            pltpu.SemaphoreType.DMA((3, 2 * n_f)),
+            pltpu.SemaphoreType.DMA((6,)),
+            pltpu.SemaphoreType.DMA((6,)),
+        ],
+        compiler_params=pltpu.CompilerParams(
+            vmem_limit_bytes=VMEM_MIDDLE, collective_id=0, has_side_effects=True
+        ),
+        cost_estimate=pl.CostEstimate(
+            flops=2 * 2 * rows * width * (2 * half_in + 4 * ff_half),
+            bytes_accessed=40 << 20, transcendentals=2 * rows * ff_half,
+        ),
+        name="middle",
+    )(*att, x_own, cot, vectors, bias_half[None], *wo, *wi, *wb)
+    return results[:10], results[10:]
 
 
 def on_device(x_in, w_qkv, w_out, w_in, w_back, vectors, bias_in, cot, *, n_ctx, n_f):
@@ -264,15 +514,18 @@
             for bit in order:
                 for m in list(held):
                     held[m ^ bit] = over_f(held[m], bit)
-            parts.append(place([held[m] for m in range(n_f)], fs, 1))
-        return jnp.concatenate(parts, axis=0)
+            parts += [held[m] for m in range(n_f)]
+        return parts
 
     def after(value, *others):
         return lax.optimization_barrier((value,) + others)[0]
 
     half_in = width // 2
     mine = lax.dynamic_slice_in_dim(w_qkv, core * half_in, half_in, 0)
-    all_cols = gather_cols(mine).reshape(half_in, 3, 2, width // 2)
+    pieces = gather_cols(mine)
+    all_cols = jnp.concatenate(
+        [place(pieces[:n_f], fs, 1), place(pieces[n_f:], fs, 1)], axis=0
+    ).reshape(half_in, 3, 2, width // 2)
     keep = lax.dynamic_index_in_dim(all_cols, core, 2, False)
     give = lax.dynamic_index_in_dim(all_cols, 1 - core, 2, False)
     got = swap(give)
@@ -284,11 +537,11 @@
     wo_mine = lax.dynamic_slice_in_dim(w_out, core * (width // 2), width // 2, 0)
     wo_half = gather_cols(after(wo_mine, got))
     wi_mine = lax.dynamic_slice_in_dim(w_in, core * ff_part, ff_part, 1)
-    wi_half = gather_cols(after(wi_mine, wo_half))
+    wi_half = gather_cols(after(wi_mine, wo_half[-1]))
     wb_mine = lax.dynamic_index_in_dim(
         w_back.reshape(n_f, 2, ff_part, w_back.shape[1]), core, 1, False
     ).reshape(n_f * ff_part, -1)
-    wb_half = gather_cols(after(wb_mine, wi_half))
+    wb_half = gather_cols(after(wb_mine, wi_half[-1]))
 
     x_two = pair(x_own)
     span = 3 * wide
@@ -305,34 +558,15 @@
         qkv.append(block if m == 0 else over_z(block, m))
     att, att_full, lse = attend(qkv, heads)
     att = [att[m] if m == 0 else over_z(att[m], m) for m in range(n_z)]
-    att_half = place(att, zed, 1)
-
-    resid_one = (
-        x_own.astype(F32) + pair_sum(dot(att_half, wo_half, NN)) + vectors[2]
-    )
-    normed, unit_one, rstd_one = norm_fwd(resid_one, vectors[3], vectors[4])
-    h_two = pair(normed.astype(BF16))
     bias_half = lax.dynamic_index_in_dim(
         bias_in.reshape(n_f, 2, ff_part), core, 1, False
     ).reshape(-1)
-    pre = dot(h_two, wi_half, NN) + bias_half
-    act, slope = gelu_both(pre)
-    act = act.astype(BF16)
-    resid_two = normed + pair_sum(dot(act, wb_half, NN)) + vectors[5]
-    result, unit_two, rstd_two = norm_fwd(resid_two, vectors[6], vectors[7])
-    layer_out = result.astype(BF16)[None]
-    grad_two, gain_two, shift_two = norm_back(grad_out, unit_two, rstd_two, vectors[6])
-    g_two = pair(grad_two.astype(BF16))
-    grad_pre = dot(g_two, wb_half, NT) * slope
-    grad_pre_low = grad_pre.astype(BF16)
-    grad_normed = grad_two + pair_sum(dot(grad_pre_low, wi_half, NT))
-    grad_one, gain_one, shift_one = norm_back(grad_normed, unit_one, rstd_one, vectors[3])
-    g_one = pair(grad_one.astype(BF16))
-    grad_att = dot(g_one, wo_half, NT).astype(BF16)
-    g_att = []
-    for m in range(n_z):
-        block = lax.dynamic_slice_in_dim(grad_att, (zed ^ m) * wide, wide, 1)
-        g_att.append(block if m == 0 else over_z(block, m))
+    outs, grad_att = middle(
+        att, x_own, grad_out, vectors, bias_half, wo_half, wi_half, wb_half, n_f, n_z
+    )
+    layer_out, grad_one, att_half, h_two, act, g_two, grad_pre_low, g_one, sums_mid, bias_sum = outs
+    layer_out = layer_out[None]
+    g_att = [grad_att[m] if m == 0 else over_z(grad_att[m], m) for m in range(n_z)]
 
     def reduce_rows(partial_grad):
         cols = partial_grad.shape[1]
@@ -404,24 +638,29 @@
 
     sums = jnp.sum(g_qkv.astype(F32), axis=0).reshape(n_z, 3, wide)
     ratio = hidden // width
-    early = jnp.stack(
-        [
-            jnp.sum(grad_one, axis=0),
-            gain_one,
-            shift_one,
-            jnp.sum(grad_two, axis=0),
-            gain_two,
-            shift_two,
-        ],
-        axis=1,
-    )
-    bias_terms = spread(jnp.sum(grad_pre, axis=0), n_f).reshape(width, ratio)
+    early = sums_mid[:6].T
+    bias_terms = spread(bias_sum[0], n_f).reshape(width, ratio)
     late = jnp.stack([spread(sums[:, 0], 1), spread(sums[:, 2], 1)], axis=1)
     table = jnp.concatenate([late, early, bias_terms], axis=1)
-    table = jnp.pad(table, ((0, 0), (0, 128 - table.shape[1])))
-    table = lax.psum_scatter(table, ("ctx", "fsdp"), scatter_dimension=0, tiled=True)
-    vector_grad = table[:, :8].T
-    in_bias_grad = table[:, 8 : 8 + ratio].reshape(-1)
+    kinds = table.shape[1]
+    low = width // (n_ctx * n_f)
+    now = table.reshape((n_z, 2) + (2,) * len(bits) + (low, kinds))
+    now = jnp.swapaxes(now, -1, -2).reshape((n_z, 2) + (2,) * len(bits) + (kinds * low,))
+    left = list(reversed(bits))
+    for bit in bits:
+        axis = 2 + left.index(bit)
+        left.remove(bit)
+        flag = (fs // bit) % 2
+        stay = lax.dynamic_index_in_dim(now, flag, axis, False)
+        now = stay + over_f(lax.dynamic_index_in_dim(now, 1 - flag, axis, False), bit)
+    total = lax.dynamic_index_in_dim(now, zed, 0, False)
+    for m in range(1, n_z):
+        total = total + over_z(lax.dynamic_index_in_dim(now, zed ^ m, 0, False), m)
+    stay = lax.dynamic_index_in_dim(total, core, 0, False)
+    table = stay + swap(lax.dynamic_index_in_dim(total, 1 - core, 0, False))
+    table = table.reshape(kinds, low)
+    vector_grad = table[:8]
+    in_bias_grad = table[8:].T.reshape(-1)
     return (
         layer_out,
         grad_in[None],

time: 795 us -> 611 us (0.77)
  waiting for transfers between devices: 363 us -> 252 us
  other arithmetic: 106 us -> 54.3 us
  matrix products: 82.8 us -> 32.4 us
  Pallas kernels: 82.2 us -> 129 us
  between operations: 15.7 us -> 2.03 us
    unnamed x2 -> x0, waiting for transfers between devices: 102 us -> none
    dot_general x15 -> x9, matrix products: 82.8 us -> 32.4 us  [dot(): return lax.dot_general(left, right, dims, preferred_element_type=F32)]
    pallas_call x0 -> x1, Pallas kernels: none -> 45.5 us  [middle(): pl.pallas_call(partial(mid_kernel, n_f=n_f, n_z=n_z, cfg=cfg), out_shape=...]
    concatenate x3 -> x1, other arithmetic: 52.7 us -> 20.6 us  [on_device(): jnp.concatenate([place(pieces[:n_f], fs, 1), place(pieces[n_f:], fs, 1)],...]
    ppermute x18 -> x21, waiting for transfers between devices: 157 us -> 133 us  [over_z(): return lax.ppermute(v, 'ctx', [(i, i ^ 2 * m) for i in range(n_ctx)])]
    ppermute x32 -> x34, waiting for transfers between devices: 94.7 us -> 117 us  [over_f(): return lax.ppermute(v, 'fsdp', [(i, i ^ m) for i in range(n_f)])]
    reduce_sum x9 -> x0, other arithmetic: 9.4 us -> none  [the longest x3 4.57 us: norm_back(): return (rstd * inner, jnp.sum(grad * unit, axis=0), jnp.sum(grad, axis=0))]
    ppermute x12 -> x7, waiting for transfers between devices: 10.1 us -> 2.1 us  [swap(): return lax.ppermute(v, 'ctx', [(i, i ^ 1) for i in range(n_ctx)])]
  transfers between devices with their start and end apart: 63 -> 62, of which waited for: 38 -> 28; matrix products, arithmetic and copies ran while one was open for 24% -> 16% of each run, Pallas kernels for 4% -> 5%
where the time goes in v2:
time: 611 us; the launch traced here: 601 us
  waiting for transfers between devices  252 us (41%)
  Pallas kernels  129 us (21%)
  starting transfers between devices  78.8 us (13%)
  other arithmetic  54.3 us (9%)
  local copies, waits for them, and re-layouts  53.3 us (9%)
  matrix products  32.4 us (5%)
    ppermute x21, waiting for transfers between devices, over_z(): return lax.ppermute(v, 'ctx', [(i, i ^ 2 * m) for i in range(n_ctx)])  133 us
    ppermute x34, waiting for transfers between devices, over_f(): return lax.ppermute(v, 'fsdp', [(i, i ^ m) for i in range(n_f)])  117 us
    pallas_call x1, Pallas kernels, attend_back(): pl.pallas_call(partial(attend_back_kernel, blocks=blocks, heads=heads, q_...  50.4 us
    pallas_call x1, Pallas kernels, middle(): pl.pallas_call(partial(mid_kernel, n_f=n_f, n_z=n_z, cfg=cfg), out_shape=...  45.5 us
    pallas_call x1, Pallas kernels, attend(): pl.pallas_call(partial(attend_kernel, blocks=blocks, heads=heads, q_rows=...  32.9 us
    dot_general x9, matrix products, dot(): return lax.dot_general(left, right, dims, preferred_element_type=F32)  32.4 us
    ppermute x34, starting transfers between devices, over_f(): return lax.ppermute(v, 'fsdp', [(i, i ^ m) for i in range(n_f)])  29.3 us
    ppermute x7, starting transfers between devices, swap(): return lax.ppermute(v, 'ctx', [(i, i ^ 1) for i in range(n_ctx)])  25 us
  transfers between devices with their start and end apart: 62, of which 28 were waited for; matrix products, arithmetic and copies ran while one was open for 16% of the time, Pallas kernels for 5%

profile of v2, /device:TPU:23, one launch (start us, length us, event | category | flops | bytes accessed | tf_op | source)
XLA Modules:
  0.0 601.4 jit_solution(5705133112597292826)
XLA Ops:
  4.2 8.1 %collective-permute-done.1 = bf16[256,768]{0,1:T(8,128)(2,1)} collective-permute-done((bf16[256,768]{0,1:T(8,128)(2,1)S(1)}, bf16[256,768]{0,1:T(8,128)(2,1)}, u32[]{:S(2)}, u32[]{:S(2)}) %collective-permute-start.1) | collective-permute-done | bytes 393248 | tf_op jit(solution)/shard_map/ppermute | solution.py:492
  14.0 6.9 %collective-permute-done.3 = bf16[256,768]{0,1:T(8,128)(2,1)} collective-permute-done((bf16[256,768]{0,1:T(8,128)(2,1)S(1)}, bf16[256,768]{0,1:T(8,128)(2,1)}, u32[]{:S(2)}, u32[]{:S(2)}) %collective-permute-start.3) | collective-permute-done | bytes 393248 | tf_op jit(solution)/shard_map/ppermute | solution.py:492
  20.9 8.4 %collective-permute-done.2 = bf16[256,768]{0,1:T(8,128)(2,1)} collective-permute-done((bf16[256,768]{0,1:T(8,128)(2,1)}, bf16[256,768]{0,1:T(8,128)(2,1)}, u32[]{:S(2)}, u32[]{:S(2)}) %collective-permute-start.2) | collective-permute-done | bytes 393248 | tf_op jit(solution)/shard_map/ppermute | solution.py:492
  32.0 20.6 %maximum_maximum_fusion = bf16[512,3072]{0,1:T(8,128)(2,1)S(1)} fusion(bf16[256,768]{0,1:T(8,128)(2,1)S(1)} %get-tuple-element.102, bf16[256,768]{0,1:T(8,128)(2,1)S(1)} %get-tuple-element.101, bf16[256,768]{0,1:T(8,128)(2,1)S(1)} %get-tuple-element.100, bf16[256,768]{0,1:T(8,128)(2,1)S(1)} %get-tuple-element.99, bf16[256,768]{0,1:T(8,128)(2,1)S(1)} %get-tuple-element.96, ...), kind=kLoop, calls=%fused_computation.10 | loop fusion | flops 25165824 | bytes 6291456 | tf_op jit(solution)/shard_map/concatenate | solution.py:526
  96.1 22.5 %collective-permute-done.10.refs_3_ = bf16[768,384]{1,0:T(8,128)(2,1)S(1)} collective-permute-done((bf16[768,384]{1,0:T(8,128)(2,1)S(1)}, bf16[768,384]{1,0:T(8,128)(2,1)S(1)}, u32[]{:S(2)}, u32[]{:S(2)}) %collective-permute-start.10) | collective-permute-done | bytes 589856 | tf_op jit(solution)/shard_map/ppermute | solution.py:489
  119.8 9.4 %collective-permute-done.9.refs_2_ = bf16[768,384]{1,0:T(8,128)(2,1)S(1)} collective-permute-done((bf16[768,384]{1,0:T(8,128)(2,1)S(1)}, bf16[768,384]{1,0:T(8,128)(2,1)S(1)}, u32[]{:S(2)}, u32[]{:S(2)}) %collective-permute-start.9) | collective-permute-done | bytes 589856 | tf_op jit(solution)/shard_map/ppermute | solution.py:489
  130.7 32.9 %attend.1 = (bf16[768,128]{1,0:T(8,128)(2,1)S(1)}, bf16[768,128]{1,0:T(8,128)(2,1)S(1)}, bf16[768,128]{1,0:T(8,128)(2,1)S(1)}, bf16[768,128]{1,0:T(8,128)(2,1)S(...) custom-call(bf16[768,384]{1,0:T(8,128)(2,1)S(1)} %fusion.15.refs_0_, bf16[768,384]{1,0:T(8,128)(2,1)S(1)} %collective-permute-done.8.refs_1_, ...), custom_call_target="tpu_custom_call" | custom-call | flops 19327352832 | bytes 3932160 | tf_op jit(solution)/shard_map/attend/pallas_call | solution.py:97
  175.9 8.8 %collective-permute-done.13.refs_3_ = bf16[768,128]{1,0:T(8,128)(2,1)S(1)} collective-permute-done((bf16[768,128]{1,0:T(8,128)(2,1)S(1)}, bf16[768,128]{1,0:T(8,128)(2,1)S(1)}, u32[]{:S(2)}, u32[]{:S(2)}) %collective-permute-start.13) | collective-permute-done | bytes 196640 | tf_op jit(solution)/shard_map/ppermute | solution.py:489
  192.4 10.1 %collective-permute-done.26.refs_25_ = bf16[1024,256]{1,0:T(8,128)(2,1)} collective-permute-done((bf16[1024,256]{1,0:T(8,128)(2,1)S(1)}, bf16[1024,256]{1,0:T(8,128)(2,1)}, u32[]{:S(2)}, u32[]{:S(2)}) %collective-permute-start.26) | collective-permute-done | bytes 524320 | tf_op jit(solution)/shard_map/ppermute | solution.py:492
  207.3 11.2 %collective-permute-done.27.refs_26_ = bf16[1024,256]{1,0:T(8,128)(2,1)} collective-permute-done((bf16[1024,256]{1,0:T(8,128)(2,1)S(1)}, bf16[1024,256]{1,0:T(8,128)(2,1)}, u32[]{:S(2)}, u32[]{:S(2)}) %collective-permute-start.27) | collective-permute-done | bytes 524320 | tf_op jit(solution)/shard_map/ppermute | solution.py:492
  218.5 11.2 %collective-permute-done.28.refs_27_ = bf16[1024,256]{1,0:T(8,128)(2,1)} collective-permute-done((bf16[1024,256]{1,0:T(8,128)(2,1)}, bf16[1024,256]{1,0:T(8,128)(2,1)}, u32[]{:S(2)}, u32[]{:S(2)}) %collective-permute-start.28) | collective-permute-done | bytes 524320 | tf_op jit(solution)/shard_map/ppermute | solution.py:492
  229.8 45.5 %middle.1 = (bf16[384,1024]{1,0:T(8,128)(2,1)}, f32[384,1024]{1,0:T(8,128)}, bf16[768,512]{1,0:T(8,128)(2,1)}, bf16[768,1024]{1,0:T(8,128)(2,1)}, bf16[768,2048]...) custom-call(bf16[768,128]{1,0:T(8,128)(2,1)} %copy-done.7, ...), custom_call_target="tpu_custom_call" | custom-call | flops 14495514624 | bytes 41943040 | tf_op jit(solution)/shard_map/middle/pallas_call | solution.py:441
  278.0 8.1 %convolution_convert_fusion.2 = bf16[1024,2048]{1,0:T(8,128)(2,1)} fusion(bf16[768,1024]{1,0:T(8,128)(2,1)} %get-tuple-element.57, bf16[768,2048]{1,0:T(8,128)(2,1)} %get-tuple-element.58), kind=kOutput, calls=%fused_computation.9 | convolution fusion | flops 3223322624 | bytes 8912896 | tf_op jit(solution)/shard_map/dot_general | solution.py:25
  286.1 5.0 convolution_convert_fusion.1
  291.1 7.9 %pad_maximum_fusion = bf16[1024,4096]{1,0:T(8,128)(2,1)} fusion(bf16[1024,2048]{1,0:T(8,128)(2,1)} %convolution_convert_fusion.1, bf16[1024,2048]{1,0:T(8,128)(2,1)} %convolution_convert_fusion.2), kind=kLoop, calls=%fused_computation | loop fusion | flops 16777216 | bytes 16777216 | tf_op jit(solution)/shard_map/concatenate | solution.py:603
  299.1 5.5 fusion.68
  306.3 50.4 %attend_back.1 = (bf16[768,384]{1,0:T(8,128)(2,1)S(1)}, bf16[768,384]{1,0:T(8,128)(2,1)S(1)}, bf16[768,384]{1,0:T(8,128)(2,1)S(1)}, bf16[768,384]{1,0:T(8,128)(2,1)S(1)}) custom-call(bf16[768,384]{1,0:T(8,128)(2,1)S(1)} %copy-done.6, bf16[768,384]{1,0:T(8,128)(2,1)} %copy-done.4, bf16[768,384]{1,0:T(8,128)(2,1)} %copy-done.3, bf16[768,384]{1,0:T(8,128)(2,1)} %copy-done.2, ...), custom_call_target="tpu_custom_call" | custom-call | flops 48318382080 | bytes 7864320 | tf_op jit(solution)/shard_map/attend_back/pallas_call | solution.py:180
  369.7 26.1 %collective-permute-done.35 = bf16[768,384]{1,0:T(8,128)(2,1)} collective-permute-done((bf16[768,384]{1,0:T(8,128)(2,1)S(1)}, bf16[768,384]{1,0:T(8,128)(2,1)}, u32[]{:S(2)}, u32[]{:S(2)}) %collective-permute-start.35) | collective-permute-done | bytes 589856 | tf_op jit(solution)/shard_map/ppermute | solution.py:489
  395.8 10.5 %collective-permute-done.36 = bf16[768,384]{1,0:T(8,128)(2,1)} collective-permute-done((bf16[768,384]{1,0:T(8,128)(2,1)S(1)}, bf16[768,384]{1,0:T(8,128)(2,1)}, u32[]{:S(2)}, u32[]{:S(2)}) %collective-permute-start.36) | collective-permute-done | bytes 589856 | tf_op jit(solution)/shard_map/ppermute | solution.py:489
  414.0 5.0 convolution_convert_fusion
  447.4 48.2 %collective-permute-done.40 = bf16[4,2,32,2048]{3,2,0,1:T(8,128)(2,1)S(1)} collective-permute-done((bf16[4,2,32,2048]{3,2,0,1:T(8,128)(2,1)}, bf16[4,2,32,2048]{3,2,0,1:T(8,128)(2,1)S(1)}, u32[]{:S(2)}, u32[]{:S(2)}) %collective-permute-start.40) | collective-permute-done | bytes 1048608 | tf_op jit(solution)/shard_map/ppermute | solution.py:492
  523.3 15.0 %collective-permute-start.47 = (bf16[32,2048]{1,0:T(8,128)(2,1)S(1)}, bf16[32,2048]{1,0:T(8,128)(2,1)S(1)}, u32[]{:S(2)}, u32[]{:S(2)}) collective-permute-start(bf16[32,2048]{1,0:T(8,128)(2,1)S(1)} %fusion.51), channel_id=1, source_target_pairs={{0,4},{4,0},{8,12},{12,8},{16,20},{20,16},{24,28},{28,24},{1,5},{5... | collective-permute-start | bytes 393224 | tf_op jit(solution)/shard_map/ppermute | solution.py:486
  546.5 16.9 %collective-permute-done.52 = bf16[2,32,4096]{2,1,0:T(8,128)(2,1)S(1)} collective-permute-done((bf16[2,32,4096]{2,1,0:T(8,128)(2,1)}, bf16[2,32,4096]{2,1,0:T(8,128)(2,1)S(1)}, u32[]{:S(2)}, u32[]{:S(2)}) %collective-permute-start.52) | collective-permute-done | bytes 524320 | tf_op jit(solution)/shard_map/ppermute | solution.py:489
  566.5 23.5 %collective-permute-done.54 = bf16[2,32,4096]{2,1,0:T(8,128)(2,1)} collective-permute-done((bf16[2,32,4096]{2,1,0:T(8,128)(2,1)}, bf16[2,32,4096]{2,1,0:T(8,128)(2,1)}, u32[]{:S(2)}, u32[]{:S(2)}) %collective-permute-start.54) | collective-permute-done | bytes 524320 | tf_op jit(solution)/shard_map/ppermute | solution.py:489
  (336 shorter events, 181.5 us)
Async XLA Ops:
  78.9 39.7 %collective-permute-start.10 = (bf16[768,384]{1,0:T(8,128)(2,1)S(1)}, bf16[768,384]{1,0:T(8,128)(2,1)S(1)}, u32[]{:S(2)}, u32[]{:S(2)}) collective-permute-start(bf16[768,384]{1,0:T(8,128)(2,1)S(1)} %fusion.18), channel_id=1, source_target_pairs={{0,24},{4,28},{8,16},{12,20},{16,8},{20,12},{24,0},{28,4},{1,25},{... | collective-permute-start | bytes 1769480 | tf_op jit(solution)/shard_map/ppermute | solution.py:489
  82.8 46.4 %collective-permute-start.9 = (bf16[768,384]{1,0:T(8,128)(2,1)S(1)}, bf16[768,384]{1,0:T(8,128)(2,1)S(1)}, u32[]{:S(2)}, u32[]{:S(2)}) collective-permute-start(bf16[768,384]{1,0:T(8,128)(2,1)S(1)} %fusion.17), channel_id=1, source_target_pairs={{0,16},{4,20},{8,24},{12,28},{16,0},{20,4},{24,8},{28,12},{1,17},{... | collective-permute-start | bytes 1769480 | tf_op jit(solution)/shard_map/ppermute | solution.py:489
  88.8 42.0 %collective-permute-start.8 = (bf16[768,384]{1,0:T(8,128)(2,1)S(1)}, bf16[768,384]{1,0:T(8,128)(2,1)S(1)}, u32[]{:S(2)}, u32[]{:S(2)}) collective-permute-start(bf16[768,384]{1,0:T(8,128)(2,1)S(1)} %fusion.16), channel_id=1, source_target_pairs={{0,8},{4,12},{8,0},{12,4},{16,24},{20,28},{24,16},{28,20},{1,9},{5... | collective-permute-start | bytes 1769480 | tf_op jit(solution)/shard_map/ppermute | solution.py:489
  90.3 40.1 %collective-permute-start.24 = (bf16[512,512]{1,0:T(8,128)(2,1)S(1)}, bf16[512,512]{1,0:T(8,128)(2,1)S(1)}, u32[]{:S(2)}, u32[]{:S(2)}) collective-permute-start(bf16[512,512]{1,0:T(8,128)(2,1)S(1)} %get-tuple-element.112.refs_20_), channel_id=1, source_target_pairs={{0,2},{1,3},{2,0},{3,1},{4,6},{5,7},{6,4},{7,5},{8,10},{9,11},{10,... | collective-permute-start | bytes 1572872 | tf_op jit(solution)/shard_map/ppermute | solution.py:492
  94.9 72.0 %collective-permute-start.15 = (bf16[256,256]{1,0:T(8,128)(2,1)S(1)}, bf16[256,256]{1,0:T(8,128)(2,1)S(1)}, u32[]{:S(2)}, u32[]{:S(2)}) collective-permute-start(bf16[256,256]{1,0:T(8,128)(2,1)S(1)} %get-tuple-element.121.refs_8_), channel_id=1, source_target_pairs={{0,2},{1,3},{2,0},{3,1},{4,6},{5,7},{6,4},{7,5},{8,10},{9,11},{10,... | collective-permute-start | bytes 393224 | tf_op jit(solution)/shard_map/ppermute | solution.py:492
  118.6 50.3 %collective-permute-start.17 = (bf16[256,256]{1,0:T(8,128)(2,1)S(1)}, bf16[256,256]{1,0:T(8,128)(2,1)S(1)}, u32[]{:S(2)}, u32[]{:S(2)}) collective-permute-start(bf16[256,256]{1,0:T(8,128)(2,1)S(1)} %get-tuple-element.120.refs_12_), channel_id=1, source_target_pairs={{0,1},{1,0},{2,3},{3,2},{4,5},{5,4},{6,7},{7,6},{8,9},{9,8},{10,11... | collective-permute-start | bytes 393224 | tf_op jit(solution)/shard_map/ppermute | solution.py:492
  129.2 41.0 %collective-permute-start.16 = (bf16[256,256]{1,0:T(8,128)(2,1)S(1)}, bf16[256,256]{1,0:T(8,128)(2,1)}, u32[]{:S(2)}, u32[]{:S(2)}) collective-permute-start(bf16[256,256]{1,0:T(8,128)(2,1)S(1)} %collective-permute-done.14.refs_9_), channel_id=1, source_target_pairs={{0,2},{1,3},{2,0},{3,1},{4,6},{5,7},{6,4},{7,5},{8,10},{9,11},{10,... | collective-permute-start | bytes 393224 | tf_op jit(solution)/shard_map/ppermute | solution.py:492
  130.5 36.4 %collective-permute-start.25 = (bf16[512,512]{1,0:T(8,128)(2,1)S(1)}, bf16[512,512]{1,0:T(8,128)(2,1)S(1)}, u32[]{:S(2)}, u32[]{:S(2)}) collective-permute-start(bf16[512,512]{1,0:T(8,128)(2,1)S(1)} %collective-permute-done.24.refs_22_), channel_id=1, source_target_pairs={{0,1},{1,0},{2,3},{3,2},{4,5},{5,4},{6,7},{7,6},{8,9},{9,8},{10,11... | collective-permute-start | bytes 1572872 | tf_op jit(solution)/shard_map/ppermute | solution.py:492
  186.1 32.4 %collective-permute-start.27 = (bf16[1024,256]{1,0:T(8,128)(2,1)S(1)}, bf16[1024,256]{1,0:T(8,128)(2,1)}, u32[]{:S(2)}, u32[]{:S(2)}) collective-permute-start(bf16[1024,256]{1,0:T(8,128)(2,1)S(1)} %get-tuple-element.111.refs_24_), channel_id=1, source_target_pairs={{0,2},{1,3},{2,0},{3,1},{4,6},{5,7},{6,4},{7,5},{8,10},{9,11},{10,... | collective-permute-start | bytes 1572872 | tf_op jit(solution)/shard_map/ppermute | solution.py:492
  275.3 30.9 %collective-permute-start.32 = (bf16[768,128]{1,0:T(8,128)(2,1)}, bf16[768,128]{1,0:T(8,128)(2,1)S(1)}, u32[]{:S(2)}, u32[]{:S(2)}) collective-permute-start(bf16[768,128]{1,0:T(8,128)(2,1)} %get-tuple-element.46), channel_id=1, source_target_pairs={{0,8},{4,12},{8,0},{12,4},{16,24},{20,28},{24,16},{28,20},{1,9},{5... | collective-permute-start | bytes 589832 | tf_op jit(solution)/shard_map/ppermute | solution.py:489
  275.4 30.8 %collective-permute-start.33 = (bf16[768,128]{1,0:T(8,128)(2,1)}, bf16[768,128]{1,0:T(8,128)(2,1)S(1)}, u32[]{:S(2)}, u32[]{:S(2)}) collective-permute-start(bf16[768,128]{1,0:T(8,128)(2,1)} %get-tuple-element.47), channel_id=1, source_target_pairs={{0,16},{4,20},{8,24},{12,28},{16,0},{20,4},{24,8},{28,12},{1,17},{... | collective-permute-start | bytes 589832 | tf_op jit(solution)/shard_map/ppermute | solution.py:489
  276.4 29.9 %collective-permute-start.34 = (bf16[768,128]{1,0:T(8,128)(2,1)}, bf16[768,128]{1,0:T(8,128)(2,1)S(1)}, u32[]{:S(2)}, u32[]{:S(2)}) collective-permute-start(bf16[768,128]{1,0:T(8,128)(2,1)} %get-tuple-element.48), channel_id=1, source_target_pairs={{0,24},{4,28},{8,16},{12,20},{16,8},{20,12},{24,0},{28,4},{1,25},{... | collective-permute-start | bytes 589832 | tf_op jit(solution)/shard_map/ppermute | solution.py:489
  356.7 39.1 %collective-permute-start.35 = (bf16[768,384]{1,0:T(8,128)(2,1)S(1)}, bf16[768,384]{1,0:T(8,128)(2,1)}, u32[]{:S(2)}, u32[]{:S(2)}) collective-permute-start(bf16[768,384]{1,0:T(8,128)(2,1)S(1)} %get-tuple-element.51), channel_id=1, source_target_pairs={{0,24},{4,28},{8,16},{12,20},{16,8},{20,12},{24,0},{28,4},{1,25},{... | collective-permute-start | bytes 1769480 | tf_op jit(solution)/shard_map/ppermute | solution.py:489
  356.8 49.5 %collective-permute-start.36 = (bf16[768,384]{1,0:T(8,128)(2,1)S(1)}, bf16[768,384]{1,0:T(8,128)(2,1)}, u32[]{:S(2)}, u32[]{:S(2)}) collective-permute-start(bf16[768,384]{1,0:T(8,128)(2,1)S(1)} %get-tuple-element.52), channel_id=1, source_target_pairs={{0,16},{4,20},{8,24},{12,28},{16,0},{20,4},{24,8},{28,12},{1,17},{... | collective-permute-start | bytes 1769480 | tf_op jit(solution)/shard_map/ppermute | solution.py:489
  359.9 46.5 %collective-permute-start.37 = (bf16[768,384]{1,0:T(8,128)(2,1)S(1)}, bf16[768,384]{1,0:T(8,128)(2,1)}, u32[]{:S(2)}, u32[]{:S(2)}) collective-permute-start(bf16[768,384]{1,0:T(8,128)(2,1)S(1)} %get-tuple-element.53), channel_id=1, source_target_pairs={{0,8},{4,12},{8,0},{12,4},{16,24},{20,28},{24,16},{28,20},{1,9},{5... | collective-permute-start | bytes 1769480 | tf_op jit(solution)/shard_map/ppermute | solution.py:489
  360.9 135.8 %collective-permute-start.50 = (bf16[4,2,32,4096]{3,2,1,0:T(8,128)(2,1)}, bf16[4,2,32,4096]{3,2,1,0:T(8,128)(2,1)}, u32[]{:S(2)}, u32[]{:S(2)}) collective-permute-start(bf16[4,2,32,4096]{3,2,1,0:T(8,128)(2,1)} %dynamic-slice_bitcast_fusion), channel_id=1, source_target_pairs={{0,2},{1,3},{2,0},{3,1},{4,6},{5,7},{6,4},{7,5},{8,10},{9,11},{10,... | collective-permute-start | bytes 6291464 | tf_op jit(solution)/shard_map/ppermute | solution.py:492
  367.8 42.6 %collective-permute-start.39 = (bf16[768,512]{1,0:T(8,128)(2,1)}, bf16[768,512]{1,0:T(8,128)(2,1)}, u32[]{:S(2)}, u32[]{:S(2)}) collective-permute-start(bf16[768,512]{1,0:T(8,128)(2,1)} %get-tuple-element.55), channel_id=1, source_target_pairs={{0,4},{4,0},{8,12},{12,8},{16,20},{20,16},{24,28},{28,24},{1,5},{5... | collective-permute-start | bytes 2359304 | tf_op jit(solution)/shard_map/ppermute | solution.py:486
  429.9 70.3 %collective-permute-start.48 = (bf16[4,2,32,4096]{3,2,0,1:T(8,128)(2,1)}, bf16[4,2,32,4096]{3,2,0,1:T(8,128)(2,1)}, u32[]{:S(2)}, u32[]{:S(2)}) collective-permute-start(bf16[4,2,32,4096]{3,2,0,1:T(8,128)(2,1)} %bitcast.167), channel_id=1, source_target_pairs={{0,1},{1,0},{2,3},{3,2},{4,5},{5,4},{6,7},{7,6},{8,9},{9,8},{10,11... | collective-permute-start | bytes 6291464 | tf_op jit(solution)/shard_map/ppermute | solution.py:492
  430.3 65.4 %collective-permute-start.40 = (bf16[4,2,32,2048]{3,2,0,1:T(8,128)(2,1)}, bf16[4,2,32,2048]{3,2,0,1:T(8,128)(2,1)S(1)}, u32[]{:S(2)}, u32[]{:S(2)}) collective-permute-start(bf16[4,2,32,2048]{3,2,0,1:T(8,128)(2,1)} %bitcast.169), channel_id=1, source_target_pairs={{0,1},{1,0},{2,3},{3,2},{4,5},{5,4},{6,7},{7,6},{8,9},{9,8},{10,11... | collective-permute-start | bytes 3145736 | tf_op jit(solution)/shard_map/ppermute | solution.py:492
  441.7 67.9 %collective-permute-start.38 = (f32[384,1024]{1,0:T(8,128)}, f32[384,1024]{1,0:T(8,128)}, u32[]{:S(2)}, u32[]{:S(2)}) collective-permute-start(f32[384,1024]{1,0:T(8,128)} %slice.149), channel_id=1, source_target_pairs={{0,4},{4,0},{8,12},{12,8},{16,20},{20,16},{24,28},{28,24},{1,5},{5... | collective-permute-start | bytes 4718600 | tf_op jit(solution)/shard_map/ppermute | solution.py:486
  446.4 60.4 %collective-permute-start.43 = (bf16[4,32,2048]{2,1,0:T(8,128)(2,1)S(1)}, bf16[4,32,2048]{2,1,0:T(8,128)(2,1)S(1)}, u32[]{:S(2)}, u32[]{:S(2)}) collective-permute-start(bf16[4,32,2048]{2,1,0:T(8,128)(2,1)S(1)} %dynamic-slice_bitcast_fusion.4), channel_id=1, source_target_pairs={{0,1},{1,0},{2,3},{3,2},{4,5},{5,4},{6,7},{7,6},{8,9},{9,8},{10,11... | collective-permute-start | bytes 1572872 | tf_op jit(solution)/shard_map/ppermute | solution.py:492
  499.2 40.9 %collective-permute-start.51 = (bf16[4,32,4096]{2,1,0:T(8,128)(2,1)S(1)}, bf16[4,32,4096]{2,1,0:T(8,128)(2,1)S(1)}, u32[]{:S(2)}, u32[]{:S(2)}) collective-permute-start(bf16[4,32,4096]{2,1,0:T(8,128)(2,1)S(1)} %dynamic-slice_bitcast_fusion.1), channel_id=1, source_target_pairs={{0,1},{1,0},{2,3},{3,2},{4,5},{5,4},{6,7},{7,6},{8,9},{9,8},{10,11... | collective-permute-start | bytes 3145736 | tf_op jit(solution)/shard_map/ppermute | solution.py:492
  503.1 37.2 %collective-permute-start.49 = (bf16[4,32,4096]{2,1,0:T(8,128)(2,1)S(1)}, bf16[4,32,4096]{2,1,0:T(8,128)(2,1)S(1)}, u32[]{:S(2)}, u32[]{:S(2)}) collective-permute-start(bf16[4,32,4096]{2,1,0:T(8,128)(2,1)S(1)} %dynamic-slice_bitcast_fusion.2), channel_id=1, source_target_pairs={{0,2},{1,3},{2,0},{3,1},{4,6},{5,7},{6,4},{7,5},{8,10},{9,11},{10,... | collective-permute-start | bytes 3145736 | tf_op jit(solution)/shard_map/ppermute | solution.py:492
  543.2 46.7 %collective-permute-start.54 = (bf16[2,32,4096]{2,1,0:T(8,128)(2,1)}, bf16[2,32,4096]{2,1,0:T(8,128)(2,1)}, u32[]{:S(2)}, u32[]{:S(2)}) collective-permute-start(bf16[2,32,4096]{2,1,0:T(8,128)(2,1)} %get-tuple-element.86), channel_id=1, source_target_pairs={{0,24},{4,28},{8,16},{12,20},{16,8},{20,12},{24,0},{28,4},{1,25},{... | collective-permute-start | bytes 1572872 | tf_op jit(solution)/shard_map/ppermute | solution.py:489
  (91 other events, 2024.0 us)

commit v3 on v2

--- a/solution.py
+++ b/solution.py
@@ -25,6 +25,297 @@
     return lax.dot_general(left, right, dims, preferred_element_type=F32)
 
 
+def front_kernel(x_ref, wq_ref, wo_ref, wi_ref, bias_ref, qkv_ref, xf_out, wl_out, wo_out, wi_out, *scratch, n_z, n_f, heads):
+    xf, wfull, wloc = scratch[:3]
+    own_sem, x_send, x_recv, xs_send, xs_recv, w_send, w_recv, ws_send, ws_recv, o_send, o_recv, i_send, i_recv, out_sem = scratch[3:]
+    ctx, fs = lax.axis_index("ctx"), lax.axis_index("fsdp")
+    core, zed = ctx % 2, ctx // 2
+    bits = [1 << b for b in range(n_f.bit_length() - 1)]
+    orders = (bits, bits[1:] + bits[:1])
+    rows, width = x_ref.shape
+    half = width // 2
+    quarter = half // 2
+    wide = heads * HEAD
+    partner = {"ctx": zed * 2 + (1 - core)}
+
+    barrier = pltpu.get_barrier_semaphore()
+
+    def greet(device):
+        pl.semaphore_signal(barrier, inc=1, device_id=device, device_id_type=MESH)
+
+    greet(partner)
+    for bit in bits:
+        greet({"fsdp": fs ^ bit})
+
+    @pl.when(zed > 0)
+    def _():
+        greet({"ctx": ctx - 2})
+
+    @pl.when(zed < n_z - 1)
+    def _():
+        greet({"ctx": ctx + 2})
+
+    edges = (zed == 0).astype(jnp.int32) + (zed == n_z - 1).astype(jnp.int32)
+    pl.semaphore_wait(barrier, 3 + len(bits) - edges)
+
+    def remote(src, dst, send, recv, device):
+        return pltpu.make_async_remote_copy(
+            src_ref=src, dst_ref=dst, send_sem=send, recv_sem=recv, device_id=device, device_id_type=MESH
+        )
+
+    def x_move(away, step, first):
+        block = zed - step * away
+        src = x_ref if first else xf.at[block ^ zed, 0]
+        index = (step + 1) // 2
+        return remote(
+            src, xf.at[block ^ (zed + step), 0], x_send.at[index, away], x_recv.at[block ^ (zed + step)],
+            {"ctx": ctx + 2 * step},
+        )
+
+    def x_swap(m, first=False):
+        src = x_ref if first else xf.at[m, 0]
+        return remote(src, xf.at[m, 1], xs_send.at[m], xs_recv.at[m], partner)
+
+    def has(step):
+        return zed < n_z - 1 if step == 1 else zed > 0
+
+    def came(away, step):
+        return zed - away >= 0 if step == 1 else zed + away <= n_z - 1
+
+    for step in (1, -1):
+
+        @pl.when(has(step))
+        def _(step=step):
+            x_move(0, step, True).start()
+
+    x_swap(0, True).start()
+    own_x = pltpu.make_async_copy(x_ref, xf.at[0, 0], own_sem.at[0])
+    own_x.start()
+
+    def x_step(away):
+        for step in (1, -1):
+
+            @pl.when(came(away, step))
+            def _(step=step):
+                block = zed - step * away
+                remote(
+                    xf.at[block ^ zed, 0], xf.at[block ^ zed, 0], x_send.at[0, 0], x_recv.at[block ^ zed], partner
+                ).wait_recv()
+
+                @pl.when(has(step))
+                def _():
+                    x_move(away, step, False).start()
+
+                x_swap(block ^ zed).start()
+
+    def wq_place(side, origin, which):
+        cols = wq_ref.shape[1]
+        return wfull.at[
+            pl.ds(pl.multiple_of(which * half + side * quarter, quarter), quarter),
+            pl.ds(pl.multiple_of(origin * cols, 128), cols),
+        ]
+
+    def wq_own(side):
+        return wq_ref.at[pl.ds(pl.multiple_of(core * half + side * quarter, quarter), quarter), :]
+
+    def wo_place(side, origin):
+        cols = wo_ref.shape[1]
+        return wo_out.at[pl.ds(side * quarter, quarter), pl.ds(pl.multiple_of(origin * cols, 128), cols)]
+
+    def wo_own(side):
+        return wo_ref.at[pl.ds(pl.multiple_of(core * half + side * quarter, quarter), quarter), :]
+
+    def wq_hop(side, m, bit):
+        src = wq_own(side) if m == 0 else wq_place(side, fs ^ m, core)
+        return remote(src, wq_place(side, fs ^ m, core), w_send.at[side, m ^ bit], w_recv.at[side, m ^ bit], {"fsdp": fs ^ bit})
+
+    def wo_hop(side, m, bit):
+        src = wo_own(side) if m == 0 else wo_place(side, fs ^ m)
+        return remote(src, wo_place(side, fs ^ m), o_send.at[side, m ^ bit], o_recv.at[side, m ^ bit], {"fsdp": fs ^ bit})
+
+    def wq_swap(side, m):
+        src = wq_own(side) if m == 0 else wq_place(side, fs ^ m, core)
+        return remote(src, wq_place(side, fs ^ m, core), ws_send.at[side, m], ws_recv.at[side, m], partner)
+
+    own_w = []
+    for side in range(2):
+        wq_hop(side, 0, orders[side][0]).start()
+        wq_swap(side, 0).start()
+        own_w.append(pltpu.make_async_copy(wq_own(side), wq_place(side, fs, core), own_sem.at[1 + side]))
+        own_w.append(pltpu.make_async_copy(wo_own(side), wo_place(side, fs), own_sem.at[3 + side]))
+    for copy in own_w:
+        copy.start()
+
+    part = wi_ref.shape[1] // 2
+
+    def wi_hop(side):
+        src = wi_ref.at[pl.ds(side * half, half), pl.ds(pl.multiple_of(core * part, 128), part)]
+        return remote(src, wi_out.at[side], i_send.at[side], i_recv.at[side], {"fsdp": fs ^ orders[side][0]})
+
+    def doubling(hop, level, after=None):
+        for side in range(2):
+            known = [0]
+            for bit in orders[side][:level]:
+                known = known + [m ^ bit for m in known]
+            bit = orders[side][level]
+            for m in known:
+                hop(side, m, bit).wait_recv()
+                if after is not None:
+                    after(side, m ^ bit).start()
+            if level + 1 < len(bits):
+                for m in known + [m ^ bit for m in known]:
+                    hop(side, m, orders[side][level + 1]).start()
+
+    doubling(wq_hop, 0, wq_swap)
+    for side in range(2):
+        wo_hop(side, 0, orders[side][0]).start()
+    x_step(1)
+    for level in range(1, len(bits)):
+        doubling(wq_hop, level, wq_swap)
+    for side in range(2):
+        wi_hop(side).start()
+    doubling(wo_hop, 0)
+    for away in range(2, n_z - 1):
+        x_step(away)
+    for copy in own_w:
+        copy.wait()
+    for side in range(2):
+        for m in range(n_f):
+            wq_swap_in = remote(
+                wq_place(side, fs ^ m, 1 - core), wq_place(side, fs ^ m, 1 - core),
+                ws_send.at[side, m], ws_recv.at[side, m], partner,
+            )
+            wq_swap_in.wait_recv()
+    outs = []
+    for j in range(3):
+        cols = pl.ds(pl.multiple_of(j * width + core * half, 128), half)
+        outs.append(pltpu.make_async_copy(wfull.at[:, cols], wl_out.at[:, pl.ds(j * half, half)], out_sem.at[j]))
+    for copy in outs:
+        copy.start()
+    for j in range(3):
+        base = j * width + core * half + zed * wide
+        if wide % 128 == 0:
+            piece = wfull[:, pl.ds(pl.multiple_of(base, 128), wide)]
+        else:
+            block = wfull[:, pl.ds(pl.multiple_of(base // 128 * 128, 128), 128)].astype(F32)
+            piece = jnp.where(zed % 2 == 1, block[:, wide:], block[:, :wide]).astype(BF16)
+        wloc[:, j * wide : (j + 1) * wide] = piece
+
+    def x_ready(m, side):
+        remote(xf.at[m, side], xf.at[m, side], xs_send.at[m], xs_recv.at[m], partner).wait_recv()
+
+    def project(m):
+        def run(side, carry):
+            result = dot(xf[m, side], wloc[...], NN) + bias_ref[...]
+            where = pl.ds(pl.multiple_of(side * rows, rows), rows)
+            qkv_ref[m, where, :] = result.astype(BF16)
+            return carry
+
+        lax.fori_loop(0, 2, run, 0)
+
+    own_x.wait()
+    x_ready(0, 1)
+    project(0)
+
+    def finish(away):
+        def run(i, carry):
+            block = zed - (1 - 2 * i) * away
+
+            @pl.when((block >= 0) & (block <= n_z - 1))
+            def _():
+                x_ready(block ^ zed, 1)
+                project(block ^ zed)
+
+            return carry
+
+        lax.fori_loop(0, 2, run, 0)
+
+    for away in range(1, n_z - 1):
+        finish(away)
+    for level in range(1, len(bits)):
+        doubling(wo_hop, level)
+    if n_z > 2:
+        x_step(n_z - 1)
+    finish(n_z - 1)
+    x_out = pltpu.make_async_copy(xf, xf_out, own_sem.at[5])
+    x_out.start()
+
+    for step in (1, -1):
+
+        @pl.when(has(step))
+        def _(step=step):
+            x_move(0, step, True).wait_send()
+            for away in range(1, n_z):
+
+                @pl.when(came(away, step))
+                def _(away=away):
+                    x_move(away, step, False).wait_send()
+
+    x_swap(0, True).wait_send()
+    for m in range(1, n_z):
+        x_swap(m).wait_send()
+    for side in range(2):
+        known = [0]
+        for bit in orders[side]:
+            for m in known:
+                wq_hop(side, m, bit).wait_send()
+                wo_hop(side, m, bit).wait_send()
+            known = known + [m ^ bit for m in known]
+        for m in range(n_f):
+            wq_swap(side, m).wait_send()
+        wi_hop(side).wait()
+    for copy in outs:
+        copy.wait()
+    x_out.wait()
+
+
+def front(x_own, w_qkv, w_out, w_in, bias, n_f, n_z, heads):
+    rows, width = x_own.shape
+    wide = heads * HEAD
+    sds = jax.ShapeDtypeStruct
+    in_vmem, anywhere = pl.BlockSpec(memory_space=pltpu.VMEM), pl.BlockSpec(memory_space=pl.ANY)
+    part = w_in.shape[1] // 2
+    dma = pltpu.SemaphoreType.DMA
+    return pl.pallas_call(
+        partial(front_kernel, n_z=n_z, n_f=n_f, heads=heads),
+        out_shape=[
+            sds((n_z, 2 * rows, 3 * wide), BF16),
+            sds((n_z, 2, rows, width), BF16),
+            sds((width, 3 * width // 2), BF16),
+            sds((width // 2, width), BF16),
+            sds((2, width // 2, part), BF16),
+        ],
+        in_specs=[anywhere] * 4 + [in_vmem],
+        out_specs=[in_vmem] + [anywhere] * 4,
+        scratch_shapes=[
+            pltpu.VMEM((n_z, 2, rows, width), BF16),
+            pltpu.VMEM((width, 3 * width), BF16),
+            pltpu.VMEM((width, 3 * wide), BF16),
+            dma((6,)),
+            dma((2, n_z)),
+            dma((n_z,)),
+            dma((n_z,)),
+            dma((n_z,)),
+            dma((2, n_f)),
+            dma((2, n_f)),
+            dma((2, n_f)),
+            dma((2, n_f)),
+            dma((2, n_f)),
+            dma((2, n_f)),
+            dma((2,)),
+            dma((2,)),
+            dma((3,)),
+        ],
+        compiler_params=pltpu.CompilerParams(
+            vmem_limit_bytes=VMEM_LIMIT, collective_id=1, has_side_effects=True
+        ),
+        cost_estimate=pl.CostEstimate(
+            flops=4 * n_z * rows * width * 3 * wide, bytes_accessed=30 << 20, transcendentals=0
+        ),
+        name="front",
+    )(x_own, w_qkv, w_out, w_in, bias)
+
+
 def one_head(block, head, heads):
     if heads == 1:
         return block
@@ -43,7 +334,7 @@
 
 
 def attend_kernel(*refs, blocks, heads, q_rows, k_rows):
-    ins, rest = refs[:blocks], refs[blocks:]
+    ins, rest = [refs[0].at[b] for b in range(blocks)], refs[1:]
     outs, (full_ref, lse_ref, key_s, value_s) = rest[:blocks], rest[blocks:]
     rows = ins[0].shape[0]
     width = heads * HEAD
@@ -88,8 +379,7 @@
 
 
 def attend(qkv, heads):
-    blocks = len(qkv)
-    rows = qkv[0].shape[0]
+    blocks, rows, _ = qkv.shape
     width = heads * HEAD
     length = rows * blocks
     out = [jax.ShapeDtypeStruct((rows, width), BF16)] * blocks
@@ -104,12 +394,13 @@
             transcendentals=heads * length * length,
         ),
         name="attend",
-    )(*qkv)
+    )(qkv)
     return results[:blocks], results[blocks], results[blocks + 1]
 
 
 def attend_back_kernel(*refs, blocks, heads, q_rows, k_rows):
-    ins, grads, rest = refs[:blocks], refs[blocks : 2 * blocks], refs[2 * blocks :]
+    ins = [refs[0].at[b] for b in range(blocks)]
+    grads, rest = refs[1 : blocks + 1], refs[blocks + 1 :]
     full_ref, lse_ref, rest = rest[0], rest[1], rest[2:]
     outs, (lse_t, delta_t, gq_t, key_t) = rest[:blocks], rest[blocks:]
     rows = ins[0].shape[0]
@@ -173,8 +464,7 @@
 
 
 def attend_back(qkv, grads, full, lse, heads):
-    blocks = len(qkv)
-    rows = qkv[0].shape[0]
+    blocks, rows, _ = qkv.shape
     width = heads * HEAD
     length = rows * blocks
     return pl.pallas_call(
@@ -192,7 +482,7 @@
             transcendentals=heads * length * length,
         ),
         name="attend_back",
-    )(*qkv, *grads, full, lse)
+    )(qkv, *grads, full, lse)
 
 
 def gelu_both(pre):
@@ -211,7 +501,7 @@
 def mid_kernel(*refs, n_f, n_z, cfg):
     att_refs, refs = refs[:n_z], refs[n_z:]
     (x_ref, cot_ref, vec_ref, bias_ref), refs = refs[:4], refs[4:]
-    wo_refs, refs = refs[: 2 * n_f], refs[2 * n_f :]
+    wo_ref, refs = refs[0], refs[1:]
     wi_refs, refs = refs[: 2 * n_f], refs[2 * n_f :]
     wb_refs, refs = refs[: 2 * n_f], refs[2 * n_f :]
     (layer_ref, grad_one_ref, att_ref, h_ref, act_ref, g2_ref, gp_ref, g1_ref), refs = refs[:8], refs[8:]
@@ -230,8 +520,9 @@
     step = cfg["step"]
     chunk = cfg["rows"]
 
-    copies = []
-    for pieces, target in ((wo_refs, wo_s), (wi_refs, wi_s), (wb_refs, wb_s)):
+    copies = [[pltpu.make_async_copy(wo_ref, wo_s, w_sem.at[0, 0])]]
+    copies[0][0].start()
+    for pieces, target in ((wi_refs, wi_s), (wb_refs, wb_s)):
         group = []
         for side in range(2):
             for m in range(n_f):
@@ -441,7 +732,7 @@
     results = pl.pallas_call(
         partial(mid_kernel, n_f=n_f, n_z=n_z, cfg=cfg),
         out_shape=out_shape,
-        in_specs=[in_vmem] * (n_z + 4) + [anywhere] * (6 * n_f),
+        in_specs=[in_vmem] * (n_z + 4) + [anywhere] * (4 * n_f + 1),
         out_specs=[in_vmem] * len(out_shape),
         scratch_shapes=[
             pltpu.VMEM((half_in, width), BF16),
@@ -466,8 +757,79 @@
             bytes_accessed=40 << 20, transcendentals=2 * rows * ff_half,
         ),
         name="middle",
-    )(*att, x_own, cot, vectors, bias_half[None], *wo, *wi, *wb)
+    )(*att, x_own, cot, vectors, bias_half[None], wo, *wi, *wb)
     return results[:10], results[10:]
+
+
+def tail_kernel(*refs, n_z):
+    g_refs, refs = refs[:n_z], refs[n_z:]
+    wl_ref, grad_one_ref, out_ref, cat, send_s, recv_s, send_sem, recv_sem = refs
+    ctx = lax.axis_index("ctx")
+    core, zed = ctx % 2, ctx // 2
+    partner = {"ctx": zed * 2 + (1 - core)}
+    rows, width = out_ref.shape
+    half = width // 2
+    wide = g_refs[0].shape[1] // 3
+    barrier = pltpu.get_barrier_semaphore()
+    pl.semaphore_signal(barrier, inc=1, device_id=partner, device_id_type=MESH)
+    pl.semaphore_wait(barrier, 1)
+    for j in range(3):
+        part = slice(j * wide, (j + 1) * wide)
+        if wide % 128 == 0:
+            for m in range(n_z):
+                at = pl.ds(pl.multiple_of(j * half + (zed ^ m) * wide, 128), wide)
+                cat[:, at] = g_refs[m][:, part]
+        else:
+            for m in range(0, n_z, 2):
+                one, two = g_refs[m][:, part].astype(F32), g_refs[m + 1][:, part].astype(F32)
+                odd = zed % 2 == 1
+                block = jnp.concatenate([jnp.where(odd, two, one), jnp.where(odd, one, two)], axis=1)
+                at = j * half + (zed // 2 ^ (m // 2)) * 2 * wide
+                cat[:, pl.ds(pl.multiple_of(at, 128), 2 * wide)] = block.astype(BF16)
+    step = 256
+    pieces = width // step
+
+    def move(i):
+        cols = slice(i * step, (i + 1) * step)
+        return pltpu.make_async_remote_copy(
+            src_ref=send_s.at[:, cols], dst_ref=recv_s.at[:, cols], send_sem=send_sem.at[i],
+            recv_sem=recv_sem.at[i], device_id=partner, device_id_type=MESH,
+        )
+
+    for i in range(pieces):
+        cols = slice(i * step, (i + 1) * step)
+        send_s[:, cols] = dot(cat[rows:, :], wl_ref[cols, :], NT)
+        move(i).start()
+    for i in range(pieces):
+        cols = slice(i * step, (i + 1) * step)
+        part = dot(cat[:rows, :], wl_ref[cols, :], NT) + grad_one_ref[:, cols]
+        move(i).wait_recv()
+        out_ref[:, cols] = part + recv_s[:, cols]
+    for i in range(pieces):
+        move(i).wait_send()
+
+
+def tail(grads, w_local, grad_one):
+    rows, width = grad_one.shape
+    n_z = len(grads)
+    return pl.pallas_call(
+        partial(tail_kernel, n_z=n_z),
+        out_shape=jax.ShapeDtypeStruct((rows, width), F32),
+        scratch_shapes=[
+            pltpu.VMEM((2 * rows, 3 * width // 2), BF16),
+            pltpu.VMEM((rows, width), F32),
+            pltpu.VMEM((rows, width), F32),
+            pltpu.SemaphoreType.DMA((width // 256,)),
+            pltpu.SemaphoreType.DMA((width // 256,)),
+        ],
+        compiler_params=pltpu.CompilerParams(
+            vmem_limit_bytes=VMEM_LIMIT, collective_id=2, has_side_effects=True
+        ),
+        cost_estimate=pl.CostEstimate(
+            flops=6 * rows * width * width, bytes_accessed=12 << 20, transcendentals=0
+        ),
+        name="tail",
+    )(*grads, w_local, grad_one)
 
 
 def on_device(x_in, w_qkv, w_out, w_in, w_back, vectors, bias_in, cot, *, n_ctx, n_f):
@@ -506,12 +868,15 @@
             pieces = [jnp.where(flag, pieces[m ^ (1 << bit)], pieces[m]) for m in range(count)]
         return jnp.concatenate(pieces, axis=axis)
 
-    def gather_cols(shard):
+    def gather_cols(shard, begun=None):
         half = shard.shape[0] // 2
         parts = []
-        for piece, order in ((shard[:half], bits), (shard[half:], bits[1:] + bits[:1])):
-            held = {0: piece}
-            for bit in order:
+        for side, order in enumerate((bits, bits[1:] + bits[:1])):
+            held = {0: shard[side * half : (side + 1) * half]}
+            for level, bit in enumerate(order):
+                if level == 0 and begun is not None:
+                    held[bit] = begun[side]
+                    continue
                 for m in list(held):
                     held[m ^ bit] = over_f(held[m], bit)
             parts += [held[m] for m in range(n_f)]
@@ -521,41 +886,27 @@
         return lax.optimization_barrier((value,) + others)[0]
 
     half_in = width // 2
-    mine = lax.dynamic_slice_in_dim(w_qkv, core * half_in, half_in, 0)
-    pieces = gather_cols(mine)
-    all_cols = jnp.concatenate(
-        [place(pieces[:n_f], fs, 1), place(pieces[n_f:], fs, 1)], axis=0
-    ).reshape(half_in, 3, 2, width // 2)
-    keep = lax.dynamic_index_in_dim(all_cols, core, 2, False)
-    give = lax.dynamic_index_in_dim(all_cols, 1 - core, 2, False)
-    got = swap(give)
-    w_attn = place([keep, got], core, 0)
-    w_attn = w_attn.reshape(width, 3, n_z, wide).transpose(0, 2, 1, 3).reshape(width, -1)
+    first = (core * half_heads + zed * heads) * HEAD
+    span = 3 * wide
+    bias_qkv = jnp.concatenate(
+        [
+            lax.dynamic_slice_in_dim(vectors[0], first, wide, 0),
+            jnp.zeros((wide,), F32),
+            lax.dynamic_slice_in_dim(vectors[1], first, wide, 0),
+        ]
+    )[None]
+    qkv, x_all, w_local, wo_half, wi_got = front(
+        x_own, w_qkv, w_out, w_in, bias_qkv, n_f, n_z, heads
+    )
 
     ff_part = w_in.shape[1] // 2
-    token = w_attn[0, 0]
-    wo_mine = lax.dynamic_slice_in_dim(w_out, core * (width // 2), width // 2, 0)
-    wo_half = gather_cols(after(wo_mine, got))
     wi_mine = lax.dynamic_slice_in_dim(w_in, core * ff_part, ff_part, 1)
-    wi_half = gather_cols(after(wi_mine, wo_half[-1]))
+    wi_half = gather_cols(wi_mine, wi_got)
     wb_mine = lax.dynamic_index_in_dim(
         w_back.reshape(n_f, 2, ff_part, w_back.shape[1]), core, 1, False
     ).reshape(n_f * ff_part, -1)
-    wb_half = gather_cols(after(wb_mine, wi_half[-1]))
-
-    x_two = pair(x_own)
-    span = 3 * wide
-    bias_q = vectors[0].reshape(2, n_z, 1, wide)
-    bias_v = vectors[1].reshape(2, n_z, 1, wide)
-    bias_qkv = jnp.concatenate([bias_q, jnp.zeros_like(bias_q), bias_v], axis=2)
-    bias_qkv = lax.dynamic_index_in_dim(bias_qkv.reshape(2, n_z * span), core, 0, False)
-    qkv = []
-    for m in range(n_z):
-        start = (zed ^ m) * span
-        w_part = lax.dynamic_slice_in_dim(w_attn, start, span, 1)
-        b_part = lax.dynamic_slice_in_dim(bias_qkv, start, span, 0)
-        block = (dot(x_two, w_part, NN) + b_part).astype(BF16)
-        qkv.append(block if m == 0 else over_z(block, m))
+    wb_half = gather_cols(after(wb_mine, wi_got))
+
     att, att_full, lse = attend(qkv, heads)
     att = [att[m] if m == 0 else over_z(att[m], m) for m in range(n_z)]
     bias_half = lax.dynamic_index_in_dim(
@@ -568,9 +919,10 @@
     layer_out = layer_out[None]
     g_att = [grad_att[m] if m == 0 else over_z(grad_att[m], m) for m in range(n_z)]
 
-    def reduce_rows(partial_grad):
+    low = width // (n_ctx * n_f)
+
+    def over_fsdp(partial_grad):
         cols = partial_grad.shape[1]
-        low = width // (n_ctx * n_f)
         view = partial_grad.reshape((n_z, 2) + (2,) * len(bits) + (low, cols))
         done = []
         for side in range(2):
@@ -585,7 +937,9 @@
                 go = lax.dynamic_index_in_dim(now, 1 - flag, axis, False)
                 now = (stay.astype(F32) + over_f(go, bit).astype(F32)).astype(BF16)
             done.append(now)
-        both = jnp.stack(done, axis=1)
+        return jnp.stack(done, axis=1)
+
+    def over_ctx(both):
         total = lax.dynamic_index_in_dim(both, zed, 0, False).astype(F32)
         for m in range(1, n_z):
             part = lax.dynamic_index_in_dim(both, zed ^ m, 0, False)
@@ -600,35 +954,37 @@
         second = jnp.where(core == 0, came, stay).reshape(low, parts, 1, -1)
         return jnp.concatenate([first, second], axis=2).reshape(low, -1)
 
-    ffn_grad = jnp.concatenate(
-        [dot(h_two, grad_pre_low, TN).astype(BF16), dot(g_two, act, TN).astype(BF16)], axis=1
-    )
-    ffn_grad = after(ffn_grad, g_att[0])
-    stay, came = reduce_rows(ffn_grad)
-    n_half = hidden // 2
-    in_weight_grad = halves(stay[:, :n_half], came[:, :n_half], n_f)
-    back_weight_grad = halves(stay[:, n_half:], came[:, n_half:], n_f).T
-
+    def reduced(partial_grad):
+        return over_ctx(over_fsdp(partial_grad))
+
+    in_weight_grad = halves(*reduced(dot(h_two, grad_pre_low, TN).astype(BF16)), n_f)
+    back_weight_grad = halves(*reduced(dot(g_two, act, TN).astype(BF16)), n_f).T
     att_other = swap(att_half)
     att_other = jnp.concatenate([att_other[rows:], att_other[:rows]], axis=0)
-    att_both = place([att_half, att_other], core, 1)
+    att_both = place([att_half, att_other], core, 0 + 1)
     out_cols = lax.dynamic_slice_in_dim(g_one, core * half_in, half_in, 1)
-    out_grad = dot(att_both, out_cols, TN).astype(BF16)
+    out_weight_grad = halves(*reduced(dot(att_both, out_cols, TN).astype(BF16)), 1)
 
     g_qkv = attend_back(qkv, g_att, att_full, lse, heads)
-    g_qkv = [g_qkv[m] if m == 0 else over_z(g_qkv[m], m) for m in range(n_z)]
-    g_qkv = place(g_qkv, zed, 1)
-    grad_in = grad_one + pair_sum(dot(g_qkv, w_attn, NT))
-    attn_grad = jnp.concatenate([dot(x_two, g_qkv, TN).astype(BF16), out_grad], axis=1)
-    stay, came = reduce_rows(attn_grad)
-    low = stay.shape[0]
-
-    def heads_order(cols):
-        return cols.reshape(low, n_z, 3, wide).transpose(0, 2, 1, 3).reshape(low, -1)
-
-    cut = n_z * span
-    qkv_weight_grad = halves(heads_order(stay[:, :cut]), heads_order(came[:, :cut]), 3)
-    out_weight_grad = halves(stay[:, cut:], came[:, cut:], 1)
+    g_sent = [g_qkv[m] if m == 0 else over_z(g_qkv[m], m) for m in range(n_z)]
+    g_local = jnp.concatenate(g_qkv, axis=0)
+    attn_grad = dot(x_all.reshape(-1, width), g_local, TN).astype(BF16)
+    both = over_fsdp(attn_grad)
+    mine, others = [], []
+    for m in range(n_z):
+        part = lax.dynamic_index_in_dim(both, zed ^ m, 0, False)
+        part = part if m == 0 else over_z(part, m)
+        mine.append(lax.dynamic_index_in_dim(part, core, 0, False))
+        others.append(lax.dynamic_index_in_dim(part, 1 - core, 0, False))
+    others = swap(jnp.stack(others))
+    others = [others[m] for m in range(n_z)]
+
+    def heads_order(parts):
+        parts = [p.reshape(low, 3, wide) for p in parts]
+        return place(parts, zed, 2).astype(F32).reshape(low, -1)
+
+    qkv_weight_grad = halves(heads_order(mine), heads_order(others), 3)
+    grad_in = tail(g_sent, w_local, grad_one)
 
     def spread(half_row, parts):
         piece = half_row.reshape(parts, 1, -1)
@@ -636,31 +992,37 @@
         both = jnp.where(core == 0, jnp.concatenate([piece, empty], 1), jnp.concatenate([empty, piece], 1))
         return both.reshape(-1)
 
-    sums = jnp.sum(g_qkv.astype(F32), axis=0).reshape(n_z, 3, wide)
+    def halve(now):
+        left = list(reversed(bits))
+        for bit in bits:
+            axis = left.index(bit)
+            left.remove(bit)
+            flag = (fs // bit) % 2
+            stay = lax.dynamic_index_in_dim(now, flag, axis, False)
+            now = stay + over_f(lax.dynamic_index_in_dim(now, 1 - flag, axis, False), bit)
+        return now
+
+    sums = jnp.sum(g_local.astype(F32), axis=0)
+    sums = jnp.stack([sums[:wide].reshape(n_f, -1), sums[2 * wide :].reshape(n_f, -1)], axis=1)
+    late = halve(sums.reshape((2,) * len(bits) + (-1,)))
+    turn = [(2 * z + c, n_z * c + z) for z in range(n_z) for c in range(2)]
+    late = lax.ppermute(late, "ctx", turn).reshape(2, -1)
     ratio = hidden // width
     early = sums_mid[:6].T
     bias_terms = spread(bias_sum[0], n_f).reshape(width, ratio)
-    late = jnp.stack([spread(sums[:, 0], 1), spread(sums[:, 2], 1)], axis=1)
-    table = jnp.concatenate([late, early, bias_terms], axis=1)
+    table = jnp.concatenate([early, bias_terms], axis=1)
     kinds = table.shape[1]
-    low = width // (n_ctx * n_f)
-    now = table.reshape((n_z, 2) + (2,) * len(bits) + (low, kinds))
-    now = jnp.swapaxes(now, -1, -2).reshape((n_z, 2) + (2,) * len(bits) + (kinds * low,))
-    left = list(reversed(bits))
-    for bit in bits:
-        axis = 2 + left.index(bit)
-        left.remove(bit)
-        flag = (fs // bit) % 2
-        stay = lax.dynamic_index_in_dim(now, flag, axis, False)
-        now = stay + over_f(lax.dynamic_index_in_dim(now, 1 - flag, axis, False), bit)
+    now = jnp.swapaxes(table.reshape(n_z * 2, n_f, low, kinds), -1, -2)
+    now = jnp.swapaxes(now, 0, 1).reshape((2,) * len(bits) + (n_z, 2, kinds * low))
+    now = halve(now)
     total = lax.dynamic_index_in_dim(now, zed, 0, False)
     for m in range(1, n_z):
         total = total + over_z(lax.dynamic_index_in_dim(now, zed ^ m, 0, False), m)
     stay = lax.dynamic_index_in_dim(total, core, 0, False)
     table = stay + swap(lax.dynamic_index_in_dim(total, 1 - core, 0, False))
     table = table.reshape(kinds, low)
-    vector_grad = table[:8]
-    in_bias_grad = table[8:].T.reshape(-1)
+    vector_grad = jnp.concatenate([late, table[:6]], axis=0)
+    in_bias_grad = table[6:].T.reshape(-1)
     return (
         layer_out,
         grad_in[None],

time: 611 us -> 528 us (0.86)
  waiting for transfers between devices: 252 us -> 157 us
  Pallas kernels: 129 us -> 189 us
  other arithmetic: 54.3 us -> 12.2 us
  local copies, waits for them, and re-layouts: 53.3 us -> 42.1 us
  starting transfers between devices: 78.8 us -> 89.9 us
  matrix products: 32.4 us -> 26 us
    pallas_call x0 -> x2, Pallas kernels: none -> 63.7 us  [the longest x1 52.7 us: front(): pl.pallas_call(partial(front_kernel, n_z=n_z, n_f=n_f, heads=heads), out_...]
    ppermute x34 -> x30, waiting for transfers between devices: 117 us -> 62.8 us  [over_f(): return lax.ppermute(v, 'fsdp', [(i, i ^ m) for i in range(n_f)])]
    ppermute x21 -> x24, waiting for transfers between devices: 133 us -> 92.3 us  [over_z(): return lax.ppermute(v, 'ctx', [(i, i ^ 2 * m) for i in range(n_ctx)])]
    concatenate x4 -> x2, other arithmetic: 29.2 us -> 0.61 us  [the longest x1 0.6 us: on_device(): vector_grad = jnp.concatenate([late, table[:6]], axis=0)]
    ppermute x21 -> x24, starting transfers between devices: 24.5 us -> 36 us  [over_z(): return lax.ppermute(v, 'ctx', [(i, i ^ 2 * m) for i in range(n_ctx)])]
    dynamic_slice x11 -> x9, local copies, waits for them, and re-layouts: 14.1 us -> 4 us  [the longest x6 3.98 us: over_fsdp(): stay = lax.dynamic_index_in_dim(now, flag, axis, False)]
    unnamed x115 -> x76, local copies, waits for them, and re-layouts: 9.94 us -> 19.1 us
    ppermute x34 -> x30, starting transfers between devices: 29.3 us -> 22.1 us  [over_f(): return lax.ppermute(v, 'fsdp', [(i, i ^ m) for i in range(n_f)])]
  transfers between devices with their start and end apart: 62 -> 61, of which waited for: 28 -> 29; matrix products, arithmetic and copies ran while one was open for 16% -> 12% of each run, Pallas kernels for 5% -> 12%
where the time goes in v3:
time: 528 us; the launch traced here: 518 us
  Pallas kernels  189 us (36%)
  waiting for transfers between devices  157 us (30%)
  starting transfers between devices  89.9 us (17%)
  local copies, waits for them, and re-layouts  42.1 us (8%)
  matrix products  26 us (5%)
  other arithmetic  12.2 us (2%)
    ppermute x24, waiting for transfers between devices, over_z(): return lax.ppermute(v, 'ctx', [(i, i ^ 2 * m) for i in range(n_ctx)])  92.3 us
    ppermute x30, waiting for transfers between devices, over_f(): return lax.ppermute(v, 'fsdp', [(i, i ^ m) for i in range(n_f)])  62.8 us
    pallas_call x1, Pallas kernels, front(): pl.pallas_call(partial(front_kernel, n_z=n_z, n_f=n_f, heads=heads), out_...  52.7 us
    pallas_call x1, Pallas kernels, attend_back(): pl.pallas_call(partial(attend_back_kernel, blocks=blocks, heads=heads, q_...  49.9 us
    pallas_call x1, Pallas kernels, middle(): pl.pallas_call(partial(mid_kernel, n_f=n_f, n_z=n_z, cfg=cfg), out_shape=...  42.7 us
    ppermute x24, starting transfers between devices, over_z(): return lax.ppermute(v, 'ctx', [(i, i ^ 2 * m) for i in range(n_ctx)])  36 us
    pallas_call x1, Pallas kernels, attend(): pl.pallas_call(partial(attend_kernel, blocks=blocks, heads=heads, q_rows=...  32.7 us
    dot_general x4, matrix products, dot(): return lax.dot_general(left, right, dims, preferred_element_type=F32)  26 us
  transfers between devices with their start and end apart: 61, of which 29 were waited for; matrix products, arithmetic and copies ran while one was open for 12% of the time, Pallas kernels for 12%

profile of v3, /device:TPU:23, one launch (start us, length us, event | category | flops | bytes accessed | tf_op | source)
XLA Modules:
  0.0 518.0 jit_solution(16536191133343114165)
XLA Ops:
  3.8 52.7 %front.1 = (bf16[4,768,384]{2,1,0:T(8,128)(2,1)}, bf16[4,2,384,1024]{3,2,1,0:T(8,128)(2,1)}, bf16[1024,1536]{1,0:T(8,128)(2,1)}, bf16[512,1024]{1,0:T(8,128)(2,1)S(1)}, bf16[2,512,512]{2,1,0:T(8,128)(2,1)S(1)}) custom-call(bf16[384,1024]{1,0:T(8,128)(2,1)S(1)} %bitcast.263, bf16[1024,768]{1,0:T(8,128)(2,1)} %wq_ref.1, bf16[1024,256]{1,0:T(8,128)(2,1)S(1)} %copy-done.4, ...), custom_call_target="tpu_custom_call" | custom-call | flops 2415919104 | bytes 31457280 | tf_op jit(solution)/shard_map/front/pallas_call | solution.py:279
  57.5 32.7 %attend.1 = (bf16[768,128]{1,0:T(8,128)(2,1)S(1)}, bf16[768,128]{1,0:T(8,128)(2,1)}, bf16[768,128]{1,0:T(8,128)(2,1)S(1)}, bf16[768,128]{1,0:T(8,128)(2,1)S(1)},...) custom-call(bf16[4,768,384]{2,1,0:T(8,128)(2,1)} %get-tuple-element.38.refs_0_), custom_call_target="tpu_custom_call" | custom-call | flops 19327352832 | bytes 3932160 | tf_op jit(solution)/shard_map/attend/pallas_call | solution.py:387
  93.2 10.1 %collective-permute-start = (bf16[768,128]{1,0:T(8,128)(2,1)}, bf16[768,128]{1,0:T(8,128)(2,1)}, u32[]{:S(2)}, u32[]{:S(2)}) collective-permute-start(bf16[768,128]{1,0:T(8,128)(2,1)} %get-tuple-element.40), channel_id=1, source_target_pairs={{0,8},{4,12},{8,0},{12,4},{16,24},{20,28},{24,16},{28,20},{1,9},{5... | collective-permute-start | bytes 589832 | tf_op jit(solution)/shard_map/ppermute | solution.py:851
  110.7 7.9 %collective-permute-done.1.refs_2_ = bf16[768,128]{1,0:T(8,128)(2,1)} collective-permute-done((bf16[768,128]{1,0:T(8,128)(2,1)S(1)}, bf16[768,128]{1,0:T(8,128)(2,1)}, u32[]{:S(2)}, u32[]{:S(2)}) %collective-permute-start.1) | collective-permute-done | bytes 196640 | tf_op jit(solution)/shard_map/ppermute | solution.py:851
  125.2 7.1 %collective-permute-done.10.refs_22_ = bf16[1024,256]{1,0:T(8,128)(2,1)} collective-permute-done((bf16[1024,256]{1,0:T(8,128)(2,1)}, bf16[1024,256]{1,0:T(8,128)(2,1)}, u32[]{:S(2)}, u32[]{:S(2)}) %collective-permute-start.10) | collective-permute-done | bytes 524320 | tf_op jit(solution)/shard_map/ppermute | solution.py:854
  133.8 10.3 %collective-permute-done.4.refs_12_ = bf16[512,512]{1,0:T(8,128)(2,1)} collective-permute-done((bf16[512,512]{1,0:T(8,128)(2,1)}, bf16[512,512]{1,0:T(8,128)(2,1)}, u32[]{:S(2)}, u32[]{:S(2)}) %collective-permute-start.4) | collective-permute-done | bytes 524320 | tf_op jit(solution)/shard_map/ppermute | solution.py:854
  144.8 10.6 %collective-permute-done.3.refs_11_ = bf16[512,512]{1,0:T(8,128)(2,1)S(1)} collective-permute-done((bf16[512,512]{1,0:T(8,128)(2,1)}, bf16[512,512]{1,0:T(8,128)(2,1)S(1)}, u32[]{:S(2)}, u32[]{:S(2)}) %collective-permute-start.3) | collective-permute-done | bytes 524320 | tf_op jit(solution)/shard_map/ppermute | solution.py:854
  155.4 9.6 %collective-permute-done.12.refs_24_ = bf16[1024,256]{1,0:T(8,128)(2,1)S(1)} collective-permute-done((bf16[1024,256]{1,0:T(8,128)(2,1)}, bf16[1024,256]{1,0:T(8,128)(2,1)S(1)}, u32[]{:S(2)}, u32[]{:S(2)}) %collective-permute-start.12) | collective-permute-done | bytes 524320 | tf_op jit(solution)/shard_map/ppermute | solution.py:854
  165.8 42.7 %middle.1 = (bf16[384,1024]{1,0:T(8,128)(2,1)}, f32[384,1024]{1,0:T(8,128)}, bf16[768,512]{1,0:T(8,128)(2,1)}, bf16[768,1024]{1,0:T(8,128)(2,1)}, bf16[768,2048]...) custom-call(bf16[768,128]{1,0:T(8,128)(2,1)} %copy-done.8, ...), custom_call_target="tpu_custom_call" | custom-call | flops 14495514624 | bytes 41943040 | tf_op jit(solution)/shard_map/middle/pallas_call | solution.py:732
  215.4 5.6 %convolution_convert_fusion = bf16[1024,2048]{1,0:T(8,128)(2,1)S(1)} fusion(bf16[768,1024]{1,0:T(8,128)(2,1)S(1)} %copy-done.31, bf16[768,2048]{1,0:T(8,128)(2,1)} %get-tuple-element.65), kind=kOutput, calls=%fused_computation.1 | convolution fusion | flops 3223322624 | bytes 8912896 | tf_op jit(solution)/shard_map/dot_general | solution.py:25
  223.3 12.5 %convolution_convert_fusion.1 = bf16[1024,2048]{1,0:T(8,128)(2,1)S(1)} fusion(bf16[768,1024]{1,0:T(8,128)(2,1)S(1)} %copy-done.30, bf16[768,2048]{1,0:T(8,128)(2,1)S(1)} %copy-done.29), kind=kOutput, calls=%fused_computation.2 | convolution fusion | flops 3223322624 | bytes 8912896 | tf_op jit(solution)/shard_map/dot_general | solution.py:25
  257.2 49.9 %attend_back.1 = (bf16[768,384]{1,0:T(8,128)(2,1)S(1)}, bf16[768,384]{1,0:T(8,128)(2,1)S(1)}, bf16[768,384]{1,0:T(8,128)(2,1)S(1)}, bf16[768,384]{1,0:T(8,128)(2,1)S(1)}) custom-call(bf16[4,768,384]{2,1,0:T(8,128)(2,1)} %get-tuple-element.38.refs_0_, bf16[768,128]{1,0:T(8,128)(2,1)S(1)} %copy-done.9, bf16[768,128]{1,0:T(8,128)(2,1)S(1)} %collective-permute-done.13.refs_2_, ...), custom_call_target="tpu_custom_call" | custom-call | flops 48318382080 | bytes 7864320 | tf_op jit(solution)/shard_map/attend_back/pallas_call | solution.py:470
  309.7 6.9 %convolution_convert_fusion.2 = bf16[1024,384]{1,0:T(8,128)(2,1)S(1)} fusion(bf16[3072,1024]{1,0:T(8,128)(2,1)} %bitcast.283, bf16[3072,384]{1,0:T(8,128)(2,1)} %copy-done.15), kind=kOutput, calls=%fused_computation.32 | convolution fusion | flops 2416312320 | bytes 9437184 | tf_op jit(solution)/shard_map/dot_general | solution.py:25
  319.3 6.0 %collective-permute-start.54 = (f32[64]{0:T(128)S(1)}, f32[64]{0:T(128)S(1)}, u32[]{:S(2)}, u32[]{:S(2)}) collective-permute-start(f32[64]{0:T(128)S(1)} %fusion.95), channel_id=1, source_target_pairs={{0,0},{4,16},{8,4},{12,20},{16,8},{20,24},{24,12},{28,28},{1,1},{5... | collective-permute-start | bytes 776 | tf_op jit(solution)/shard_map/ppermute | solution.py:1009
  344.4 8.8 %collective-permute-done.25 = bf16[2,32,384]{2,1,0:T(8,128)(2,1)S(1)} collective-permute-done((bf16[2,32,384]{2,1,0:T(8,128)(2,1)S(1)}, bf16[2,32,384]{2,1,0:T(8,128)(2,1)S(1)}, u32[]{:S(2)}, u32[]{:S(2)}) %collective-permute-start.25) | collective-permute-done | bytes 49184 | tf_op jit(solution)/shard_map/ppermute | solution.py:851
  353.2 4.8 collective-permute-start.26
  370.7 29.7 %collective-permute-done.17.refs_2_ = bf16[768,384]{1,0:T(8,128)(2,1)} collective-permute-done((bf16[768,384]{1,0:T(8,128)(2,1)S(1)}, bf16[768,384]{1,0:T(8,128)(2,1)}, u32[]{:S(2)}, u32[]{:S(2)}) %collective-permute-start.17) | collective-permute-done | bytes 589856 | tf_op jit(solution)/shard_map/ppermute | solution.py:851
  401.2 11.8 %collective-permute-done.18.refs_3_ = bf16[768,384]{1,0:T(8,128)(2,1)S(1)} collective-permute-done((bf16[768,384]{1,0:T(8,128)(2,1)S(1)}, bf16[768,384]{1,0:T(8,128)(2,1)S(1)}, u32[]{:S(2)}, u32[]{:S(2)}) %collective-permute-start.18) | collective-permute-done | bytes 589856 | tf_op jit(solution)/shard_map/ppermute | solution.py:851
  413.0 11.0 %tail.1 = f32[384,1024]{1,0:T(8,128)S(1)} custom-call(bf16[768,384]{1,0:T(8,128)(2,1)S(1)} %get-tuple-element.53.refs_0_, bf16[768,384]{1,0:T(8,128)(2,1)S(1)} %collective-permute-done.16.refs_1_, bf16[768,384]{1,0:T(8,128)(2,1)} %collective-permute-done.17.refs_2_, bf16[768,384]{1,0:T(8,128)(2,1)S(1)} %collective-permute-done.18.refs_3_, ...), custom_call_target="tpu_custom_call" | custom-call | flops 2415919104 | bytes 12582912 | tf_op jit(solution)/shard_map/tail/pallas_call | solution.py:815
  435.5 10.6 %collective-permute-done.31 = bf16[4,32,512]{2,1,0:T(8,128)(2,1)S(1)} collective-permute-done((bf16[4,32,512]{2,1,0:T(8,128)(2,1)S(1)}, bf16[4,32,512]{2,1,0:T(8,128)(2,1)S(1)}, u32[]{:S(2)}, u32[]{:S(2)}) %collective-permute-start.31) | collective-permute-done | bytes 131104 | tf_op jit(solution)/shard_map/ppermute | solution.py:854
  462.1 8.1 %collective-permute-done.37 = bf16[4,32,2048]{2,1,0:T(8,128)(2,1)S(1)} collective-permute-done((bf16[4,32,2048]{2,1,0:T(8,128)(2,1)S(1)}, bf16[4,32,2048]{2,1,0:T(8,128)(2,1)S(1)}, u32[]{:S(2)}, u32[]{:S(2)}) %collective-permute-start.37) | collective-permute-done | bytes 524320 | tf_op jit(solution)/shard_map/ppermute | solution.py:854
  473.6 11.1 %collective-permute-done.50 = bf16[2,32,2048]{2,1,0:T(8,128)(2,1)S(1)} collective-permute-done((bf16[2,32,2048]{2,1,0:T(8,128)(2,1)S(1)}, bf16[2,32,2048]{2,1,0:T(8,128)(2,1)S(1)}, u32[]{:S(2)}, u32[]{:S(2)}) %collective-permute-start.50) | collective-permute-done | bytes 262176 | tf_op jit(solution)/shard_map/ppermute | solution.py:851
  484.9 13.7 %collective-permute-start.51 = (bf16[32,2048]{1,0:T(8,128)(2,1)S(1)}, bf16[32,2048]{1,0:T(8,128)(2,1)S(1)}, u32[]{:S(2)}, u32[]{:S(2)}) collective-permute-start(bf16[32,2048]{1,0:T(8,128)(2,1)S(1)} %fusion.49), channel_id=1, source_target_pairs={{0,4},{4,0},{8,12},{12,8},{16,20},{20,16},{24,28},{28,24},{1,5},{5... | collective-permute-start | bytes 393224 | tf_op jit(solution)/shard_map/ppermute | solution.py:848
  500.7 6.5 %collective-permute-done.42 = bf16[2,32,2048]{2,1,0:T(8,128)(2,1)S(1)} collective-permute-done((bf16[2,32,2048]{2,1,0:T(8,128)(2,1)S(1)}, bf16[2,32,2048]{2,1,0:T(8,128)(2,1)S(1)}, u32[]{:S(2)}, u32[]{:S(2)}) %collective-permute-start.42) | collective-permute-done | bytes 262176 | tf_op jit(solution)/shard_map/ppermute | solution.py:851
  (309 shorter events, 135.0 us)
Async XLA Ops:
  110.4 21.9 %collective-permute-start.10 = (bf16[1024,256]{1,0:T(8,128)(2,1)}, bf16[1024,256]{1,0:T(8,128)(2,1)}, u32[]{:S(2)}, u32[]{:S(2)}) collective-permute-start(bf16[1024,256]{1,0:T(8,128)(2,1)} %get-tuple-element.92.refs_21_), channel_id=1, source_target_pairs={{0,1},{1,0},{2,3},{3,2},{4,5},{5,4},{6,7},{7,6},{8,9},{9,8},{10,11... | collective-permute-start | bytes 1572872 | tf_op jit(solution)/shard_map/ppermute | solution.py:854
  122.6 21.4 %collective-permute-start.4 = (bf16[512,512]{1,0:T(8,128)(2,1)}, bf16[512,512]{1,0:T(8,128)(2,1)}, u32[]{:S(2)}, u32[]{:S(2)}) collective-permute-start(bf16[512,512]{1,0:T(8,128)(2,1)} %get-tuple-element.95.refs_10_), channel_id=1, source_target_pairs={{0,2},{1,3},{2,0},{3,1},{4,6},{5,7},{6,4},{7,5},{8,10},{9,11},{10,... | collective-permute-start | bytes 1572872 | tf_op jit(solution)/shard_map/ppermute | solution.py:854
  123.6 21.2 %collective-permute-start.6 = (bf16[512,512]{1,0:T(8,128)(2,1)S(1)}, bf16[512,512]{1,0:T(8,128)(2,1)S(1)}, u32[]{:S(2)}, u32[]{:S(2)}) collective-permute-start(bf16[512,512]{1,0:T(8,128)(2,1)S(1)} %copy-done.20), channel_id=1, source_target_pairs={{0,1},{1,0},{2,3},{3,2},{4,5},{5,4},{6,7},{7,6},{8,9},{9,8},{10,11... | collective-permute-start | bytes 1572872 | tf_op jit(solution)/shard_map/ppermute | solution.py:854
  123.7 31.7 %collective-permute-start.3 = (bf16[512,512]{1,0:T(8,128)(2,1)}, bf16[512,512]{1,0:T(8,128)(2,1)S(1)}, u32[]{:S(2)}, u32[]{:S(2)}) collective-permute-start(bf16[512,512]{1,0:T(8,128)(2,1)} %get-tuple-element.81.refs_9_), channel_id=1, source_target_pairs={{0,2},{1,3},{2,0},{3,1},{4,6},{5,7},{6,4},{7,5},{8,10},{9,11},{10,... | collective-permute-start | bytes 1572872 | tf_op jit(solution)/shard_map/ppermute | solution.py:854
  132.3 23.1 %collective-permute-start.5 = (bf16[512,512]{1,0:T(8,128)(2,1)S(1)}, bf16[512,512]{1,0:T(8,128)(2,1)S(1)}, u32[]{:S(2)}, u32[]{:S(2)}) collective-permute-start(bf16[512,512]{1,0:T(8,128)(2,1)S(1)} %get-tuple-element.80.refs_13_), channel_id=1, source_target_pairs={{0,1},{1,0},{2,3},{3,2},{4,5},{5,4},{6,7},{7,6},{8,9},{9,8},{10,11... | collective-permute-start | bytes 1572872 | tf_op jit(solution)/shard_map/ppermute | solution.py:854
  132.9 32.0 %collective-permute-start.12 = (bf16[1024,256]{1,0:T(8,128)(2,1)}, bf16[1024,256]{1,0:T(8,128)(2,1)S(1)}, u32[]{:S(2)}, u32[]{:S(2)}) collective-permute-start(bf16[1024,256]{1,0:T(8,128)(2,1)} %collective-permute-done.11.refs_23_), channel_id=1, source_target_pairs={{0,1},{1,0},{2,3},{3,2},{4,5},{5,4},{6,7},{7,6},{8,9},{9,8},{10,11... | collective-permute-start | bytes 1572872 | tf_op jit(solution)/shard_map/ppermute | solution.py:854
  208.5 48.4 %collective-permute-start.13 = (bf16[768,128]{1,0:T(8,128)(2,1)}, bf16[768,128]{1,0:T(8,128)(2,1)S(1)}, u32[]{:S(2)}, u32[]{:S(2)}) collective-permute-start(bf16[768,128]{1,0:T(8,128)(2,1)} %get-tuple-element.48), channel_id=1, source_target_pairs={{0,8},{4,12},{8,0},{12,4},{16,24},{20,28},{24,16},{28,20},{1,9},{5... | collective-permute-start | bytes 589832 | tf_op jit(solution)/shard_map/ppermute | solution.py:851
  210.5 46.6 %collective-permute-start.14 = (bf16[768,128]{1,0:T(8,128)(2,1)}, bf16[768,128]{1,0:T(8,128)(2,1)S(1)}, u32[]{:S(2)}, u32[]{:S(2)}) collective-permute-start(bf16[768,128]{1,0:T(8,128)(2,1)} %get-tuple-element.49), channel_id=1, source_target_pairs={{0,16},{4,20},{8,24},{12,28},{16,0},{20,4},{24,8},{28,12},{1,17},{... | collective-permute-start | bytes 589832 | tf_op jit(solution)/shard_map/ppermute | solution.py:851
  214.9 23.0 %collective-permute-start.55 = (f32[2,4,2,320]{3,2,1,0:T(2,128)S(1)}, f32[2,4,2,320]{3,2,1,0:T(2,128)S(1)}, u32[]{:S(2)}, u32[]{:S(2)}) collective-permute-start(f32[2,4,2,320]{3,2,1,0:T(2,128)S(1)} %fusion.78), channel_id=1, source_target_pairs={{0,1},{1,0},{2,3},{3,2},{4,5},{5,4},{6,7},{7,6},{8,9},{9,8},{10,11... | collective-permute-start | bytes 61448 | tf_op jit(solution)/shard_map/ppermute | solution.py:854
  245.9 178.2 %collective-permute-start.46 = (bf16[4,2,32,2048]{3,2,0,1:T(8,128)(2,1)}, bf16[4,2,32,2048]{3,2,0,1:T(8,128)(2,1)}, u32[]{:S(2)}, u32[]{:S(2)}) collective-permute-start(bf16[4,2,32,2048]{3,2,0,1:T(8,128)(2,1)} %bitcast.254), channel_id=1, source_target_pairs={{0,2},{1,3},{2,0},{3,1},{4,6},{5,7},{6,4},{7,5},{8,10},{9,11},{10,... | collective-permute-start | bytes 3145736 | tf_op jit(solution)/shard_map/ppermute | solution.py:854
  254.2 173.0 %collective-permute-start.44 = (bf16[4,2,32,2048]{3,2,0,1:T(8,128)(2,1)}, bf16[4,2,32,2048]{3,2,0,1:T(8,128)(2,1)}, u32[]{:S(2)}, u32[]{:S(2)}) collective-permute-start(bf16[4,2,32,2048]{3,2,0,1:T(8,128)(2,1)} %bitcast.255), channel_id=1, source_target_pairs={{0,1},{1,0},{2,3},{3,2},{4,5},{5,4},{6,7},{7,6},{8,9},{9,8},{10,11... | collective-permute-start | bytes 3145736 | tf_op jit(solution)/shard_map/ppermute | solution.py:854
  256.8 108.7 %collective-permute-start.27 = (bf16[768,512]{1,0:T(8,128)(2,1)}, bf16[768,512]{1,0:T(8,128)(2,1)}, u32[]{:S(2)}, u32[]{:S(2)}) collective-permute-start(bf16[768,512]{1,0:T(8,128)(2,1)} %get-tuple-element.60), channel_id=1, source_target_pairs={{0,4},{4,0},{8,12},{12,8},{16,20},{20,16},{24,28},{28,24},{1,5},{5... | collective-permute-start | bytes 2359304 | tf_op jit(solution)/shard_map/ppermute | solution.py:848
  340.6 28.9 %collective-permute-start.16 = (bf16[768,384]{1,0:T(8,128)(2,1)S(1)}, bf16[768,384]{1,0:T(8,128)(2,1)S(1)}, u32[]{:S(2)}, u32[]{:S(2)}) collective-permute-start(bf16[768,384]{1,0:T(8,128)(2,1)S(1)} %get-tuple-element.54), channel_id=1, source_target_pairs={{0,8},{4,12},{8,0},{12,4},{16,24},{20,28},{24,16},{28,20},{1,9},{5... | collective-permute-start | bytes 1769480 | tf_op jit(solution)/shard_map/ppermute | solution.py:851
  359.0 41.3 %collective-permute-start.17 = (bf16[768,384]{1,0:T(8,128)(2,1)S(1)}, bf16[768,384]{1,0:T(8,128)(2,1)}, u32[]{:S(2)}, u32[]{:S(2)}) collective-permute-start(bf16[768,384]{1,0:T(8,128)(2,1)S(1)} %get-tuple-element.55), channel_id=1, source_target_pairs={{0,16},{4,20},{8,24},{12,28},{16,0},{20,4},{24,8},{28,12},{1,17},{... | collective-permute-start | bytes 1769480 | tf_op jit(solution)/shard_map/ppermute | solution.py:851
  365.6 47.4 %collective-permute-start.18 = (bf16[768,384]{1,0:T(8,128)(2,1)S(1)}, bf16[768,384]{1,0:T(8,128)(2,1)S(1)}, u32[]{:S(2)}, u32[]{:S(2)}) collective-permute-start(bf16[768,384]{1,0:T(8,128)(2,1)S(1)} %get-tuple-element.56), channel_id=1, source_target_pairs={{0,24},{4,28},{8,16},{12,20},{16,8},{20,12},{24,0},{28,4},{1,25},{... | collective-permute-start | bytes 1769480 | tf_op jit(solution)/shard_map/ppermute | solution.py:851
  370.6 64.5 %collective-permute-start.38 = (bf16[4,2,32,2048]{3,2,1,0:T(8,128)(2,1)S(1)}, bf16[4,2,32,2048]{3,2,1,0:T(8,128)(2,1)S(1)}, u32[]{:S(2)}, u32[]{:S(2)}) collective-permute-start(bf16[4,2,32,2048]{3,2,1,0:T(8,128)(2,1)S(1)} %copy-done.16), channel_id=1, source_target_pairs={{0,2},{1,3},{2,0},{3,1},{4,6},{5,7},{6,4},{7,5},{8,10},{9,11},{10,... | collective-permute-start | bytes 3145736 | tf_op jit(solution)/shard_map/ppermute | solution.py:854
  400.3 33.1 %collective-permute-start.36 = (bf16[4,2,32,2048]{3,2,0,1:T(8,128)(2,1)S(1)}, bf16[4,2,32,2048]{3,2,0,1:T(8,128)(2,1)S(1)}, u32[]{:S(2)}, u32[]{:S(2)}) collective-permute-start(bf16[4,2,32,2048]{3,2,0,1:T(8,128)(2,1)S(1)} %bitcast.267), channel_id=1, source_target_pairs={{0,1},{1,0},{2,3},{3,2},{4,5},{5,4},{6,7},{7,6},{8,9},{9,8},{10,11... | collective-permute-start | bytes 3145736 | tf_op jit(solution)/shard_map/ppermute | solution.py:854
  427.2 31.7 %collective-permute-start.47 = (bf16[4,32,2048]{2,1,0:T(8,128)(2,1)S(1)}, bf16[4,32,2048]{2,1,0:T(8,128)(2,1)S(1)}, u32[]{:S(2)}, u32[]{:S(2)}) collective-permute-start(bf16[4,32,2048]{2,1,0:T(8,128)(2,1)S(1)} %dynamic-slice_bitcast_fusion.1), channel_id=1, source_target_pairs={{0,1},{1,0},{2,3},{3,2},{4,5},{5,4},{6,7},{7,6},{8,9},{9,8},{10,11... | collective-permute-start | bytes 1572872 | tf_op jit(solution)/shard_map/ppermute | solution.py:854
  429.3 29.6 %collective-permute-start.45 = (bf16[4,32,2048]{2,1,0:T(8,128)(2,1)S(1)}, bf16[4,32,2048]{2,1,0:T(8,128)(2,1)S(1)}, u32[]{:S(2)}, u32[]{:S(2)}) collective-permute-start(bf16[4,32,2048]{2,1,0:T(8,128)(2,1)S(1)} %dynamic-slice_bitcast_fusion.2), channel_id=1, source_target_pairs={{0,2},{1,3},{2,0},{3,1},{4,6},{5,7},{6,4},{7,5},{8,10},{9,11},{10,... | collective-permute-start | bytes 1572872 | tf_op jit(solution)/shard_map/ppermute | solution.py:854
  461.8 22.9 %collective-permute-start.50 = (bf16[2,32,2048]{2,1,0:T(8,128)(2,1)S(1)}, bf16[2,32,2048]{2,1,0:T(8,128)(2,1)S(1)}, u32[]{:S(2)}, u32[]{:S(2)}) collective-permute-start(bf16[2,32,2048]{2,1,0:T(8,128)(2,1)S(1)} %get-tuple-element.86), channel_id=1, source_target_pairs={{0,24},{4,28},{8,16},{12,20},{16,8},{20,12},{24,0},{28,4},{1,25},{... | collective-permute-start | bytes 786440 | tf_op jit(solution)/shard_map/ppermute | solution.py:851
  470.4 28.2 %collective-permute-start.40 = (bf16[2,32,2048]{2,1,0:T(8,128)(2,1)S(1)}, bf16[2,32,2048]{2,1,0:T(8,128)(2,1)S(1)}, u32[]{:S(2)}, u32[]{:S(2)}) collective-permute-start(bf16[2,32,2048]{2,1,0:T(8,128)(2,1)S(1)} %get-tuple-element.87), channel_id=1, source_target_pairs={{0,8},{4,12},{8,0},{12,4},{16,24},{20,28},{24,16},{28,20},{1,9},{5... | collective-permute-start | bytes 786440 | tf_op jit(solution)/shard_map/ppermute | solution.py:851
  471.2 29.5 %collective-permute-start.41 = (bf16[2,32,2048]{2,1,0:T(8,128)(2,1)S(1)}, bf16[2,32,2048]{2,1,0:T(8,128)(2,1)S(1)}, u32[]{:S(2)}, u32[]{:S(2)}) collective-permute-start(bf16[2,32,2048]{2,1,0:T(8,128)(2,1)S(1)} %get-tuple-element.88), channel_id=1, source_target_pairs={{0,16},{4,20},{8,24},{12,28},{16,0},{20,4},{24,8},{28,12},{1,17},{... | collective-permute-start | bytes 786440 | tf_op jit(solution)/shard_map/ppermute | solution.py:851
  473.0 34.2 %collective-permute-start.42 = (bf16[2,32,2048]{2,1,0:T(8,128)(2,1)S(1)}, bf16[2,32,2048]{2,1,0:T(8,128)(2,1)S(1)}, u32[]{:S(2)}, u32[]{:S(2)}) collective-permute-start(bf16[2,32,2048]{2,1,0:T(8,128)(2,1)S(1)} %get-tuple-element.89), channel_id=1, source_target_pairs={{0,24},{4,28},{8,16},{12,20},{16,8},{20,12},{24,0},{28,4},{1,25},{... | collective-permute-start | bytes 786440 | tf_op jit(solution)/shard_map/ppermute | solution.py:851
  484.9 24.2 %collective-permute-start.51 = (bf16[32,2048]{1,0:T(8,128)(2,1)S(1)}, bf16[32,2048]{1,0:T(8,128)(2,1)S(1)}, u32[]{:S(2)}, u32[]{:S(2)}) collective-permute-start(bf16[32,2048]{1,0:T(8,128)(2,1)S(1)} %fusion.49), channel_id=1, source_target_pairs={{0,4},{4,0},{8,12},{12,8},{16,20},{20,16},{24,28},{28,24},{1,5},{5... | collective-permute-start | bytes 393224 | tf_op jit(solution)/shard_map/ppermute | solution.py:848
  (69 other events, 708.2 us)

commit v4 on v3

--- a/solution.py
+++ b/solution.py
@@ -333,17 +333,90 @@
     return result
 
 
-def attend_kernel(*refs, blocks, heads, q_rows, k_rows):
-    ins, rest = [refs[0].at[b] for b in range(blocks)], refs[1:]
-    outs, (full_ref, lse_ref, key_s, value_s) = rest[:blocks], rest[blocks:]
+def remote(src, dst, send, recv, device):
+    return pltpu.make_async_remote_copy(
+        src_ref=src, dst_ref=dst, send_sem=send, recv_sem=recv, device_id=device, device_id_type=MESH
+    )
+
+
+def greet(barrier, devices):
+    for device in devices:
+        pl.semaphore_signal(barrier, inc=1, device_id=device, device_id_type=MESH)
+    pl.semaphore_wait(barrier, len(devices))
+
+
+def fsdp_orders(n_f):
+    bits = [1 << b for b in range(n_f.bit_length() - 1)]
+    return bits, (bits, bits[1:] + bits[:1])
+
+
+def known_at(order, level):
+    known = [0]
+    for bit in order[:level]:
+        known = known + [m ^ bit for m in known]
+    return known
+
+
+def attend_kernel(*refs, blocks, heads, n_f, q_rows, k_rows):
+    qkv_ref, wi_ref, got_ref, wb_ref = refs[:4]
+    att_ref, full_ref, lse_ref, wi_out, wb_out = refs[4:9]
+    key_s, value_s, send_s, a_send, a_recv, i_send, i_recv, b_send, b_recv, own_sem = refs[9:]
+    ins = [qkv_ref.at[b] for b in range(blocks)]
     rows = ins[0].shape[0]
     width = heads * HEAD
     length = rows * blocks
+    ctx, fs = lax.axis_index("ctx"), lax.axis_index("fsdp")
+    core, zed = ctx % 2, ctx // 2
+    bits, orders = fsdp_orders(n_f)
+    greet(
+        pltpu.get_barrier_semaphore(),
+        [{"fsdp": fs ^ bit} for bit in bits] + [{"ctx": (zed ^ m) * 2 + core} for m in range(1, blocks)],
+    )
+
+    half, part = got_ref.shape[1:]
+
+    def wi_place(side, m):
+        return wi_out.at[pl.ds(side * half, half), pl.ds(pl.multiple_of((fs ^ m) * part, 128), part)]
+
+    def wi_source(side, m):
+        if m == 0:
+            return wi_ref.at[pl.ds(side * half, half), pl.ds(pl.multiple_of(core * part, 128), part)]
+        return got_ref.at[side] if m == orders[side][0] else wi_place(side, m)
+
+    def wi_hop(side, m, bit):
+        return remote(
+            wi_source(side, m), wi_place(side, m), i_send.at[side, m ^ bit], i_recv.at[side, m ^ bit], {"fsdp": fs ^ bit}
+        )
+
+    def wb_hop(seg):
+        return remote(
+            wb_ref.at[seg, core], wb_out.at[seg], b_send.at[seg], b_recv.at[seg],
+            {"fsdp": fs ^ orders[seg * 2 // n_f][0]},
+        )
+
+    def level(number, act):
+        for side in range(2):
+            for m in known_at(orders[side], number):
+                act(wi_hop(side, m, orders[side][number]))
+
+    locals_ = []
+    for side in range(2):
+        for i, m in enumerate((0, orders[side][0])):
+            locals_.append(pltpu.make_async_copy(wi_source(side, m), wi_place(side, m), own_sem.at[2 * side + i]))
+    for copy in locals_:
+        copy.start()
+    level(1, lambda hop: hop.start())
+    for seg in range(n_f):
+        wb_hop(seg).start()
+
+    def att_hop(b):
+        return remote(send_s.at[b - 1], att_ref.at[b], a_send.at[b], a_recv.at[b], {"ctx": (zed ^ b) * 2 + core})
+
     for b in range(blocks):
         here = slice(b * rows, (b + 1) * rows)
         key_s[here, :] = ins[b][:, width : 2 * width]
         value_s[here, :] = ins[b][:, 2 * width : 3 * width]
-    for b in range(blocks):
+    for turn, b in enumerate(list(range(blocks - 1, 0, -1)) + [0]):
 
         def step(i, carry, b=b):
             local = pl.ds(pl.multiple_of(i * q_rows, q_rows), q_rows)
@@ -371,36 +444,75 @@
                 sums.append(jnp.broadcast_to(top + jnp.log(total), (q_rows, width)))
             result = merge_heads(outputs)
             full_ref[where, :] = result
-            outs[b][local, :] = result.astype(BF16)
+            if b == 0:
+                att_ref[0, local, :] = result.astype(BF16)
+            else:
+                send_s[b - 1, local, :] = result.astype(BF16)
             lse_ref[where, :] = merge_heads(sums)
             return carry
 
         lax.fori_loop(0, rows // q_rows, step, 0)
-
-
-def attend(qkv, heads):
+        if b > 0:
+            att_hop(b).start()
+        if 0 < turn < len(bits) - 1:
+            level(turn, lambda hop: hop.wait_recv())
+            level(turn + 1, lambda hop: hop.start())
+    level(len(bits) - 1, lambda hop: hop.wait_recv())
+    for number in range(1, len(bits)):
+        level(number, lambda hop: hop.wait_send())
+    for seg in range(n_f):
+        wb_hop(seg).wait()
+    for b in range(1, blocks):
+        att_hop(b).wait()
+    for copy in locals_:
+        copy.wait()
+
+
+def attend(qkv, w_in, wi_got, w_back4, heads, n_f):
     blocks, rows, _ = qkv.shape
     width = heads * HEAD
     length = rows * blocks
-    out = [jax.ShapeDtypeStruct((rows, width), BF16)] * blocks
-    out += [jax.ShapeDtypeStruct((length, width), F32)] * 2
-    results = pl.pallas_call(
-        partial(attend_kernel, blocks=blocks, heads=heads, q_rows=256, k_rows=512),
-        out_shape=out,
-        scratch_shapes=[pltpu.VMEM((length, width), BF16)] * 2,
-        compiler_params=pltpu.CompilerParams(vmem_limit_bytes=VMEM_LIMIT),
+    _, half, part = wi_got.shape
+    _, _, seg_rows, seg_cols = w_back4.shape
+    sds = jax.ShapeDtypeStruct
+    in_vmem, anywhere = pl.BlockSpec(memory_space=pltpu.VMEM), pl.BlockSpec(memory_space=pl.ANY)
+    dma = pltpu.SemaphoreType.DMA
+    return pl.pallas_call(
+        partial(attend_kernel, blocks=blocks, heads=heads, n_f=n_f, q_rows=256, k_rows=512),
+        out_shape=[
+            sds((blocks, rows, width), BF16),
+            sds((length, width), F32),
+            sds((length, width), F32),
+            sds((2 * half, n_f * part), BF16),
+            sds((n_f, seg_rows, seg_cols), BF16),
+        ],
+        in_specs=[in_vmem] + [anywhere] * 3,
+        out_specs=[in_vmem] * 3 + [anywhere] * 2,
+        scratch_shapes=[pltpu.VMEM((length, width), BF16)] * 2
+        + [
+            pltpu.VMEM((blocks - 1, rows, width), BF16),
+            dma((blocks,)),
+            dma((blocks,)),
+            dma((2, n_f)),
+            dma((2, n_f)),
+            dma((n_f,)),
+            dma((n_f,)),
+            dma((4,)),
+        ],
+        compiler_params=pltpu.CompilerParams(
+            vmem_limit_bytes=VMEM_LIMIT, collective_id=3, has_side_effects=True
+        ),
         cost_estimate=pl.CostEstimate(
             flops=16 * length * length * width, bytes_accessed=10 * length * width,
             transcendentals=heads * length * length,
         ),
         name="attend",
-    )(qkv)
-    return results[:blocks], results[blocks], results[blocks + 1]
+    )(qkv, w_in, wi_got, w_back4)
 
 
 def attend_back_kernel(*refs, blocks, heads, q_rows, k_rows):
     ins = [refs[0].at[b] for b in range(blocks)]
-    grads, rest = refs[1 : blocks + 1], refs[blocks + 1 :]
+    grads, rest = [refs[1].at[b] for b in range(blocks)], refs[2:]
     full_ref, lse_ref, rest = rest[0], rest[1], rest[2:]
     outs, (lse_t, delta_t, gq_t, key_t) = rest[:blocks], rest[blocks:]
     rows = ins[0].shape[0]
@@ -482,7 +594,7 @@
             transcendentals=heads * length * length,
         ),
         name="attend_back",
-    )(qkv, *grads, full, lse)
+    )(qkv, grads, full, lse)
 
 
 def gelu_both(pre):
@@ -499,51 +611,67 @@
 
 
 def mid_kernel(*refs, n_f, n_z, cfg):
-    att_refs, refs = refs[:n_z], refs[n_z:]
-    (x_ref, cot_ref, vec_ref, bias_ref), refs = refs[:4], refs[4:]
-    wo_ref, refs = refs[0], refs[1:]
-    wi_refs, refs = refs[: 2 * n_f], refs[2 * n_f :]
-    wb_refs, refs = refs[: 2 * n_f], refs[2 * n_f :]
-    (layer_ref, grad_one_ref, att_ref, h_ref, act_ref, g2_ref, gp_ref, g1_ref), refs = refs[:8], refs[8:]
-    (sums_ref, bias_sum_ref), refs = refs[:2], refs[2:]
-    ga_refs, refs = refs[:n_z], refs[n_z:]
-    (wo_s, wi_s, wb_s, slope_s, normed_s, unit_s, acc_s, send_s, recv_s, rstd_s), refs = refs[:10], refs[10:]
-    w_sem, send_sem, recv_sem = refs
+    att_in, x_ref, cot_ref, vec_ref, bias_ref, wo_ref, wi_ref, wb_ref, got_ref = refs[:9]
+    layer_ref, grad_one_ref, ga_ref, sums_ref, bias_sum_ref, grads_out = refs[9:15]
+    att_ref, att2_s, h_ref, act_ref, g2_ref, gp_ref, g1_ref, ga_s, turned_s, og_s = refs[15:25]
+    wo_s, wi_s, wb_s, slope_s, normed_s, unit_s, acc_s, send_s, recv_s, rstd_s = refs[25:35]
+    w_sem, send_sem, recv_sem, b_send, b_recv, a_send, a_recv, g_sem = refs[35:]
     ctx, fs = lax.axis_index("ctx"), lax.axis_index("fsdp")
     core, zed = ctx % 2, ctx // 2
     partner = {"ctx": zed * 2 + (1 - core)}
     rows, width = x_ref.shape
     own, other = slice(0, rows), slice(rows, 2 * rows)
-    wide = att_refs[0].shape[1]
+    wide = att_in.shape[2]
     half_in = n_z * wide
     ff_half = wi_s.shape[1]
     step = cfg["step"]
     chunk = cfg["rows"]
-
-    copies = [[pltpu.make_async_copy(wo_ref, wo_s, w_sem.at[0, 0])]]
-    copies[0][0].start()
-    for pieces, target in ((wi_refs, wi_s), (wb_refs, wb_s)):
-        group = []
-        for side in range(2):
-            for m in range(n_f):
-                piece = pieces[side * n_f + m]
-                p_rows, p_cols = piece.shape
-                where = pl.ds(pl.multiple_of((fs ^ m) * p_cols, p_cols), p_cols)
-                copy = pltpu.make_async_copy(
-                    piece, target.at[pl.ds(side * p_rows, p_rows), where], w_sem.at[len(copies), side * n_f + m]
-                )
-                copy.start()
-                group.append(copy)
-        copies.append(group)
-    barrier = pltpu.get_barrier_semaphore()
-    pl.semaphore_signal(barrier, inc=1, device_id=partner, device_id_type=MESH)
-    pl.semaphore_wait(barrier, 1)
+    bits, orders = fsdp_orders(n_f)
+    _, _, seg_rows, seg_cols = wb_ref.shape
+
+    def wb_place(seg, m):
+        return wb_s.at[
+            pl.ds(seg * seg_rows, seg_rows), pl.ds(pl.multiple_of((fs ^ m) * seg_cols, 128), seg_cols)
+        ]
+
+    def wb_order(seg):
+        return orders[seg * 2 // n_f]
+
+    def wb_source(seg, m):
+        if m == 0:
+            return wb_ref.at[seg, core]
+        return got_ref.at[seg] if m == wb_order(seg)[0] else wb_place(seg, m)
+
+    def wb_hop(seg, m, bit):
+        return remote(
+            wb_source(seg, m), wb_place(seg, m), b_send.at[seg, m ^ bit], b_recv.at[seg, m ^ bit], {"fsdp": fs ^ bit}
+        )
+
+    def wb_level(number, act):
+        for seg in range(n_f):
+            for m in known_at(wb_order(seg), number):
+                act(wb_hop(seg, m, wb_order(seg)[number]))
+
+    copies = [
+        [pltpu.make_async_copy(wo_ref, wo_s, w_sem.at[0])],
+        [pltpu.make_async_copy(wi_ref, wi_s, w_sem.at[1])],
+        [],
+    ]
+    for seg in range(n_f):
+        for i, m in enumerate((0, wb_order(seg)[0])):
+            copies[2].append(pltpu.make_async_copy(wb_source(seg, m), wb_place(seg, m), w_sem.at[2 + 2 * seg + i]))
+    for copy in copies[0] + copies[1]:
+        copy.start()
+    greet(
+        pltpu.get_barrier_semaphore(),
+        [partner] + [{"fsdp": fs ^ bit} for bit in bits] + [{"ctx": (zed ^ m) * 2 + core} for m in range(1, n_z)],
+    )
+    wb_level(1, lambda hop: hop.start())
+    for copy in copies[2]:
+        copy.start()
 
     def exchange(n, src, dst):
-        return pltpu.make_async_remote_copy(
-            src_ref=src, dst_ref=dst, send_sem=send_sem.at[n], recv_sem=recv_sem.at[n],
-            device_id=partner, device_id_type=MESH,
-        )
+        return remote(src, dst, send_sem.at[n], recv_sem.at[n], partner)
 
     def over_cols(total, body):
         def run(i, carry):
@@ -561,10 +689,10 @@
 
     if wide % 128 == 0:
         for m in range(n_z):
-            att_ref[:, pl.ds(pl.multiple_of((zed ^ m) * wide, wide), wide)] = att_refs[m][...]
+            att_ref[:, pl.ds(pl.multiple_of((zed ^ m) * wide, wide), wide)] = att_in[m]
     else:
         for m in range(0, n_z, 2):
-            one, two = att_refs[m][...].astype(F32), att_refs[m + 1][...].astype(F32)
+            one, two = att_in[m].astype(F32), att_in[m + 1].astype(F32)
             odd = zed % 2 == 1
             block = jnp.concatenate([jnp.where(odd, two, one), jnp.where(odd, one, two)], axis=1)
             at = pl.ds(pl.multiple_of((zed // 2 ^ (m // 2)) * 2 * wide, 2 * wide), 2 * wide)
@@ -573,6 +701,9 @@
     def wait_all(group):
         for copy in group:
             copy.wait()
+
+    att_move = exchange(6, att_ref, att2_s)
+    att_move.start()
 
     wait_all(copies[0])
 
@@ -620,6 +751,10 @@
     up(own)
     move.wait()
     up(other)
+    for number in range(1, len(bits)):
+        wb_level(number, lambda hop: hop.wait_recv())
+        if number + 1 < len(bits):
+            wb_level(number + 1, lambda hop: hop.start())
     wait_all(copies[2])
 
     def down_other(cols):
@@ -701,64 +836,122 @@
         sums_ref[i : 1 + i, :] = total
     sums_ref[6:8, :] = jnp.zeros((2, width), F32)
 
-    for where in (own, other):
-        if where is other:
-            move.wait()
-        for m in range(n_z):
-            at = pl.ds(pl.multiple_of((zed ^ m) * wide, wide), wide)
-            ga_refs[m][where, :] = dot(g1_ref[where, :], wo_s[at, :], NT).astype(BF16)
-
-
-def middle(att, x_own, cot, vectors, bias_half, wo, wi, wb, n_f, n_z):
+    def att_hop(m):
+        return remote(ga_s.at[m - 1], ga_ref.at[m], a_send.at[m], a_recv.at[m], {"ctx": (zed ^ m) * 2 + core})
+
+    move.wait()
+    for m in list(range(n_z - 1, 0, -1)) + [0]:
+        at = pl.ds(pl.multiple_of((zed ^ m) * wide, wide), wide)
+        block = dot(g1_ref[...], wo_s[at, :], NT).astype(BF16)
+        if m == 0:
+            ga_ref[0] = block
+        else:
+            ga_s[m - 1] = block
+            att_hop(m).start()
+
+    def out_grad(i):
+        return pltpu.make_async_copy(
+            wi_s.at[:, pl.ds(i % n_out * step, step)], grads_out.at[:, pl.ds(i * step, step)], g_sem.at[i]
+        )
+
+    n_out = ff_half // step
+    for which, (left, right) in enumerate(((h_ref, gp_ref), (g2_ref, act_ref))):
+        for i in range(0, width, 256):
+            turned_s[i : i + 256, :] = left[:, i : i + 256].T
+        for i in range(n_out):
+            if which == 1:
+                out_grad(i).wait()
+
+            def rows_of(j, carry, i=i, right=right):
+                part = pl.ds(pl.multiple_of(j * 256, 256), 256)
+                cols = slice(i * step, (i + 1) * step)
+                wi_s[part, cols] = dot(turned_s[part, :], right[:, cols], NN).astype(BF16)
+                return carry
+
+            lax.fori_loop(0, width // 256, rows_of, 0)
+            out_grad(which * n_out + i).start()
+    att_move.wait()
+    half = width // 2
+    cols = pl.ds(pl.multiple_of(core * half, 128), half)
+    for i in range(0, half_in, 256):
+        at = pl.ds(pl.multiple_of(core * half + i, 128), 256)
+        og_s[at, :] = dot(att_ref[:, i : i + 256].T, g1_ref[:, cols], NN).astype(BF16)
+        at = pl.ds(pl.multiple_of((1 - core) * half + i, 128), 256)
+        turned = att2_s[:, i : i + 256].T
+        og_s[at, :] = (
+            dot(turned[:, :rows], g1_ref[rows:, cols], NN) + dot(turned[:, rows:], g1_ref[:rows, cols], NN)
+        ).astype(BF16)
+    out_move = pltpu.make_async_copy(og_s, grads_out.at[:, pl.ds(2 * ff_half, half)], g_sem.at[2 * n_out])
+    out_move.start()
+    for number in range(1, len(bits)):
+        wb_level(number, lambda hop: hop.wait_send())
+    for m in range(1, n_z):
+        att_hop(m).wait()
+    for i in range(n_out):
+        out_grad(n_out + i).wait()
+    out_move.wait()
+
+
+def middle(att, x_own, cot, vectors, bias_half, wo, wi, wb4, got, n_f, n_z):
     rows, width = x_own.shape
-    wide = att[0].shape[1]
+    wide = att.shape[2]
     ff_half = bias_half.shape[0]
     half_in = n_z * wide
     sds = jax.ShapeDtypeStruct
-    out_shape = [
-        sds((rows, width), BF16),
-        sds((rows, width), F32),
-        sds((2 * rows, half_in), BF16),
-        sds((2 * rows, width), BF16),
-        sds((2 * rows, ff_half), BF16),
-        sds((2 * rows, width), BF16),
-        sds((2 * rows, ff_half), BF16),
-        sds((2 * rows, width), BF16),
-        sds((8, width), F32),
-        sds((1, ff_half), F32),
-    ] + [sds((2 * rows, wide), BF16)] * n_z
+    vmem, dma = pltpu.VMEM, pltpu.SemaphoreType.DMA
     in_vmem, anywhere = pl.BlockSpec(memory_space=pltpu.VMEM), pl.BlockSpec(memory_space=pl.ANY)
     cfg = {"step": 512, "rows": 64}
-    results = pl.pallas_call(
+    return pl.pallas_call(
         partial(mid_kernel, n_f=n_f, n_z=n_z, cfg=cfg),
-        out_shape=out_shape,
-        in_specs=[in_vmem] * (n_z + 4) + [anywhere] * (4 * n_f + 1),
-        out_specs=[in_vmem] * len(out_shape),
+        out_shape=[
+            sds((rows, width), BF16),
+            sds((rows, width), F32),
+            sds((n_z, 2 * rows, wide), BF16),
+            sds((8, width), F32),
+            sds((1, ff_half), F32),
+            sds((width, 2 * ff_half + width // 2), BF16),
+        ],
+        in_specs=[in_vmem] * 5 + [anywhere] * 4,
+        out_specs=[in_vmem] * 5 + [anywhere],
         scratch_shapes=[
-            pltpu.VMEM((half_in, width), BF16),
-            pltpu.VMEM((width, ff_half), BF16),
-            pltpu.VMEM((ff_half, width), BF16),
-            pltpu.VMEM((2 * rows, ff_half), F32),
-            pltpu.VMEM((rows, width), F32),
-            pltpu.VMEM((rows, width), F32),
-            pltpu.VMEM((rows, width), F32),
-            pltpu.VMEM((rows, width), F32),
-            pltpu.VMEM((rows, width), F32),
-            pltpu.VMEM((rows, 128), F32),
-            pltpu.SemaphoreType.DMA((3, 2 * n_f)),
-            pltpu.SemaphoreType.DMA((6,)),
-            pltpu.SemaphoreType.DMA((6,)),
+            vmem((2 * rows, half_in), BF16),
+            vmem((2 * rows, half_in), BF16),
+            vmem((2 * rows, width), BF16),
+            vmem((2 * rows, ff_half), BF16),
+            vmem((2 * rows, width), BF16),
+            vmem((2 * rows, ff_half), BF16),
+            vmem((2 * rows, width), BF16),
+            vmem((n_z - 1, 2 * rows, wide), BF16),
+            vmem((width, 2 * rows), BF16),
+            vmem((width, width // 2), BF16),
+            vmem((half_in, width), BF16),
+            vmem((width, ff_half), BF16),
+            vmem((ff_half, width), BF16),
+            vmem((2 * rows, ff_half), F32),
+            vmem((rows, width), F32),
+            vmem((rows, width), F32),
+            vmem((rows, width), F32),
+            vmem((rows, width), F32),
+            vmem((rows, width), F32),
+            vmem((rows, 128), F32),
+            dma((2 + 2 * n_f,)),
+            dma((7,)),
+            dma((7,)),
+            dma((n_f, n_f)),
+            dma((n_f, n_f)),
+            dma((n_z,)),
+            dma((n_z,)),
+            dma((2 * (ff_half // cfg["step"]) + 1,)),
         ],
         compiler_params=pltpu.CompilerParams(
             vmem_limit_bytes=VMEM_MIDDLE, collective_id=0, has_side_effects=True
         ),
         cost_estimate=pl.CostEstimate(
-            flops=2 * 2 * rows * width * (2 * half_in + 4 * ff_half),
+            flops=2 * 2 * rows * width * (3 * half_in + 6 * ff_half),
             bytes_accessed=40 << 20, transcendentals=2 * rows * ff_half,
         ),
         name="middle",
-    )(*att, x_own, cot, vectors, bias_half[None], wo, *wi, *wb)
-    return results[:10], results[10:]
+    )(att, x_own, cot, vectors, bias_half[None], wo, wi, wb4, got)
 
 
 def tail_kernel(*refs, n_z):
@@ -855,35 +1048,12 @@
 
     bits = [1 << b for b in range(n_f.bit_length() - 1)]
 
-    def pair(v):
-        return jnp.concatenate([v, swap(v)], axis=0)
-
-    def pair_sum(partial_sum):
-        return partial_sum[:rows] + swap(partial_sum[rows:])
-
     def place(pieces, index, axis):
         count = len(pieces)
         for bit in range(count.bit_length() - 1):
             flag = (index >> bit) & 1
             pieces = [jnp.where(flag, pieces[m ^ (1 << bit)], pieces[m]) for m in range(count)]
         return jnp.concatenate(pieces, axis=axis)
-
-    def gather_cols(shard, begun=None):
-        half = shard.shape[0] // 2
-        parts = []
-        for side, order in enumerate((bits, bits[1:] + bits[:1])):
-            held = {0: shard[side * half : (side + 1) * half]}
-            for level, bit in enumerate(order):
-                if level == 0 and begun is not None:
-                    held[bit] = begun[side]
-                    continue
-                for m in list(held):
-                    held[m ^ bit] = over_f(held[m], bit)
-            parts += [held[m] for m in range(n_f)]
-        return parts
-
-    def after(value, *others):
-        return lax.optimization_barrier((value,) + others)[0]
 
     half_in = width // 2
     first = (core * half_heads + zed * heads) * HEAD
@@ -900,24 +1070,15 @@
     )
 
     ff_part = w_in.shape[1] // 2
-    wi_mine = lax.dynamic_slice_in_dim(w_in, core * ff_part, ff_part, 1)
-    wi_half = gather_cols(wi_mine, wi_got)
-    wb_mine = lax.dynamic_index_in_dim(
-        w_back.reshape(n_f, 2, ff_part, w_back.shape[1]), core, 1, False
-    ).reshape(n_f * ff_part, -1)
-    wb_half = gather_cols(after(wb_mine, wi_got))
-
-    att, att_full, lse = attend(qkv, heads)
-    att = [att[m] if m == 0 else over_z(att[m], m) for m in range(n_z)]
+    w_back4 = w_back.reshape(n_f, 2, ff_part, w_back.shape[1])
+    att, att_full, lse, wi_half, wb_got = attend(qkv, w_in, wi_got, w_back4, heads, n_f)
     bias_half = lax.dynamic_index_in_dim(
         bias_in.reshape(n_f, 2, ff_part), core, 1, False
     ).reshape(-1)
-    outs, grad_att = middle(
-        att, x_own, grad_out, vectors, bias_half, wo_half, wi_half, wb_half, n_f, n_z
+    layer_out, grad_one, g_att, sums_mid, bias_sum, mid_grads = middle(
+        att, x_own, grad_out, vectors, bias_half, wo_half, wi_half, w_back4, wb_got, n_f, n_z
     )
-    layer_out, grad_one, att_half, h_two, act, g_two, grad_pre_low, g_one, sums_mid, bias_sum = outs
     layer_out = layer_out[None]
-    g_att = [grad_att[m] if m == 0 else over_z(grad_att[m], m) for m in range(n_z)]
 
     low = width // (n_ctx * n_f)
 
@@ -957,13 +1118,11 @@
     def reduced(partial_grad):
         return over_ctx(over_fsdp(partial_grad))
 
-    in_weight_grad = halves(*reduced(dot(h_two, grad_pre_low, TN).astype(BF16)), n_f)
-    back_weight_grad = halves(*reduced(dot(g_two, act, TN).astype(BF16)), n_f).T
-    att_other = swap(att_half)
-    att_other = jnp.concatenate([att_other[rows:], att_other[:rows]], axis=0)
-    att_both = place([att_half, att_other], core, 0 + 1)
-    out_cols = lax.dynamic_slice_in_dim(g_one, core * half_in, half_in, 1)
-    out_weight_grad = halves(*reduced(dot(att_both, out_cols, TN).astype(BF16)), 1)
+    stay, came = reduced(mid_grads)
+    n_half = hidden // 2
+    in_weight_grad = halves(stay[:, :n_half], came[:, :n_half], n_f)
+    back_weight_grad = halves(stay[:, n_half : 2 * n_half], came[:, n_half : 2 * n_half], n_f).T
+    out_weight_grad = halves(stay[:, 2 * n_half :], came[:, 2 * n_half :], 1)
 
     g_qkv = attend_back(qkv, g_att, att_full, lse, heads)
     g_sent = [g_qkv[m] if m == 0 else over_z(g_qkv[m], m) for m in range(n_z)]

time: 528 us -> 502 us (0.951)
  the two profiles are of different devices: /device:TPU:23 before, /device:TPU:0 now
where the time goes in v4:
time: 502 us; the launch traced here: 494 us
  Pallas kernels  237 us (47%)
  waiting for transfers between devices  155 us (31%)
  local copies, waits for them, and re-layouts  45.2 us (9%)
  starting transfers between devices  30.6 us (6%)
  other arithmetic  17.4 us (3%)
  matrix products  6.52 us (1%)
    ppermute x12, waiting for transfers between devices, over_f(): return lax.ppermute(v, 'fsdp', [(i, i ^ m) for i in range(n_f)])  110 us
    pallas_call x1, Pallas kernels, middle(): pl.pallas_call(partial(mid_kernel, n_f=n_f, n_z=n_z, cfg=cfg), out_shape=...  72.4 us
    pallas_call x1, Pallas kernels, front(): pl.pallas_call(partial(front_kernel, n_z=n_z, n_f=n_f, heads=heads), out_...  63.6 us
    pallas_call x1, Pallas kernels, attend_back(): pl.pallas_call(partial(attend_back_kernel, blocks=blocks, heads=heads, q_...  49.8 us
    ppermute x12, waiting for transfers between devices, over_z(): return lax.ppermute(v, 'ctx', [(i, i ^ 2 * m) for i in range(n_ctx)])  43.4 us
    pallas_call x1, Pallas kernels, attend(): pl.pallas_call(partial(attend_kernel, blocks=blocks, heads=heads, n_f=n_f...  41.3 us
    ppermute x12, starting transfers between devices, over_z(): return lax.ppermute(v, 'ctx', [(i, i ^ 2 * m) for i in range(n_ctx)])  18.6 us
    unnamed x45, local copies, waits for them, and re-layouts  15 us
  transfers between devices with their start and end apart: 28, of which 12 were waited for; matrix products, arithmetic and copies ran while one was open for 10% of the time, Pallas kernels for 2%

profile of v4, /device:TPU:0, one launch (start us, length us, event | category | flops | bytes accessed | tf_op | source)
XLA Modules:
  0.0 493.5 jit_solution(6574710759192920017)
XLA Ops:
  5.1 63.6 %front.1 = (bf16[4,768,384]{2,1,0:T(8,128)(2,1)}, bf16[4,2,384,1024]{3,2,1,0:T(8,128)(2,1)}, bf16[1024,1536]{1,0:T(8,128)(2,1)}, bf16[512,1024]{1,0:T(8,128)(2,1)S(1)}, bf16[2,512,512]{2,1,0:T(8,128)(2,1)S(1)}) custom-call(bf16[384,1024]{1,0:T(8,128)(2,1)S(1)} %bitcast.157, bf16[1024,768]{1,0:T(8,128)(2,1)} %wq_ref.1, bf16[1024,256]{1,0:T(8,128)(2,1)S(1)} %copy-done.1, ...), custom_call_target="tpu_custom_call" | custom-call | flops 2415919104 | bytes 31457280 | tf_op jit(solution)/shard_map/front/pallas_call | solution.py:279
  69.6 41.3 %attend.1 = (bf16[4,768,128]{2,1,0:T(8,128)(2,1)S(1)}, f32[3072,128]{1,0:T(8,128)}, f32[3072,128]{1,0:T(8,128)}, bf16[1024,2048]{1,0:T(8,128)(2,1)}, bf16[4,512,256]{2,1,0:T(8,128)(2,1)S(1)}) custom-call(bf16[4,768,384]{2,1,0:T(8,128)(2,1)} %get-tuple-element.28.refs_0_, bf16[1024,1024]{1,0:T(8,128)(2,1)} %refs_1_.1, ...), custom_call_target="tpu_custom_call" | custom-call | flops 19327352832 | bytes 3932160 | tf_op jit(solution)/shard_map/attend/pallas_call | solution.py:480
  112.8 72.4 %middle.1 = (bf16[384,1024]{1,0:T(8,128)(2,1)}, f32[384,1024]{1,0:T(8,128)}, bf16[4,768,128]{2,1,0:T(8,128)(2,1)}, f32[8,1024]{1,0:T(8,128)}, f32[1,2048]{1,0:T(1,128)}, /*index=5*/bf16[1024,4608]{1,0:T(8,128)(2,1)}) custom-call(bf16[4,768,128]{2,1,0:T(8,128)(2,1)} %copy-done.4, bf16[384,1024]{1,0:T(8,128)(2,1)} %bitcast.156, f32[384,1024]{1,0:T(8,128)} %bitcast.174, ...), custom_call_target="tpu_custom_call" | custom-call | flops 21743271936 | bytes 41943040 | tf_op jit(solution)/shard_map/middle/pallas_call | solution.py:904
  186.3 49.8 %attend_back.1 = (bf16[768,384]{1,0:T(8,128)(2,1)S(1)}, bf16[768,384]{1,0:T(8,128)(2,1)S(1)}, bf16[768,384]{1,0:T(8,128)(2,1)S(1)}, bf16[768,384]{1,0:T(8,128)(2,1)S(1)}) custom-call(bf16[4,768,384]{2,1,0:T(8,128)(2,1)} %get-tuple-element.28.refs_0_, bf16[4,768,128]{2,1,0:T(8,128)(2,1)S(1)} %copy-done.5, f32[3072,128]{1,0:T(8,128)} %get-tuple-element.36.refs_2_, ...), custom_call_target="tpu_custom_call" | custom-call | flops 48318382080 | bytes 7864320 | tf_op jit(solution)/shard_map/attend_back/pallas_call | solution.py:582
  236.6 6.5 %convolution_convert_fusion = bf16[1024,384]{1,0:T(8,128)(2,1)S(1)} fusion(bf16[3072,1024]{1,0:T(8,128)(2,1)} %bitcast.175, bf16[3072,384]{1,0:T(8,128)(2,1)S(1)} %constant_dynamic-update-slice_fusion), kind=kOutput, calls=%fused_computation.20 | convolution fusion | flops 2416312320 | bytes 9437184 | tf_op jit(solution)/shard_map/dot_general | solution.py:25
  253.0 6.7 %fusion.49 = (bf16[4,1,2,2,32,4608]{5,4,3,2,1,0:T(8,128)(2,1)}, bf16[4,1,2,2,32,4608]{5,4,3,2,1,0:T(8,128)(2,1)S(1)}) fusion(bf16[4,2,2,2,32,4608]{5,4,3,2,1,0:T(8,128)(2,1)} %bitcast.160), kind=kLoop, calls=%fused_computation.159 | loop fusion | bytes 18874368 | tf_op jit(solution)/shard_map/slice | solution.py:1090
  259.7 2.5 constant_dynamic-slice_fusion.13
  262.3 3.2 dynamic-slice_bitcast_fusion
  267.8 3.3 copy.83
  272.5 2.4 collective-permute-start.26
  280.1 2.9 collective-permute-done.20
  285.0 4.9 collective-permute-start.1
  299.1 2.4 collective-permute-done.4
  301.6 29.5 %collective-permute-done.6 = bf16[4,32,384]{2,1,0:T(8,128)(2,1)S(1)} collective-permute-done((bf16[4,32,384]{2,1,0:T(8,128)(2,1)S(1)}, bf16[4,32,384]{2,1,0:T(8,128)(2,1)S(1)}, u32[]{:S(2)}, u32[]{:S(2)}) %collective-permute-start.6) | collective-permute-done | bytes 98336 | tf_op jit(solution)/shard_map/ppermute | solution.py:1047
  333.7 10.1 %collective-permute-done.8 = bf16[2,32,384]{2,1,0:T(8,128)(2,1)S(1)} collective-permute-done((bf16[2,32,384]{2,1,0:T(8,128)(2,1)S(1)}, bf16[2,32,384]{2,1,0:T(8,128)(2,1)S(1)}, u32[]{:S(2)}, u32[]{:S(2)}) %collective-permute-start.8) | collective-permute-done | bytes 49184 | tf_op jit(solution)/shard_map/ppermute | solution.py:1044
  343.8 2.3 collective-permute-start.2
  346.2 9.9 %collective-permute-done.9 = bf16[2,32,384]{2,1,0:T(8,128)(2,1)S(1)} collective-permute-done((bf16[2,32,384]{2,1,0:T(8,128)(2,1)S(1)}, bf16[2,32,384]{2,1,0:T(8,128)(2,1)S(1)}, u32[]{:S(2)}, u32[]{:S(2)}) %collective-permute-start.9) | collective-permute-done | bytes 49184 | tf_op jit(solution)/shard_map/ppermute | solution.py:1044
  357.2 3.1 fusion.1
  360.4 47.4 %collective-permute-done.13 = bf16[4,2,32,4608]{3,2,1,0:T(8,128)(2,1)} collective-permute-done((bf16[4,2,32,4608]{3,2,1,0:T(8,128)(2,1)}, bf16[4,2,32,4608]{3,2,1,0:T(8,128)(2,1)}, u32[]{:S(2)}, u32[]{:S(2)}) %collective-permute-start.13) | collective-permute-done | bytes 2359328 | tf_op jit(solution)/shard_map/ppermute | solution.py:1047
  410.9 13.1 %collective-permute-done.12 = bf16[4,32,4608]{2,1,0:T(8,128)(2,1)S(1)} collective-permute-done((bf16[4,32,4608]{2,1,0:T(8,128)(2,1)S(1)}, bf16[4,32,4608]{2,1,0:T(8,128)(2,1)S(1)}, u32[]{:S(2)}, u32[]{:S(2)}) %collective-permute-start.12) | collective-permute-done | bytes 1179680 | tf_op jit(solution)/shard_map/ppermute | solution.py:1047
  425.0 15.1 %collective-permute-done.14 = bf16[4,32,4608]{2,1,0:T(8,128)(2,1)S(1)} collective-permute-done((bf16[4,32,4608]{2,1,0:T(8,128)(2,1)S(1)}, bf16[4,32,4608]{2,1,0:T(8,128)(2,1)S(1)}, u32[]{:S(2)}, u32[]{:S(2)}) %collective-permute-start.14) | collective-permute-done | bytes 1179680 | tf_op jit(solution)/shard_map/ppermute | solution.py:1047
  443.8 2.4 collective-permute-start.15
  448.0 9.9 %tail.1 = f32[384,1024]{1,0:T(8,128)S(1)} custom-call(bf16[768,384]{1,0:T(8,128)(2,1)S(1)} %get-tuple-element.38.refs_0_, bf16[768,384]{1,0:T(8,128)(2,1)S(1)} %collective-permute-done.refs_1_, bf16[768,384]{1,0:T(8,128)(2,1)} %collective-permute-done.1.refs_2_, bf16[768,384]{1,0:T(8,128)(2,1)} %collective-permute-done.2.refs_3_, ...), custom_call_target="tpu_custom_call" | custom-call | flops 2415919104 | bytes 12582912 | tf_op jit(solution)/shard_map/tail/pallas_call | solution.py:1008
  457.9 21.5 %collective-permute-done.16 = bf16[2,32,4608]{2,1,0:T(8,128)(2,1)} collective-permute-done((bf16[2,32,4608]{2,1,0:T(8,128)(2,1)}, bf16[2,32,4608]{2,1,0:T(8,128)(2,1)}, u32[]{:S(2)}, u32[]{:S(2)}) %collective-permute-start.16) | collective-permute-done | bytes 589856 | tf_op jit(solution)/shard_map/ppermute | solution.py:1044
  (181 shorter events, 65.7 us)
Async XLA Ops:
  236.1 207.6 %collective-permute-start = (bf16[768,384]{1,0:T(8,128)(2,1)S(1)}, bf16[768,384]{1,0:T(8,128)(2,1)S(1)}, u32[]{:S(2)}, u32[]{:S(2)}) collective-permute-start(bf16[768,384]{1,0:T(8,128)(2,1)S(1)} %get-tuple-element.39), channel_id=1, source_target_pairs={{0,8},{4,12},{8,0},{12,4},{16,24},{20,28},{24,16},{28,20},{1,9},{5... | collective-permute-start | bytes 1769480 | tf_op jit(solution)/shard_map/ppermute | solution.py:1044
  245.4 50.4 %collective-permute-start.3 = (bf16[4,2,32,384]{3,2,0,1:T(8,128)(2,1)}, bf16[4,2,32,384]{3,2,0,1:T(8,128)(2,1)}, u32[]{:S(2)}, u32[]{:S(2)}) collective-permute-start(bf16[4,2,32,384]{3,2,0,1:T(8,128)(2,1)} %bitcast.154), channel_id=1, source_target_pairs={{0,1},{1,0},{2,3},{3,2},{4,5},{5,4},{6,7},{7,6},{8,9},{9,8},{10,11... | collective-permute-start | bytes 589832 | tf_op jit(solution)/shard_map/ppermute | solution.py:1047
  248.0 17.5 %collective-permute-start.22 = (f32[2,4,2,320]{3,2,1,0:T(2,128)S(1)}, f32[2,4,2,320]{3,2,1,0:T(2,128)S(1)}, u32[]{:S(2)}, u32[]{:S(2)}) collective-permute-start(f32[2,4,2,320]{3,2,1,0:T(2,128)S(1)} %dynamic-slice_bitcast_fusion.6), channel_id=1, source_target_pairs={{0,1},{1,0},{2,3},{3,2},{4,5},{5,4},{6,7},{7,6},{8,9},{9,8},{10,11... | collective-permute-start | bytes 61448 | tf_op jit(solution)/shard_map/ppermute | solution.py:1047
  252.4 18.7 %collective-permute-start.19 = (f32[2,64]{1,0:T(2,128)}, f32[2,64]{1,0:T(2,128)}, u32[]{:S(2)}, u32[]{:S(2)}) collective-permute-start(f32[2,64]{1,0:T(2,128)} %bitcast.49), channel_id=1, source_target_pairs={{0,1},{1,0},{2,3},{3,2},{4,5},{5,4},{6,7},{7,6},{8,9},{9,8},{10,11... | collective-permute-start | bytes 1544 | tf_op jit(solution)/shard_map/ppermute | solution.py:1047
  265.6 6.2 %collective-permute-start.23 = (f32[4,2,320]{2,1,0:T(2,128)S(1)}, f32[4,2,320]{2,1,0:T(2,128)}, u32[]{:S(2)}, u32[]{:S(2)}) collective-permute-start(f32[4,2,320]{2,1,0:T(2,128)S(1)} %fusion.34), channel_id=1, source_target_pairs={{0,2},{1,3},{2,0},{3,1},{4,6},{5,7},{6,4},{7,5},{8,10},{9,11},{10,... | collective-permute-start | bytes 30728 | tf_op jit(solution)/shard_map/ppermute | solution.py:1047
  272.5 5.5 %collective-permute-start.26 = (f32[2,320]{1,0:T(2,128)S(1)}, f32[2,320]{1,0:T(2,128)S(1)}, u32[]{:S(2)}, u32[]{:S(2)}) collective-permute-start(f32[2,320]{1,0:T(2,128)S(1)} %get-tuple-element.95), channel_id=1, source_target_pairs={{0,24},{4,28},{8,16},{12,20},{16,8},{20,12},{24,0},{28,4},{1,25},{... | collective-permute-start | bytes 7688 | tf_op jit(solution)/shard_map/ppermute | solution.py:1044
  274.9 4.5 collective-permute-start.25
  278.0 79.1 %collective-permute-start.11 = (bf16[4,2,32,4608]{3,2,0,1:T(8,128)(2,1)}, bf16[4,2,32,4608]{3,2,0,1:T(8,128)(2,1)}, u32[]{:S(2)}, u32[]{:S(2)}) collective-permute-start(bf16[4,2,32,4608]{3,2,0,1:T(8,128)(2,1)} %bitcast.161), channel_id=1, source_target_pairs={{0,1},{1,0},{2,3},{3,2},{4,5},{5,4},{6,7},{7,6},{8,9},{9,8},{10,11... | collective-permute-start | bytes 7077896 | tf_op jit(solution)/shard_map/ppermute | solution.py:1047
  280.0 11.2 %collective-permute-start.27 = (f32[320]{0:T(512)S(1)}, f32[320]{0:T(512)S(1)}, u32[]{:S(2)}, u32[]{:S(2)}) collective-permute-start(f32[320]{0:T(512)S(1)} %get-tuple-element.48), channel_id=1, source_target_pairs={{0,4},{4,0},{8,12},{12,8},{16,20},{20,16},{24,28},{28,24},{1,5},{5... | collective-permute-start | bytes 3848 | tf_op jit(solution)/shard_map/ppermute | solution.py:1041
  285.0 162.9 %collective-permute-start.1 = (bf16[768,384]{1,0:T(8,128)(2,1)S(1)}, bf16[768,384]{1,0:T(8,128)(2,1)}, u32[]{:S(2)}, u32[]{:S(2)}) collective-permute-start(bf16[768,384]{1,0:T(8,128)(2,1)S(1)} %get-tuple-element.40), channel_id=1, source_target_pairs={{0,16},{4,20},{8,24},{12,28},{16,0},{20,4},{24,8},{28,12},{1,17},{... | collective-permute-start | bytes 1769480 | tf_op jit(solution)/shard_map/ppermute | solution.py:1044
  291.2 7.2 %collective-permute-start.5 = (bf16[4,2,32,384]{3,2,0,1:T(8,128)(2,1)}, bf16[4,2,32,384]{3,2,0,1:T(8,128)(2,1)S(1)}, u32[]{:S(2)}, u32[]{:S(2)}) collective-permute-start(bf16[4,2,32,384]{3,2,0,1:T(8,128)(2,1)} %bitcast.166), channel_id=1, source_target_pairs={{0,2},{1,3},{2,0},{3,1},{4,6},{5,7},{6,4},{7,5},{8,10},{9,11},{10,... | collective-permute-start | bytes 589832 | tf_op jit(solution)/shard_map/ppermute | solution.py:1047
  296.9 4.7 collective-permute-start.4
  298.5 32.6 %collective-permute-start.6 = (bf16[4,32,384]{2,1,0:T(8,128)(2,1)S(1)}, bf16[4,32,384]{2,1,0:T(8,128)(2,1)S(1)}, u32[]{:S(2)}, u32[]{:S(2)}) collective-permute-start(bf16[4,32,384]{2,1,0:T(8,128)(2,1)S(1)} %dynamic-slice_bitcast_fusion.4), channel_id=1, source_target_pairs={{0,1},{1,0},{2,3},{3,2},{4,5},{5,4},{6,7},{7,6},{8,9},{9,8},{10,11... | collective-permute-start | bytes 294920 | tf_op jit(solution)/shard_map/ppermute | solution.py:1047
  331.1 12.7 %collective-permute-start.8 = (bf16[2,32,384]{2,1,0:T(8,128)(2,1)S(1)}, bf16[2,32,384]{2,1,0:T(8,128)(2,1)S(1)}, u32[]{:S(2)}, u32[]{:S(2)}) collective-permute-start(bf16[2,32,384]{2,1,0:T(8,128)(2,1)S(1)} %get-tuple-element.75), channel_id=1, source_target_pairs={{0,16},{4,20},{8,24},{12,28},{16,0},{20,4},{24,8},{28,12},{1,17},{... | collective-permute-start | bytes 147464 | tf_op jit(solution)/shard_map/ppermute | solution.py:1044
  332.2 14.0 %collective-permute-start.7 = (bf16[2,32,384]{2,1,0:T(8,128)(2,1)S(1)}, bf16[2,32,384]{2,1,0:T(8,128)(2,1)S(1)}, u32[]{:S(2)}, u32[]{:S(2)}) collective-permute-start(bf16[2,32,384]{2,1,0:T(8,128)(2,1)S(1)} %get-tuple-element.74), channel_id=1, source_target_pairs={{0,24},{4,28},{8,16},{12,20},{16,8},{20,12},{24,0},{28,4},{1,25},{... | collective-permute-start | bytes 147464 | tf_op jit(solution)/shard_map/ppermute | solution.py:1044
  343.8 104.2 %collective-permute-start.2 = (bf16[768,384]{1,0:T(8,128)(2,1)S(1)}, bf16[768,384]{1,0:T(8,128)(2,1)}, u32[]{:S(2)}, u32[]{:S(2)}) collective-permute-start(bf16[768,384]{1,0:T(8,128)(2,1)S(1)} %get-tuple-element.41), channel_id=1, source_target_pairs={{0,24},{4,28},{8,16},{12,20},{16,8},{20,12},{24,0},{28,4},{1,25},{... | collective-permute-start | bytes 1769480 | tf_op jit(solution)/shard_map/ppermute | solution.py:1044
  346.2 10.0 %collective-permute-start.9 = (bf16[2,32,384]{2,1,0:T(8,128)(2,1)S(1)}, bf16[2,32,384]{2,1,0:T(8,128)(2,1)S(1)}, u32[]{:S(2)}, u32[]{:S(2)}) collective-permute-start(bf16[2,32,384]{2,1,0:T(8,128)(2,1)S(1)} %get-tuple-element.73), channel_id=1, source_target_pairs={{0,8},{4,12},{8,0},{12,4},{16,24},{20,28},{24,16},{28,20},{1,9},{5... | collective-permute-start | bytes 147464 | tf_op jit(solution)/shard_map/ppermute | solution.py:1044
  356.1 51.6 %collective-permute-start.13 = (bf16[4,2,32,4608]{3,2,1,0:T(8,128)(2,1)}, bf16[4,2,32,4608]{3,2,1,0:T(8,128)(2,1)}, u32[]{:S(2)}, u32[]{:S(2)}) collective-permute-start(bf16[4,2,32,4608]{3,2,1,0:T(8,128)(2,1)} %dynamic-slice_bitcast_fusion), channel_id=1, source_target_pairs={{0,2},{1,3},{2,0},{3,1},{4,6},{5,7},{6,4},{7,5},{8,10},{9,11},{10,... | collective-permute-start | bytes 7077896 | tf_op jit(solution)/shard_map/ppermute | solution.py:1047
  357.1 86.7 %collective-permute-start.10 = (bf16[4,32,384]{2,1,0:T(8,128)(2,1)S(1)}, bf16[4,32,384]{2,1,0:T(8,128)(2,1)S(1)}, u32[]{:S(2)}, u32[]{:S(2)}) collective-permute-start(bf16[4,32,384]{2,1,0:T(8,128)(2,1)S(1)} %pad_maximum_fusion.6), channel_id=1, source_target_pairs={{0,4},{4,0},{8,12},{12,8},{16,20},{20,16},{24,28},{28,24},{1,5},{5... | collective-permute-start | bytes 294920 | tf_op jit(solution)/shard_map/ppermute | solution.py:1041
  407.7 16.2 %collective-permute-start.12 = (bf16[4,32,4608]{2,1,0:T(8,128)(2,1)S(1)}, bf16[4,32,4608]{2,1,0:T(8,128)(2,1)S(1)}, u32[]{:S(2)}, u32[]{:S(2)}) collective-permute-start(bf16[4,32,4608]{2,1,0:T(8,128)(2,1)S(1)} %dynamic-slice_bitcast_fusion.2), channel_id=1, source_target_pairs={{0,2},{1,3},{2,0},{3,1},{4,6},{5,7},{6,4},{7,5},{8,10},{9,11},{10,... | collective-permute-start | bytes 3538952 | tf_op jit(solution)/shard_map/ppermute | solution.py:1047
  423.9 16.2 %collective-permute-start.14 = (bf16[4,32,4608]{2,1,0:T(8,128)(2,1)S(1)}, bf16[4,32,4608]{2,1,0:T(8,128)(2,1)S(1)}, u32[]{:S(2)}, u32[]{:S(2)}) collective-permute-start(bf16[4,32,4608]{2,1,0:T(8,128)(2,1)S(1)} %dynamic-slice_bitcast_fusion.1), channel_id=1, source_target_pairs={{0,1},{1,0},{2,3},{3,2},{4,5},{5,4},{6,7},{7,6},{8,9},{9,8},{10,11... | collective-permute-start | bytes 3538952 | tf_op jit(solution)/shard_map/ppermute | solution.py:1047
  441.8 16.1 %collective-permute-start.17 = (bf16[2,32,4608]{2,1,0:T(8,128)(2,1)}, bf16[2,32,4608]{2,1,0:T(8,128)(2,1)}, u32[]{:S(2)}, u32[]{:S(2)}) collective-permute-start(bf16[2,32,4608]{2,1,0:T(8,128)(2,1)} %get-tuple-element.56), channel_id=1, source_target_pairs={{0,24},{4,28},{8,16},{12,20},{16,8},{20,12},{24,0},{28,4},{1,25},{... | collective-permute-start | bytes 1769480 | tf_op jit(solution)/shard_map/ppermute | solution.py:1044
  443.8 35.6 %collective-permute-start.16 = (bf16[2,32,4608]{2,1,0:T(8,128)(2,1)}, bf16[2,32,4608]{2,1,0:T(8,128)(2,1)}, u32[]{:S(2)}, u32[]{:S(2)}) collective-permute-start(bf16[2,32,4608]{2,1,0:T(8,128)(2,1)} %get-tuple-element.55), channel_id=1, source_target_pairs={{0,16},{4,20},{8,24},{12,28},{16,0},{20,4},{24,8},{28,12},{1,17},{... | collective-permute-start | bytes 1769480 | tf_op jit(solution)/shard_map/ppermute | solution.py:1044
  443.8 35.6 %collective-permute-start.15 = (bf16[2,32,4608]{2,1,0:T(8,128)(2,1)}, bf16[2,32,4608]{2,1,0:T(8,128)(2,1)}, u32[]{:S(2)}, u32[]{:S(2)}) collective-permute-start(bf16[2,32,4608]{2,1,0:T(8,128)(2,1)} %get-tuple-element.54), channel_id=1, source_target_pairs={{0,8},{4,12},{8,0},{12,4},{16,24},{20,28},{24,16},{28,20},{1,9},{5... | collective-permute-start | bytes 1769480 | tf_op jit(solution)/shard_map/ppermute | solution.py:1044
  (22 other events, 277.6 us)
